TPU v7x, 1024 devices: a whole 4x4x32 slice. The times are simulated.
1024 devices in a mesh: row: 16 (over z_lo), col: 64 (over z_hi, x, y, core).
Axes of the slice: x: 4, y: 4, z: 32 (z_hi: 2, z_lo: 16; z = z_hi * 16 + z_lo), core: 2. Of those that a mesh axis runs over, the one named last changes fastest.
Arguments:
- photo_features: bfloat16 [12288, 1152], P(('row', 'col')), may hold values from -6 to 6
- sentence_features: bfloat16 [12288, 1152], P(('row', 'col')), may hold values from -6 to 6
- described_photo_number: int32 [12288], P(('row', 'col')), may hold values from 0 to 12287, each once
- logit_multiplier: float32 [], replicated, may hold values from 3 to 8
- logit_offset: float32 [], replicated, may hold values from -4 to -1
Outputs:
- img_grad: float32 [12288, 1152], P(('row', 'col'))
- txt_grad: float32 [12288, 1152], P(('row', 'col'))
Inputs may be any that keep to these rules, and one draw needn't show every extreme that they name: `described_photo_number`: every image index appears exactly once among the text ids.
All inputs are finite; a program needn't handle non-finite values.
Results may differ from a plain program's by a relative error of at most 0.004.
Values may be sent and summed in bfloat16 or wider, within the bound.
No kernel may reach another device: no remote copies, remote signals or barrier semaphores. Data moves between devices by JAX's collectives and lax.ppermute only.
A program may use at most 32 MiB of HBM per device.

v0:
```python
import jax
import jax.numpy as jnp
from jax import lax
from jax.sharding import PartitionSpec as P


def unit_rows(raw):
    values = raw.astype(jnp.float32)
    scale = lax.rsqrt(jnp.sum(values * values, axis=1, keepdims=True) + 1e-06)
    return (values * scale, scale)


def back_through(unit, scale, upstream):
    inner = jnp.sum(unit * upstream, axis=1, keepdims=True)
    return scale * (upstream - unit * inner)


def coupling_coefficient(
    photo_entries, sentence_tile, tile_numbers, diagonal_marker, logit_multiplier, logit_offset
):
    similarity_logits = (
        logit_multiplier
        * jnp.einsum("id,jd->ij", photo_entries, sentence_tile, preferred_element_type=jnp.float32)
        + logit_offset
    )
    ids = diagonal_marker + lax.iota(jnp.int32, photo_entries.shape[0])
    match_polarity = jnp.where(ids[:, None] == tile_numbers[None, :], 1.0, -1.0).astype(jnp.float32)
    return (
        logit_multiplier * -match_polarity * jax.nn.sigmoid(-match_polarity * similarity_logits)
    ).astype(jnp.bfloat16)


def shards(
    photo_features, sentence_features, described_photo_number, logit_multiplier, logit_offset
):
    img_unit, img_scale = unit_rows(photo_features)
    txt_unit, txt_scale = unit_rows(sentence_features)
    img_send = img_unit.astype(jnp.bfloat16)
    sentence_sent_onward = txt_unit.astype(jnp.bfloat16)
    sentence_tile, tile_numbers = (
        lax.all_gather(sentence_sent_onward, "row", axis=0, tiled=True),
        lax.all_gather(described_photo_number, "row", axis=0, tiled=True),
    )
    own_rows = img_send.shape[0]
    block_rows = own_rows * lax.axis_size("col")
    diagonal_marker = lax.axis_index("row") * block_rows
    photo_tile = lax.all_gather(img_send, "col", axis=0, tiled=True)
    coefficient_table = coupling_coefficient(
        photo_tile, sentence_tile, tile_numbers, diagonal_marker, logit_multiplier, logit_offset
    )
    txt_term = jnp.einsum(
        "ij,id->jd", coefficient_table, photo_tile, preferred_element_type=jnp.float32
    )
    img_upstream = lax.psum_scatter(
        jnp.dot(coefficient_table, sentence_tile, preferred_element_type=jnp.float32),
        "col",
        scatter_dimension=0,
        tiled=True,
    )
    txt_upstream = lax.psum_scatter(txt_term, "row", scatter_dimension=0, tiled=True)
    return (
        back_through(img_unit, img_scale, img_upstream),
        back_through(txt_unit, txt_scale, txt_upstream),
    )


def solution(mesh):
    placed = (P(("row", "col"), None), P(("row", "col"), None), P(("row", "col")), P(), P())
    return jax.shard_map(
        shards,
        mesh=mesh,
        in_specs=placed,
        out_specs=(P(("row", "col"), None), P(("row", "col"), None)),
        check_vma=False,
    )
```

profile of v0, /device:TPU:960, one launch (start us, length us, event | category | flops | bytes accessed | tf_op | source)
XLA Modules:
  0.0 1045.9 jit_solution(13857235973171578498)
XLA Ops:
  12.7 84.7 %all-gather.1 = bf16[16,12,1152]{2,1,0:T(8,128)(2,1)S(1)} all-gather(bf16[1,12,1152]{2,1,0:T(8,128)(2,1)S(1)} %fusion.25), channel_id=1, replica_groups=mesh['row'=16,'col'=64] {'row'}, dimensions={0}, use_global_device_ids=true | all-gather | bytes 470016 | tf_op jit(solution)/shard_map/all_gather | solution.py:41
  99.8 53.5 %all-reduce = s32[192]{0:T(256)S(1)} all-reduce(s32[192]{0:T(256)S(1)} %dynamic-update-slice), channel_id=1, replica_groups=mesh['row'=16,'col'=64] {'row'}, use_global_device_ids=true, to_apply=%add | all-reduce | flops 192 | bytes 1536
  153.3 26.7 %all-gather.4.cloned.1.call-done = bf16[64,12,1152]{2,1,0:T(8,128)(2,1)} async-done(((bf16[1,12,1152]{2,1,0:T(8,128)(2,1)}), bf16[64,12,1152]{2,1,0:T(8,128)(2,1)}) %all-gather.4.cloned.1.call-update) | async-done | bytes 1769488 | tf_op jit(solution)/shard_map/all_gather | solution.py:47
  180.0 2.5 reshape.27
  184.6 81.5 %fusion.1 = f32[16,1152]{1,0:T(8,128)} fusion(f32[192,1152]{1,0:T(8,128)S(1)} %fusion.28), kind=kCustom, calls=%all-reduce-scatter.1 | all-reduce-scatter fusion | flops 294913 | bytes 962560
  270.2 14.4 %collective-permute-start.16 = (f32[16,1152]{1,0:T(8,128)}, f32[16,1152]{1,0:T(8,128)}, u32[]{:S(2)}, u32[]{:S(2)}) collective-permute-start(f32[16,1152]{1,0:T(8,128)} %fusion.1), channel_id=1, source_target_pairs={{0,64},{64,128},{128,192},{192,256},{256,320},{320,384},{384,448},... | collective-permute-start | bytes 221192
  287.7 627.9 %fusion = f32[16,1152]{1,0:T(8,128)} fusion(f32[768,1152]{1,0:T(8,128)S(1)} %fusion.27), kind=kCustom, calls=%all-reduce-scatter | all-reduce-scatter fusion | flops 1179649 | bytes 3616768
  918.4 1.9 collective-permute-start.14
  920.3 23.2 %collective-permute-done.15 = f32[12,1152]{1,0:T(8,128)S(1)} collective-permute-done((f32[12,1152]{1,0:T(8,128)S(1)}, f32[12,1152]{1,0:T(8,128)S(1)}, u32[]{:S(2)}, u32[]{:S(2)}) %collective-permute-start.15) | collective-permute-done | bytes 55328
  945.4 1.9 collective-permute-start.12
  947.3 1.9 collective-permute-start.11
  949.3 1.9 collective-permute-start.10
  953.8 4.8 concatenate.1
  958.6 1.9 collective-permute-start.9
  960.5 11.6 %collective-permute-done.13 = f32[16,1152]{1,0:T(8,128)S(1)} collective-permute-done((f32[16,1152]{1,0:T(8,128)}, f32[16,1152]{1,0:T(8,128)S(1)}, u32[]{:S(2)}, u32[]{:S(2)}) %collective-permute-start.13) | collective-permute-done | bytes 73760
  974.0 1.9 collective-permute-start.7
  978.8 1.9 collective-permute-start.5
  981.7 6.3 collective-permute-done.9
  990.0 10.8 %collective-permute-done.8 = f32[16,1152]{1,0:T(8,128)S(1)} collective-permute-done((f32[16,1152]{1,0:T(8,128)}, f32[16,1152]{1,0:T(8,128)S(1)}, u32[]{:S(2)}, u32[]{:S(2)}) %collective-permute-start.8) | collective-permute-done | bytes 73760
  1002.7 1.9 collective-permute-start.2
  1010.0 5.2 collective-permute-done.4
  1015.3 14.8 %collective-permute-done.3 = f32[16,1152]{1,0:T(8,128)S(1)} collective-permute-done((f32[16,1152]{1,0:T(8,128)}, f32[16,1152]{1,0:T(8,128)S(1)}, u32[]{:S(2)}, u32[]{:S(2)}) %collective-permute-start.3) | collective-permute-done | bytes 73760
  1031.5 2.2 collective-permute-done.1
  1035.1 3.1 concatenate
  (55 shorter events, 39.8 us)
Async XLA Ops:
  7.2 92.4 %copy-start.3 = (s32[12]{0:T(128)S(1)}, s32[12]{0:T(128)}, u32[]{:S(2)}) copy-start(s32[12]{0:T(128)} %param.7) | copy-start | bytes 148
  7.2 172.8 %all-gather.4.cloned.1.call-start = ((), (), s32[]{:S(2)}) async-start(), calls=%async_computation | async-start | bytes 2396160 | tf_op jit(solution)/shard_map/all_gather | solution.py:47
  97.5 85.0 %copy-start = (bf16[192,1152]{1,0:T(8,128)(2,1)}, bf16[192,1152]{1,0:T(8,128)(2,1)S(1)}, u32[]{:S(2)}) copy-start(bf16[192,1152]{1,0:T(8,128)(2,1)S(1)} %reshape.29) | copy-start | bytes 1327108
  267.6 677.8 %collective-permute-start.18 = (f32[16,1152]{1,0:T(8,128)}, f32[16,1152]{1,0:T(8,128)}, u32[]{:S(2)}, u32[]{:S(2)}) collective-permute-start(f32[16,1152]{1,0:T(8,128)} %fusion.1), channel_id=1, source_target_pairs={{0,192},{64,256},{128,320},{192,384},{256,448},{320,512},{384,576}... | collective-permute-start | bytes 221192
  268.9 678.4 %collective-permute-start.17 = (f32[16,1152]{1,0:T(8,128)}, f32[16,1152]{1,0:T(8,128)}, u32[]{:S(2)}, u32[]{:S(2)}) collective-permute-start(f32[16,1152]{1,0:T(8,128)} %fusion.1), channel_id=1, source_target_pairs={{0,128},{64,192},{128,256},{192,320},{256,384},{320,448},{384,512}... | collective-permute-start | bytes 221192
  270.2 679.1 %collective-permute-start.16 = (f32[16,1152]{1,0:T(8,128)}, f32[16,1152]{1,0:T(8,128)}, u32[]{:S(2)}, u32[]{:S(2)}) collective-permute-start(f32[16,1152]{1,0:T(8,128)} %fusion.1), channel_id=1, source_target_pairs={{0,64},{64,128},{128,192},{192,256},{256,320},{320,384},{384,448},... | collective-permute-start | bytes 221192
  286.4 632.0 %collective-permute-start.19 = (f32[12,1152]{1,0:T(8,128)}, f32[12,1152]{1,0:T(8,128)}, u32[]{:S(2)}, u32[]{:S(2)}) collective-permute-start(f32[12,1152]{1,0:T(8,128)} %slice.1), channel_id=1, source_target_pairs={{0,256},{64,320},{128,384},{192,448},{256,512},{320,576},{384,640}... | collective-permute-start | bytes 165896
  916.5 27.0 %collective-permute-start.15 = (f32[12,1152]{1,0:T(8,128)S(1)}, f32[12,1152]{1,0:T(8,128)S(1)}, u32[]{:S(2)}, u32[]{:S(2)}) collective-permute-start(f32[12,1152]{1,0:T(8,128)S(1)} %slice), channel_id=1, source_target_pairs={{0,16},{1,17},{2,18},{3,19},{4,20},{5,21},{6,22},{7,23},{8,24},{9,... | collective-permute-start | bytes 165896
  918.4 40.2 %collective-permute-start.14 = (f32[16,1152]{1,0:T(8,128)}, f32[16,1152]{1,0:T(8,128)S(1)}, u32[]{:S(2)}, u32[]{:S(2)}) collective-permute-start(f32[16,1152]{1,0:T(8,128)} %fusion), channel_id=1, source_target_pairs={{0,15},{1,16},{2,17},{3,18},{4,19},{5,20},{6,21},{7,22},{8,23},{9,... | collective-permute-start | bytes 221192
  943.5 28.6 %collective-permute-start.13 = (f32[16,1152]{1,0:T(8,128)}, f32[16,1152]{1,0:T(8,128)S(1)}, u32[]{:S(2)}, u32[]{:S(2)}) collective-permute-start(f32[16,1152]{1,0:T(8,128)} %fusion), channel_id=1, source_target_pairs={{0,14},{1,15},{2,16},{3,17},{4,18},{5,19},{6,20},{7,21},{8,22},{9,... | collective-permute-start | bytes 221192
  945.4 28.6 %collective-permute-start.12 = (f32[16,1152]{1,0:T(8,128)}, f32[16,1152]{1,0:T(8,128)S(1)}, u32[]{:S(2)}, u32[]{:S(2)}) collective-permute-start(f32[16,1152]{1,0:T(8,128)} %fusion), channel_id=1, source_target_pairs={{0,13},{1,14},{2,15},{3,16},{4,17},{5,18},{6,19},{7,20},{8,21},{9,... | collective-permute-start | bytes 221192
  947.3 29.6 %collective-permute-start.11 = (f32[16,1152]{1,0:T(8,128)}, f32[16,1152]{1,0:T(8,128)S(1)}, u32[]{:S(2)}, u32[]{:S(2)}) collective-permute-start(f32[16,1152]{1,0:T(8,128)} %fusion), channel_id=1, source_target_pairs={{0,12},{1,13},{2,14},{3,15},{4,16},{5,17},{6,18},{7,19},{8,20},{9,... | collective-permute-start | bytes 221192
  949.3 29.6 %collective-permute-start.10 = (f32[16,1152]{1,0:T(8,128)}, f32[16,1152]{1,0:T(8,128)S(1)}, u32[]{:S(2)}, u32[]{:S(2)}) collective-permute-start(f32[16,1152]{1,0:T(8,128)} %fusion), channel_id=1, source_target_pairs={{0,11},{1,12},{2,13},{3,14},{4,15},{5,16},{6,17},{7,18},{8,19},{9,... | collective-permute-start | bytes 221192
  953.8 84.4 %copy-start.2 = (bf16[12,1152]{1,0:T(8,128)(2,1)S(1)}, bf16[12,1152]{1,0:T(8,128)(2,1)}, u32[]{:S(2)}) copy-start(bf16[12,1152]{1,0:T(8,128)(2,1)} %param.5) | copy-start | bytes 82948
  958.6 29.5 %collective-permute-start.9 = (f32[16,1152]{1,0:T(8,128)}, f32[16,1152]{1,0:T(8,128)S(1)}, u32[]{:S(2)}, u32[]{:S(2)}) collective-permute-start(f32[16,1152]{1,0:T(8,128)} %fusion), channel_id=1, source_target_pairs={{0,10},{1,11},{2,12},{3,13},{4,14},{5,15},{6,16},{7,17},{8,18},{9,... | collective-permute-start | bytes 221192
  972.1 28.7 %collective-permute-start.8 = (f32[16,1152]{1,0:T(8,128)}, f32[16,1152]{1,0:T(8,128)S(1)}, u32[]{:S(2)}, u32[]{:S(2)}) collective-permute-start(f32[16,1152]{1,0:T(8,128)} %fusion), channel_id=1, source_target_pairs={{0,9},{1,10},{2,11},{3,12},{4,13},{5,14},{6,15},{7,16},{8,17},{9,1... | collective-permute-start | bytes 221192
  974.0 28.7 %collective-permute-start.7 = (f32[16,1152]{1,0:T(8,128)}, f32[16,1152]{1,0:T(8,128)S(1)}, u32[]{:S(2)}, u32[]{:S(2)}) collective-permute-start(f32[16,1152]{1,0:T(8,128)} %fusion), channel_id=1, source_target_pairs={{0,8},{1,9},{2,10},{3,11},{4,12},{5,13},{6,14},{7,15},{8,16},{9,17... | collective-permute-start | bytes 221192
  976.9 27.7 %collective-permute-start.6 = (f32[16,1152]{1,0:T(8,128)}, f32[16,1152]{1,0:T(8,128)S(1)}, u32[]{:S(2)}, u32[]{:S(2)}) collective-permute-start(f32[16,1152]{1,0:T(8,128)} %fusion), channel_id=1, source_target_pairs={{0,7},{1,8},{2,9},{3,10},{4,11},{5,12},{6,13},{7,14},{8,15},{9,16}... | collective-permute-start | bytes 221192
  978.8 27.8 %collective-permute-start.5 = (f32[16,1152]{1,0:T(8,128)}, f32[16,1152]{1,0:T(8,128)S(1)}, u32[]{:S(2)}, u32[]{:S(2)}) collective-permute-start(f32[16,1152]{1,0:T(8,128)} %fusion), channel_id=1, source_target_pairs={{0,6},{1,7},{2,8},{3,9},{4,10},{5,11},{6,12},{7,13},{8,14},{9,15},... | collective-permute-start | bytes 221192
  988.1 27.2 %collective-permute-start.4 = (f32[16,1152]{1,0:T(8,128)}, f32[16,1152]{1,0:T(8,128)S(1)}, u32[]{:S(2)}, u32[]{:S(2)}) collective-permute-start(f32[16,1152]{1,0:T(8,128)} %fusion), channel_id=1, source_target_pairs={{0,5},{1,6},{2,7},{3,8},{4,9},{5,10},{6,11},{7,12},{8,13},{9,14},{... | collective-permute-start | bytes 221192
  1000.8 29.3 %collective-permute-start.3 = (f32[16,1152]{1,0:T(8,128)}, f32[16,1152]{1,0:T(8,128)S(1)}, u32[]{:S(2)}, u32[]{:S(2)}) collective-permute-start(f32[16,1152]{1,0:T(8,128)} %fusion), channel_id=1, source_target_pairs={{0,4},{1,5},{2,6},{3,7},{4,8},{5,9},{6,10},{7,11},{8,12},{9,13},{1... | collective-permute-start | bytes 221192
  1002.7 28.7 %collective-permute-start.2 = (f32[16,1152]{1,0:T(8,128)}, f32[16,1152]{1,0:T(8,128)S(1)}, u32[]{:S(2)}, u32[]{:S(2)}) collective-permute-start(f32[16,1152]{1,0:T(8,128)} %fusion), channel_id=1, source_target_pairs={{0,3},{1,4},{2,5},{3,6},{4,7},{5,8},{6,9},{7,10},{8,11},{9,12},{10... | collective-permute-start | bytes 221192
  1004.7 29.0 %collective-permute-start.1 = (f32[16,1152]{1,0:T(8,128)}, f32[16,1152]{1,0:T(8,128)S(1)}, u32[]{:S(2)}, u32[]{:S(2)}) collective-permute-start(f32[16,1152]{1,0:T(8,128)} %fusion), channel_id=1, source_target_pairs={{0,2},{1,3},{2,4},{3,5},{4,6},{5,7},{6,8},{7,9},{8,10},{9,11},{10,... | collective-permute-start | bytes 221192
  1006.6 28.4 %collective-permute-start = (f32[16,1152]{1,0:T(8,128)}, f32[16,1152]{1,0:T(8,128)S(1)}, u32[]{:S(2)}, u32[]{:S(2)}) collective-permute-start(f32[16,1152]{1,0:T(8,128)} %fusion), channel_id=1, source_target_pairs={{0,1},{1,2},{2,3},{3,4},{4,5},{5,6},{6,7},{7,8},{8,9},{9,10},{10,1... | collective-permute-start | bytes 221192
  (1 other events, 0.7 us)
Sparse Core Ops, SparseCore 0:
  14.4 165.5 all-gather.3
where the time goes:
time: 1050 us
  blocking collectives  848 us (81%)
  waiting for transfers between devices  105 us (10%)
  starting transfers between devices  48.9 us (5%)
  between operations  17.6 us (2%)
  local copies, waits for them, and re-layouts  16.6 us (2%)
    unnamed x3, blocking collectives  763 us
    all_gather x1, blocking collectives, shards(): lax.all_gather(sentence_sent_onward, 'row', axis=0, tiled=True)  84.7 us
    unnamed x21, waiting for transfers between devices  77.9 us
    unnamed x20, starting transfers between devices  48.9 us
    all_gather x1, waiting for transfers between devices, shards(): photo_tile = lax.all_gather(img_send, 'col', axis=0, tiled=True)  26.7 us
  transfers between devices with their start and end apart: 21, of which 11 were waited for; matrix products, arithmetic and copies ran while one was open for 61% of the time, Pallas kernels for 0%

commit v1 on v0

v1 whole, which is shorter than its diff:
```python
import jax
import jax.numpy as jnp
from jax import lax
from jax.sharding import PartitionSpec as P

NZ, NX, NY, NC = 32, 4, 4, 2
OWN = 12
SLOT = 16
BOTH = ("row", "col")


def device_at(z, x, y, c):
    return (z % 16) * 64 + (z // 16) * 32 + x * 8 + y * 2 + c


def send(value, dz=0, dx=0, dy=0, dc=0):
    pairs = [
        (
            device_at(z, x, y, c),
            device_at((z + dz) % NZ, (x + dx) % NX, (y + dy) % NY, (c + dc) % NC),
        )
        for z in range(NZ)
        for x in range(NX)
        for y in range(NY)
        for c in range(NC)
    ]
    return lax.ppermute(value, BOTH, pairs)


IMG_Z = (0, 16, -2, 14)
TXT_Z = (0, 8, 4, 12, 1, 9, 5, 13)
RING = (0, 1, -1, 2)


def unit_rows(raw):
    values = raw.astype(jnp.float32)
    scale = lax.rsqrt(jnp.sum(values * values, axis=1, keepdims=True) + 1e-06)
    return (values * scale, scale)


def back_through(unit, scale, upstream):
    inner = jnp.sum(unit * upstream, axis=1, keepdims=True)
    return scale * (upstream - unit * inner)


def cat(*parts):
    return jnp.concatenate(parts, axis=0)


def gather_images(block):
    with jax.named_scope("img_z16"):
        block = cat(block, send(block, dz=16))
    with jax.named_scope("img_z2"):
        block = cat(block, send(block, dz=2))
    with jax.named_scope("img_x"):
        block = cat(block, *(send(block, dx=-k) for k in RING[1:]))
    with jax.named_scope("img_core"):
        return cat(block, send(block, dc=1))


def gather_texts(block):
    with jax.named_scope("txt_z8"):
        block = cat(block, send(block, dz=-8))
    with jax.named_scope("txt_z4"):
        block = cat(block, send(block, dz=-4))
    with jax.named_scope("txt_z1"):
        block = cat(block, send(block, dz=-1))
    with jax.named_scope("txt_y"):
        return cat(block, *(send(block, dy=-k) for k in RING[1:]))


def halve(total, **shift):
    rows = total.shape[0] // 2
    return total[:rows] + send(total[rows:].astype(jnp.bfloat16), **shift).astype(jnp.float32)


def quarter(total, axis):
    rows = total.shape[0] // 4
    acc = total[:rows]
    for g in (1, 2, 3):
        part = total[g * rows : (g + 1) * rows].astype(jnp.bfloat16)
        acc = acc + send(part, **{axis: RING[g]}).astype(jnp.float32)
    return acc


def reduce_images(total):
    with jax.named_scope("img_core_sum"):
        total = halve(total, dc=1)
    with jax.named_scope("img_x_sum"):
        total = quarter(total, "dx")
    with jax.named_scope("img_z2_sum"):
        total = halve(total, dz=-2)
    with jax.named_scope("img_z16_sum"):
        return halve(total, dz=16)


def reduce_texts(total):
    with jax.named_scope("txt_y_sum"):
        total = quarter(total, "dy")
    with jax.named_scope("txt_z1_sum"):
        total = halve(total, dz=1)
    with jax.named_scope("txt_z4_sum"):
        total = halve(total, dz=4)
    with jax.named_scope("txt_z8_sum"):
        return halve(total, dz=8)


def image_ids(z, x, y, c):
    row = lax.iota(jnp.int32, 32 * SLOT)
    r = row % SLOT
    slot = row // SLOT
    zslot, xslot, cslot = slot % 4, (slot // 4) % 4, slot // 16
    zoff = jnp.where(zslot % 2 == 1, 16, 0) + jnp.where(zslot >= 2, NZ - 2, 0)
    xoff = jnp.where(xslot == 1, 1, jnp.where(xslot == 2, NX - 1, jnp.where(xslot == 3, 2, 0)))
    owner = device_at((z + zoff) % NZ, (x + xoff) % NX, y, (c + cslot) % NC)
    return jnp.where(r < OWN, owner * OWN + r, -1)


def shards(
    photo_features, sentence_features, described_photo_number, logit_multiplier, logit_offset
):
    img_unit, img_scale = unit_rows(photo_features)
    txt_unit, txt_scale = unit_rows(sentence_features)
    pad = SLOT - OWN
    img_block = jnp.pad(img_unit.astype(jnp.bfloat16), ((0, pad), (0, 0)))
    width = txt_unit.shape[1]
    ids = jnp.stack([described_photo_number // 128, described_photo_number % 128])
    ids = jnp.pad(ids.astype(jnp.bfloat16), ((0, pad - 2), (0, width - OWN)))
    txt_block = cat(txt_unit.astype(jnp.bfloat16), ids)

    imgs = gather_images(img_block)
    txts = gather_texts(txt_block)

    low = lax.axis_index("row")
    rest = lax.axis_index("col")
    z, x, y, c = (rest // 32) * 16 + low, (rest // 8) % 4, (rest // 2) % 4, rest % 2
    coded = txts.reshape(32, SLOT, width)[:, OWN : OWN + 2, :OWN].astype(jnp.int32)
    numbers = jnp.pad(coded[:, 0] * 128 + coded[:, 1], ((0, 0), (0, pad)), constant_values=-2)
    numbers = numbers.reshape(32 * SLOT)
    used = lax.iota(jnp.int32, 32 * SLOT) % SLOT < OWN
    txts = jnp.where(used[:, None], txts, jnp.zeros_like(txts))

    logits = (
        logit_multiplier
        * jnp.einsum("id,jd->ij", imgs, txts, preferred_element_type=jnp.float32)
        + logit_offset
    )
    ids = image_ids(z, x, y, c)
    sign = jnp.where(ids[:, None] == numbers[None, :], 1.0, -1.0).astype(jnp.float32)
    weights = (logit_multiplier * -sign * jax.nn.sigmoid(-sign * logits)).astype(jnp.bfloat16)
    txt_part = jnp.einsum("ij,id->jd", weights, imgs, preferred_element_type=jnp.float32)
    img_part = jnp.dot(weights, txts, preferred_element_type=jnp.float32)

    img_upstream = reduce_images(img_part)[:OWN]
    txt_upstream = reduce_texts(txt_part)[:OWN]
    return (
        back_through(img_unit, img_scale, img_upstream),
        back_through(txt_unit, txt_scale, txt_upstream),
    )


def solution(mesh):
    placed = (P(("row", "col"), None), P(("row", "col"), None), P(("row", "col")), P(), P())
    return jax.shard_map(
        shards,
        mesh=mesh,
        in_specs=placed,
        out_specs=(P(("row", "col"), None), P(("row", "col"), None)),
        check_vma=False,
    )
```

time: 1050 us -> 198 us (0.19)
  the two profiles are of different devices: /device:TPU:960 before, /device:TPU:24 now
where the time goes in v1:
time: 198 us; the launch traced here: 196 us
  starting transfers between devices  109 us (55%)
  waiting for transfers between devices  65.6 us (33%)
  local copies, waits for them, and re-layouts  8.96 us (5%)
  other arithmetic  7.6 us (4%)
  matrix products  3.12 us (2%)
  between operations  2.44 us (1%)
    ppermute x24, starting transfers between devices, send(): return lax.ppermute(value, BOTH, pairs)  109 us
    ppermute x24, waiting for transfers between devices, send(): return lax.ppermute(value, BOTH, pairs)  65.6 us
    concatenate x4, local copies, waits for them, and re-layouts, cat(): return jnp.concatenate(parts, axis=0)  4.92 us
  transfers between devices with their start and end apart: 24, of which 12 were waited for; matrix products, arithmetic and copies ran while one was open for 7% of the time, Pallas kernels for 0%

profile of v1, /device:TPU:24, one launch (start us, length us, event | category | flops | bytes accessed | tf_op | source)
XLA Modules:
  0.0 196.3 jit_solution(11405280450742120149)
XLA Ops:
  3.1 23.0 %collective-permute-start = (bf16[16,1152]{1,0:T(8,128)(2,1)S(1)}, bf16[16,1152]{1,0:T(8,128)(2,1)S(1)}, u32[]{:S(2)}, u32[]{:S(2)}) collective-permute-start(bf16[16,1152]{1,0:T(8,128)(2,1)S(1)} %pad_maximum_fusion.4), channel_id=1, source_target_pairs={{0,544},{1,545},{2,546},{3,547},{4,548},{5,549},{6,550},{7,551},{8... | collective-permute-start | bytes 110600 | tf_op jit(solution)/shard_map/txt_z8/ppermute | solution.py:27
  28.5 7.9 %collective-permute-start.6 = (bf16[16,1152]{1,0:T(8,128)(2,1)S(1)}, bf16[16,1152]{1,0:T(8,128)(2,1)S(1)}, u32[]{:S(2)}, u32[]{:S(2)}) collective-permute-start(bf16[16,1152]{1,0:T(8,128)(2,1)S(1)} %get-tuple-element.22), channel_id=1, source_target_pairs={{0,32},{1,33},{2,34},{3,35},{4,36},{5,37},{6,38},{7,39},{8,40},{9,... | collective-permute-start | bytes 110600 | tf_op jit(solution)/shard_map/img_z16/ppermute | solution.py:27
  36.4 3.2 %collective-permute-start.1 = (bf16[32,1152]{1,0:T(8,128)(2,1)S(1)}, bf16[32,1152]{1,0:T(8,128)(2,1)S(1)}, u32[]{:S(2)}, u32[]{:S(2)}) collective-permute-start(bf16[32,1152]{1,0:T(8,128)(2,1)S(1)} %pad_maximum_fusion.2), channel_id=1, source_target_pairs={{0,800},{1,801},{2,802},{3,803},{4,804},{5,805},{6,806},{7,807},{8... | collective-permute-start | bytes 221192 | tf_op jit(solution)/shard_map/txt_z4/ppermute | solution.py:27
  39.6 13.0 %collective-permute-done.6 = bf16[16,1152]{1,0:T(8,128)(2,1)S(1)} collective-permute-done((bf16[16,1152]{1,0:T(8,128)(2,1)S(1)}, bf16[16,1152]{1,0:T(8,128)(2,1)S(1)}, u32[]{:S(2)}, u32[]{:S(2)}) %collective-permute-start.6) | collective-permute-done | bytes 36896 | tf_op jit(solution)/shard_map/img_z16/ppermute | solution.py:27
  52.6 3.4 %collective-permute-start.7 = (bf16[32,1152]{1,0:T(8,128)(2,1)S(1)}, bf16[32,1152]{1,0:T(8,128)(2,1)S(1)}, u32[]{:S(2)}, u32[]{:S(2)}) collective-permute-start(bf16[32,1152]{1,0:T(8,128)(2,1)S(1)} %pad_maximum_fusion.3), channel_id=1, source_target_pairs={{0,128},{1,129},{2,130},{3,131},{4,132},{5,133},{6,134},{7,135},{8... | collective-permute-start | bytes 221192 | tf_op jit(solution)/shard_map/img_z2/ppermute | solution.py:27
  56.6 4.3 %collective-permute-done.7 = bf16[32,1152]{1,0:T(8,128)(2,1)S(1)} collective-permute-done((bf16[32,1152]{1,0:T(8,128)(2,1)S(1)}, bf16[32,1152]{1,0:T(8,128)(2,1)S(1)}, u32[]{:S(2)}, u32[]{:S(2)}) %collective-permute-start.7) | collective-permute-done | bytes 73760 | tf_op jit(solution)/shard_map/img_z2/ppermute | solution.py:27
  61.0 4.9 %collective-permute-start.10 = (bf16[64,1152]{1,0:T(8,128)(2,1)S(1)}, bf16[64,1152]{1,0:T(8,128)(2,1)S(1)}, u32[]{:S(2)}, u32[]{:S(2)}) collective-permute-start(bf16[64,1152]{1,0:T(8,128)(2,1)S(1)} %pad_maximum_fusion.1), channel_id=1, source_target_pairs={{0,16},{1,17},{2,18},{3,19},{4,20},{5,21},{6,22},{7,23},{8,24},{9,... | collective-permute-start | bytes 442376 | tf_op jit(solution)/shard_map/img_x/ppermute | solution.py:27
  68.4 4.6 %collective-permute-start.8 = (bf16[64,1152]{1,0:T(8,128)(2,1)S(1)}, bf16[64,1152]{1,0:T(8,128)(2,1)S(1)}, u32[]{:S(2)}, u32[]{:S(2)}) collective-permute-start(bf16[64,1152]{1,0:T(8,128)(2,1)S(1)} %pad_maximum_fusion.1), channel_id=1, source_target_pairs={{0,24},{1,25},{2,26},{3,27},{4,28},{5,29},{6,30},{7,31},{8,0},{9,1... | collective-permute-start | bytes 442376 | tf_op jit(solution)/shard_map/img_x/ppermute | solution.py:27
  73.0 4.7 %collective-permute-start.2 = (bf16[64,1152]{1,0:T(8,128)(2,1)S(1)}, bf16[64,1152]{1,0:T(8,128)(2,1)S(1)}, u32[]{:S(2)}, u32[]{:S(2)}) collective-permute-start(bf16[64,1152]{1,0:T(8,128)(2,1)S(1)} %pad_maximum_fusion), channel_id=1, source_target_pairs={{0,992},{1,993},{2,994},{3,995},{4,996},{5,997},{6,998},{7,999},{8... | collective-permute-start | bytes 442376 | tf_op jit(solution)/shard_map/txt_z1/ppermute | solution.py:27
  78.4 4.3 %collective-permute-done.2 = bf16[64,1152]{1,0:T(8,128)(2,1)S(1)} collective-permute-done((bf16[64,1152]{1,0:T(8,128)(2,1)S(1)}, bf16[64,1152]{1,0:T(8,128)(2,1)S(1)}, u32[]{:S(2)}, u32[]{:S(2)}) %collective-permute-start.2) | collective-permute-done | bytes 147488 | tf_op jit(solution)/shard_map/txt_z1/ppermute | solution.py:27
  82.8 3.1 %collective-permute-start.5 = (bf16[128,1152]{1,0:T(8,128)(2,1)S(1)}, bf16[128,1152]{1,0:T(8,128)(2,1)S(1)}, u32[]{:S(2)}, u32[]{:S(2)}) collective-permute-start(bf16[128,1152]{1,0:T(8,128)(2,1)S(1)} %concatenate.37), channel_id=1, source_target_pairs={{0,4},{1,5},{2,6},{3,7},{4,0},{5,1},{6,2},{7,3},{8,12},{9,13},{10,... | collective-permute-start | bytes 884744 | tf_op jit(solution)/shard_map/txt_y/ppermute | solution.py:27
  86.0 4.1 %collective-permute-start.4 = (bf16[128,1152]{1,0:T(8,128)(2,1)S(1)}, bf16[128,1152]{1,0:T(8,128)(2,1)}, u32[]{:S(2)}, u32[]{:S(2)}) collective-permute-start(bf16[128,1152]{1,0:T(8,128)(2,1)S(1)} %concatenate.37), channel_id=1, source_target_pairs={{0,2},{1,3},{2,4},{3,5},{4,6},{5,7},{6,0},{7,1},{8,10},{9,11},{10,... | collective-permute-start | bytes 884744 | tf_op jit(solution)/shard_map/txt_y/ppermute | solution.py:27
  100.0 4.0 %concatenate.38 = bf16[512,1152]{1,0:T(8,128)(2,1)S(1)} concatenate(bf16[12,1152]{1,0:T(8,128)(2,1)S(1)} %fusion.15, bf16[4,1152]{1,0:T(4,128)(2,1)S(1)} %fusion.32, bf16[16,1152]{1,0:T(8,128)(2,1)S(1)} %collective-permute-done, bf16[32,1152]{1,0:T(8,128)(2,1)S(1)} %collective-permute-done.1, bf16[64,1152]{1,0:T(8,128)(2,1)S(1)} %collective-permute-done.2, ...), dimensions={0} | concatenate | bytes 2359296 | tf_op jit(solution)/shard_map/txt_y/concatenate | solution.py:47
  107.0 3.5 %collective-permute-start.18 = (bf16[128,1152]{1,0:T(8,128)(2,1)S(1)}, bf16[128,1152]{1,0:T(8,128)(2,1)S(1)}, u32[]{:S(2)}, u32[]{:S(2)}) collective-permute-start(bf16[128,1152]{1,0:T(8,128)(2,1)S(1)} %get-tuple-element.4), channel_id=1, source_target_pairs={{0,2},{1,3},{2,4},{3,5},{4,6},{5,7},{6,0},{7,1},{8,10},{9,11},{10,... | collective-permute-start | bytes 884744 | tf_op jit(solution)/shard_map/txt_y_sum/ppermute | solution.py:27
  115.2 8.5 %collective-permute-done.18 = bf16[128,1152]{1,0:T(8,128)(2,1)S(1)} collective-permute-done((bf16[128,1152]{1,0:T(8,128)(2,1)S(1)}, bf16[128,1152]{1,0:T(8,128)(2,1)S(1)}, u32[]{:S(2)}, u32[]{:S(2)}) %collective-permute-start.18) | collective-permute-done | bytes 294944 | tf_op jit(solution)/shard_map/txt_y_sum/ppermute | solution.py:27
  123.8 5.6 %collective-permute-done.19 = bf16[128,1152]{1,0:T(8,128)(2,1)S(1)} collective-permute-done((bf16[128,1152]{1,0:T(8,128)(2,1)S(1)}, bf16[128,1152]{1,0:T(8,128)(2,1)S(1)}, u32[]{:S(2)}, u32[]{:S(2)}) %collective-permute-start.19) | collective-permute-done | bytes 294944 | tf_op jit(solution)/shard_map/txt_y_sum/ppermute | solution.py:27
  129.5 3.9 %collective-permute-start.21 = (bf16[64,1152]{1,0:T(8,128)(2,1)S(1)}, bf16[64,1152]{1,0:T(8,128)(2,1)S(1)}, u32[]{:S(2)}, u32[]{:S(2)}) collective-permute-start(bf16[64,1152]{1,0:T(8,128)(2,1)S(1)} %slice.180), channel_id=1, source_target_pairs={{0,64},{1,65},{2,66},{3,67},{4,68},{5,69},{6,70},{7,71},{8,72},{9,... | collective-permute-start | bytes 442376 | tf_op jit(solution)/shard_map/txt_z1_sum/ppermute | solution.py:27
  138.5 3.5 %collective-permute-start.22 = (bf16[32,1152]{1,0:T(8,128)(2,1)S(1)}, bf16[32,1152]{1,0:T(8,128)(2,1)S(1)}, u32[]{:S(2)}, u32[]{:S(2)}) collective-permute-start(bf16[32,1152]{1,0:T(8,128)(2,1)S(1)} %slice.181), channel_id=1, source_target_pairs={{0,256},{1,257},{2,258},{3,259},{4,260},{5,261},{6,262},{7,263},{8... | collective-permute-start | bytes 221192 | tf_op jit(solution)/shard_map/txt_z4_sum/ppermute | solution.py:27
  144.1 3.4 %collective-permute-start.15 = (bf16[64,1152]{1,0:T(8,128)(2,1)S(1)}, bf16[64,1152]{1,0:T(8,128)(2,1)S(1)}, u32[]{:S(2)}, u32[]{:S(2)}) collective-permute-start(bf16[64,1152]{1,0:T(8,128)(2,1)S(1)} %get-tuple-element.8), channel_id=1, source_target_pairs={{0,16},{1,17},{2,18},{3,19},{4,20},{5,21},{6,22},{7,23},{8,24},{9,... | collective-permute-start | bytes 442376 | tf_op jit(solution)/shard_map/img_x_sum/ppermute | solution.py:27
  147.5 3.7 %collective-permute-start.14 = (bf16[64,1152]{1,0:T(8,128)(2,1)S(1)}, bf16[64,1152]{1,0:T(8,128)(2,1)S(1)}, u32[]{:S(2)}, u32[]{:S(2)}) collective-permute-start(bf16[64,1152]{1,0:T(8,128)(2,1)S(1)} %get-tuple-element.9), channel_id=1, source_target_pairs={{0,24},{1,25},{2,26},{3,27},{4,28},{5,29},{6,30},{7,31},{8,0},{9,1... | collective-permute-start | bytes 442376 | tf_op jit(solution)/shard_map/img_x_sum/ppermute | solution.py:27
  156.3 4.5 %collective-permute-start.16 = (bf16[32,1152]{1,0:T(8,128)(2,1)S(1)}, bf16[32,1152]{1,0:T(8,128)(2,1)S(1)}, u32[]{:S(2)}, u32[]{:S(2)}) collective-permute-start(bf16[32,1152]{1,0:T(8,128)(2,1)S(1)} %slice.182), channel_id=1, source_target_pairs={{0,928},{1,929},{2,930},{3,931},{4,932},{5,933},{6,934},{7,935},{8... | collective-permute-start | bytes 221192 | tf_op jit(solution)/shard_map/img_z2_sum/ppermute | solution.py:27
  160.8 8.6 %collective-permute-done.23 = bf16[16,1152]{1,0:T(8,128)(2,1)S(1)} collective-permute-done((bf16[16,1152]{1,0:T(8,128)(2,1)S(1)}, bf16[16,1152]{1,0:T(8,128)(2,1)S(1)}, u32[]{:S(2)}, u32[]{:S(2)}) %collective-permute-start.23) | collective-permute-done | bytes 36896 | tf_op jit(solution)/shard_map/txt_z8_sum/ppermute | solution.py:27
  169.7 9.4 %collective-permute-start.17 = (bf16[16,1152]{1,0:T(8,128)(2,1)S(1)}, bf16[16,1152]{1,0:T(8,128)(2,1)S(1)}, u32[]{:S(2)}, u32[]{:S(2)}) collective-permute-start(bf16[16,1152]{1,0:T(8,128)(2,1)S(1)} %slice.184), channel_id=1, source_target_pairs={{0,32},{1,33},{2,34},{3,35},{4,36},{5,37},{6,38},{7,39},{8,40},{9,... | collective-permute-start | bytes 110600 | tf_op jit(solution)/shard_map/img_z16_sum/ppermute | solution.py:27
  179.8 15.7 %collective-permute-done.17 = bf16[16,1152]{1,0:T(8,128)(2,1)S(1)} collective-permute-done((bf16[16,1152]{1,0:T(8,128)(2,1)S(1)}, bf16[16,1152]{1,0:T(8,128)(2,1)S(1)}, u32[]{:S(2)}, u32[]{:S(2)}) %collective-permute-start.17) | collective-permute-done | bytes 36896 | tf_op jit(solution)/shard_map/img_z16_sum/ppermute | solution.py:27
  (88 shorter events, 39.2 us)
Async XLA Ops:
  3.1 33.3 %collective-permute-start = (bf16[16,1152]{1,0:T(8,128)(2,1)S(1)}, bf16[16,1152]{1,0:T(8,128)(2,1)S(1)}, u32[]{:S(2)}, u32[]{:S(2)}) collective-permute-start(bf16[16,1152]{1,0:T(8,128)(2,1)S(1)} %pad_maximum_fusion.4), channel_id=1, source_target_pairs={{0,544},{1,545},{2,546},{3,547},{4,548},{5,549},{6,550},{7,551},{8... | collective-permute-start | bytes 110600 | tf_op jit(solution)/shard_map/txt_z8/ppermute | solution.py:27
  28.5 24.2 %collective-permute-start.6 = (bf16[16,1152]{1,0:T(8,128)(2,1)S(1)}, bf16[16,1152]{1,0:T(8,128)(2,1)S(1)}, u32[]{:S(2)}, u32[]{:S(2)}) collective-permute-start(bf16[16,1152]{1,0:T(8,128)(2,1)S(1)} %get-tuple-element.22), channel_id=1, source_target_pairs={{0,32},{1,33},{2,34},{3,35},{4,36},{5,37},{6,38},{7,39},{8,40},{9,... | collective-permute-start | bytes 110600 | tf_op jit(solution)/shard_map/img_z16/ppermute | solution.py:27
  36.4 36.6 %collective-permute-start.1 = (bf16[32,1152]{1,0:T(8,128)(2,1)S(1)}, bf16[32,1152]{1,0:T(8,128)(2,1)S(1)}, u32[]{:S(2)}, u32[]{:S(2)}) collective-permute-start(bf16[32,1152]{1,0:T(8,128)(2,1)S(1)} %pad_maximum_fusion.2), channel_id=1, source_target_pairs={{0,800},{1,801},{2,802},{3,803},{4,804},{5,805},{6,806},{7,807},{8... | collective-permute-start | bytes 221192 | tf_op jit(solution)/shard_map/txt_z4/ppermute | solution.py:27
  52.6 8.3 %collective-permute-start.7 = (bf16[32,1152]{1,0:T(8,128)(2,1)S(1)}, bf16[32,1152]{1,0:T(8,128)(2,1)S(1)}, u32[]{:S(2)}, u32[]{:S(2)}) collective-permute-start(bf16[32,1152]{1,0:T(8,128)(2,1)S(1)} %pad_maximum_fusion.3), channel_id=1, source_target_pairs={{0,128},{1,129},{2,130},{3,131},{4,132},{5,133},{6,134},{7,135},{8... | collective-permute-start | bytes 221192 | tf_op jit(solution)/shard_map/img_z2/ppermute | solution.py:27
  61.0 32.4 %collective-permute-start.10 = (bf16[64,1152]{1,0:T(8,128)(2,1)S(1)}, bf16[64,1152]{1,0:T(8,128)(2,1)S(1)}, u32[]{:S(2)}, u32[]{:S(2)}) collective-permute-start(bf16[64,1152]{1,0:T(8,128)(2,1)S(1)} %pad_maximum_fusion.1), channel_id=1, source_target_pairs={{0,16},{1,17},{2,18},{3,19},{4,20},{5,21},{6,22},{7,23},{8,24},{9,... | collective-permute-start | bytes 442376 | tf_op jit(solution)/shard_map/img_x/ppermute | solution.py:27
  65.9 26.8 %collective-permute-start.9 = (bf16[64,1152]{1,0:T(8,128)(2,1)S(1)}, bf16[64,1152]{1,0:T(8,128)(2,1)S(1)}, u32[]{:S(2)}, u32[]{:S(2)}) collective-permute-start(bf16[64,1152]{1,0:T(8,128)(2,1)S(1)} %pad_maximum_fusion.1), channel_id=1, source_target_pairs={{0,8},{1,9},{2,10},{3,11},{4,12},{5,13},{6,14},{7,15},{8,16},{9,17... | collective-permute-start | bytes 442376 | tf_op jit(solution)/shard_map/img_x/ppermute | solution.py:27
  68.4 21.6 %collective-permute-start.8 = (bf16[64,1152]{1,0:T(8,128)(2,1)S(1)}, bf16[64,1152]{1,0:T(8,128)(2,1)S(1)}, u32[]{:S(2)}, u32[]{:S(2)}) collective-permute-start(bf16[64,1152]{1,0:T(8,128)(2,1)S(1)} %pad_maximum_fusion.1), channel_id=1, source_target_pairs={{0,24},{1,25},{2,26},{3,27},{4,28},{5,29},{6,30},{7,31},{8,0},{9,1... | collective-permute-start | bytes 442376 | tf_op jit(solution)/shard_map/img_x/ppermute | solution.py:27
  73.0 9.6 %collective-permute-start.2 = (bf16[64,1152]{1,0:T(8,128)(2,1)S(1)}, bf16[64,1152]{1,0:T(8,128)(2,1)S(1)}, u32[]{:S(2)}, u32[]{:S(2)}) collective-permute-start(bf16[64,1152]{1,0:T(8,128)(2,1)S(1)} %pad_maximum_fusion), channel_id=1, source_target_pairs={{0,992},{1,993},{2,994},{3,995},{4,996},{5,997},{6,998},{7,999},{8... | collective-permute-start | bytes 442376 | tf_op jit(solution)/shard_map/txt_z1/ppermute | solution.py:27
  82.8 15.6 %collective-permute-start.5 = (bf16[128,1152]{1,0:T(8,128)(2,1)S(1)}, bf16[128,1152]{1,0:T(8,128)(2,1)S(1)}, u32[]{:S(2)}, u32[]{:S(2)}) collective-permute-start(bf16[128,1152]{1,0:T(8,128)(2,1)S(1)} %concatenate.37), channel_id=1, source_target_pairs={{0,4},{1,5},{2,6},{3,7},{4,0},{5,1},{6,2},{7,3},{8,12},{9,13},{10,... | collective-permute-start | bytes 884744 | tf_op jit(solution)/shard_map/txt_y/ppermute | solution.py:27
  86.0 12.4 %collective-permute-start.4 = (bf16[128,1152]{1,0:T(8,128)(2,1)S(1)}, bf16[128,1152]{1,0:T(8,128)(2,1)}, u32[]{:S(2)}, u32[]{:S(2)}) collective-permute-start(bf16[128,1152]{1,0:T(8,128)(2,1)S(1)} %concatenate.37), channel_id=1, source_target_pairs={{0,2},{1,3},{2,4},{3,5},{4,6},{5,7},{6,0},{7,1},{8,10},{9,11},{10,... | collective-permute-start | bytes 884744 | tf_op jit(solution)/shard_map/txt_y/ppermute | solution.py:27
  90.1 9.9 %collective-permute-start.3 = (bf16[128,1152]{1,0:T(8,128)(2,1)S(1)}, bf16[128,1152]{1,0:T(8,128)(2,1)}, u32[]{:S(2)}, u32[]{:S(2)}) collective-permute-start(bf16[128,1152]{1,0:T(8,128)(2,1)S(1)} %concatenate.37), channel_id=1, source_target_pairs={{0,6},{1,7},{2,0},{3,1},{4,2},{5,3},{6,4},{7,5},{8,14},{9,15},{10,... | collective-permute-start | bytes 884744 | tf_op jit(solution)/shard_map/txt_y/ppermute | solution.py:27
  94.1 10.1 %collective-permute-start.11 = (bf16[256,1152]{1,0:T(8,128)(2,1)}, bf16[256,1152]{1,0:T(8,128)(2,1)S(1)}, u32[]{:S(2)}, u32[]{:S(2)}) collective-permute-start(bf16[256,1152]{1,0:T(8,128)(2,1)} %get-tuple-element.10), channel_id=1, source_target_pairs={{0,1},{1,0},{2,3},{3,2},{4,5},{5,4},{6,7},{7,6},{8,9},{9,8},{10,11... | collective-permute-start | bytes 1769480 | tf_op jit(solution)/shard_map/img_core/ppermute | solution.py:27
  107.0 16.8 %collective-permute-start.18 = (bf16[128,1152]{1,0:T(8,128)(2,1)S(1)}, bf16[128,1152]{1,0:T(8,128)(2,1)S(1)}, u32[]{:S(2)}, u32[]{:S(2)}) collective-permute-start(bf16[128,1152]{1,0:T(8,128)(2,1)S(1)} %get-tuple-element.4), channel_id=1, source_target_pairs={{0,2},{1,3},{2,4},{3,5},{4,6},{5,7},{6,0},{7,1},{8,10},{9,11},{10,... | collective-permute-start | bytes 884744 | tf_op jit(solution)/shard_map/txt_y_sum/ppermute | solution.py:27
  110.5 13.3 %collective-permute-start.20 = (bf16[128,1152]{1,0:T(8,128)(2,1)S(1)}, bf16[128,1152]{1,0:T(8,128)(2,1)S(1)}, u32[]{:S(2)}, u32[]{:S(2)}) collective-permute-start(bf16[128,1152]{1,0:T(8,128)(2,1)S(1)} %get-tuple-element.5), channel_id=1, source_target_pairs={{0,4},{1,5},{2,6},{3,7},{4,0},{5,1},{6,2},{7,3},{8,12},{9,13},{10,... | collective-permute-start | bytes 884744 | tf_op jit(solution)/shard_map/txt_y_sum/ppermute | solution.py:27
  112.5 16.9 %collective-permute-start.19 = (bf16[128,1152]{1,0:T(8,128)(2,1)S(1)}, bf16[128,1152]{1,0:T(8,128)(2,1)S(1)}, u32[]{:S(2)}, u32[]{:S(2)}) collective-permute-start(bf16[128,1152]{1,0:T(8,128)(2,1)S(1)} %get-tuple-element.6), channel_id=1, source_target_pairs={{0,6},{1,7},{2,0},{3,1},{4,2},{5,3},{6,4},{7,5},{8,14},{9,15},{10,... | collective-permute-start | bytes 884744 | tf_op jit(solution)/shard_map/txt_y_sum/ppermute | solution.py:27
  129.5 8.9 %collective-permute-start.21 = (bf16[64,1152]{1,0:T(8,128)(2,1)S(1)}, bf16[64,1152]{1,0:T(8,128)(2,1)S(1)}, u32[]{:S(2)}, u32[]{:S(2)}) collective-permute-start(bf16[64,1152]{1,0:T(8,128)(2,1)S(1)} %slice.180), channel_id=1, source_target_pairs={{0,64},{1,65},{2,66},{3,67},{4,68},{5,69},{6,70},{7,71},{8,72},{9,... | collective-permute-start | bytes 442376 | tf_op jit(solution)/shard_map/txt_z1_sum/ppermute | solution.py:27
  134.5 7.4 %collective-permute-start.12 = (bf16[256,1152]{1,0:T(8,128)(2,1)S(1)}, bf16[256,1152]{1,0:T(8,128)(2,1)S(1)}, u32[]{:S(2)}, u32[]{:S(2)}) collective-permute-start(bf16[256,1152]{1,0:T(8,128)(2,1)S(1)} %slice.179), channel_id=1, source_target_pairs={{0,1},{1,0},{2,3},{3,2},{4,5},{5,4},{6,7},{7,6},{8,9},{9,8},{10,11... | collective-permute-start | bytes 1769480 | tf_op jit(solution)/shard_map/img_core_sum/ppermute | solution.py:27
  138.5 14.0 %collective-permute-start.22 = (bf16[32,1152]{1,0:T(8,128)(2,1)S(1)}, bf16[32,1152]{1,0:T(8,128)(2,1)S(1)}, u32[]{:S(2)}, u32[]{:S(2)}) collective-permute-start(bf16[32,1152]{1,0:T(8,128)(2,1)S(1)} %slice.181), channel_id=1, source_target_pairs={{0,256},{1,257},{2,258},{3,259},{4,260},{5,261},{6,262},{7,263},{8... | collective-permute-start | bytes 221192 | tf_op jit(solution)/shard_map/txt_z4_sum/ppermute | solution.py:27
  142.2 13.5 %collective-permute-start.13 = (bf16[64,1152]{1,0:T(8,128)(2,1)S(1)}, bf16[64,1152]{1,0:T(8,128)(2,1)S(1)}, u32[]{:S(2)}, u32[]{:S(2)}) collective-permute-start(bf16[64,1152]{1,0:T(8,128)(2,1)S(1)} %get-tuple-element.7), channel_id=1, source_target_pairs={{0,8},{1,9},{2,10},{3,11},{4,12},{5,13},{6,14},{7,15},{8,16},{9,17... | collective-permute-start | bytes 442376 | tf_op jit(solution)/shard_map/img_x_sum/ppermute | solution.py:27
  144.1 11.6 %collective-permute-start.15 = (bf16[64,1152]{1,0:T(8,128)(2,1)S(1)}, bf16[64,1152]{1,0:T(8,128)(2,1)S(1)}, u32[]{:S(2)}, u32[]{:S(2)}) collective-permute-start(bf16[64,1152]{1,0:T(8,128)(2,1)S(1)} %get-tuple-element.8), channel_id=1, source_target_pairs={{0,16},{1,17},{2,18},{3,19},{4,20},{5,21},{6,22},{7,23},{8,24},{9,... | collective-permute-start | bytes 442376 | tf_op jit(solution)/shard_map/img_x_sum/ppermute | solution.py:27
  147.5 8.8 %collective-permute-start.14 = (bf16[64,1152]{1,0:T(8,128)(2,1)S(1)}, bf16[64,1152]{1,0:T(8,128)(2,1)S(1)}, u32[]{:S(2)}, u32[]{:S(2)}) collective-permute-start(bf16[64,1152]{1,0:T(8,128)(2,1)S(1)} %get-tuple-element.9), channel_id=1, source_target_pairs={{0,24},{1,25},{2,26},{3,27},{4,28},{5,29},{6,30},{7,31},{8,0},{9,1... | collective-permute-start | bytes 442376 | tf_op jit(solution)/shard_map/img_x_sum/ppermute | solution.py:27
  152.5 16.9 %collective-permute-start.23 = (bf16[16,1152]{1,0:T(8,128)(2,1)S(1)}, bf16[16,1152]{1,0:T(8,128)(2,1)S(1)}, u32[]{:S(2)}, u32[]{:S(2)}) collective-permute-start(bf16[16,1152]{1,0:T(8,128)(2,1)S(1)} %slice.183), channel_id=1, source_target_pairs={{0,512},{1,513},{2,514},{3,515},{4,516},{5,517},{6,518},{7,519},{8... | collective-permute-start | bytes 110600 | tf_op jit(solution)/shard_map/txt_z8_sum/ppermute | solution.py:27
  156.3 13.3 %collective-permute-start.16 = (bf16[32,1152]{1,0:T(8,128)(2,1)S(1)}, bf16[32,1152]{1,0:T(8,128)(2,1)S(1)}, u32[]{:S(2)}, u32[]{:S(2)}) collective-permute-start(bf16[32,1152]{1,0:T(8,128)(2,1)S(1)} %slice.182), channel_id=1, source_target_pairs={{0,928},{1,929},{2,930},{3,931},{4,932},{5,933},{6,934},{7,935},{8... | collective-permute-start | bytes 221192 | tf_op jit(solution)/shard_map/img_z2_sum/ppermute | solution.py:27
  169.7 25.8 %collective-permute-start.17 = (bf16[16,1152]{1,0:T(8,128)(2,1)S(1)}, bf16[16,1152]{1,0:T(8,128)(2,1)S(1)}, u32[]{:S(2)}, u32[]{:S(2)}) collective-permute-start(bf16[16,1152]{1,0:T(8,128)(2,1)S(1)} %slice.184), channel_id=1, source_target_pairs={{0,32},{1,33},{2,34},{3,35},{4,36},{5,37},{6,38},{7,39},{8,40},{9,... | collective-permute-start | bytes 110600 | tf_op jit(solution)/shard_map/img_z16_sum/ppermute | solution.py:27
  (6 other events, 170.2 us)

commit v2 on v0

v2 whole, which is shorter than its diff:
```python
import jax
import jax.numpy as jnp
from jax import lax
from jax.sharding import PartitionSpec as P

NZ, NX, NY = 32, 4, 4
OWN = 12
CHIP = 2 * OWN
LANES = 128
BOTH = ("row", "col")
RING = (0, 1, NX - 1, 2)


def device_at(z, x, y, c):
    return (z & 15) * 64 + (z >> 4) * 32 + x * 8 + y * 2 + c


def permute(value, images=None, texts=None):
    pairs = []
    for z in range(NZ):
        for x in range(NX):
            for y in range(NY):
                for c, to in enumerate((images, texts)):
                    if to is not None:
                        pairs.append((device_at(z, x, y, c), device_at(*to(z, x, y), c)))
    return lax.ppermute(value, BOTH, pairs)


def z_far(value):
    return permute(
        value,
        lambda z, x, y: (z ^ 8, x, y),
        lambda z, x, y: ((((z + 8) % NZ) ^ 8) - 8 & (NZ - 1), x, y),
    )


def z_mid(value):
    return permute(value, lambda z, x, y: (z ^ 2, x, y), lambda z, x, y: (z ^ 4, x, y))


def z_near(value):
    return permute(value, None, lambda z, x, y: (z ^ 1, x, y))


def along_ring(value, shift):
    return permute(
        value,
        lambda z, x, y: (z, (x + shift) % NX, y),
        lambda z, x, y: (z, x, (y + shift) % NY),
    )


def swap_cores(value):
    n = NZ * NX * NY * 2
    return lax.ppermute(value, BOTH, [(d, d ^ 1) for d in range(n)])


def unit_rows(raw):
    values = raw.astype(jnp.float32)
    scale = lax.rsqrt(jnp.sum(values * values, axis=1, keepdims=True) + 1e-06)
    return (values * scale, scale)


def back_through(unit, scale, upstream):
    inner = jnp.sum(unit * upstream, axis=1, keepdims=True)
    return scale * (upstream - unit * inner)


def cat(*parts):
    return jnp.concatenate(parts, axis=0)


def image_ids(z, x, y):
    row = lax.iota(jnp.int32, 16 * CHIP)
    group, zslot, r = row // (4 * CHIP), row // CHIP % 4, row % CHIP
    owner_z = z ^ jnp.where(zslot % 2 == 1, 8, 0) ^ jnp.where(zslot >= 2, 2, 0)
    step = jnp.where(group == 1, RING[1], jnp.where(group == 2, RING[2], jnp.where(group == 3, RING[3], 0)))
    owner = device_at(owner_z, (x + step) & (NX - 1), y, r // OWN)
    return owner * OWN + r % OWN


def shards(
    photo_features, sentence_features, described_photo_number, logit_multiplier, logit_offset
):
    low = lax.axis_index("row")
    rest = lax.axis_index("col")
    z, x, y = (rest >> 5) * 16 + low, (rest >> 3) & 3, (rest >> 1) & 3
    holds_images = (rest & 1) == 0

    img_unit, img_scale = unit_rows(photo_features)
    txt_unit, txt_scale = unit_rows(sentence_features)
    width = img_unit.shape[1]
    ids = jnp.stack([described_photo_number // 128, described_photo_number % 128], axis=1)
    ids = jnp.pad(ids.astype(jnp.bfloat16), ((0, 0), (0, LANES - 2)))
    img_block = jnp.pad(img_unit.astype(jnp.bfloat16), ((0, 0), (0, LANES)))
    txt_block = jnp.concatenate([txt_unit.astype(jnp.bfloat16), ids], axis=1)

    with jax.named_scope("pair_swap"):
        given = swap_cores(jnp.where(holds_images, txt_block, img_block))
        block = cat(jnp.where(holds_images, img_block, txt_block), given)
    with jax.named_scope("gather_z_far"):
        block = cat(block, z_far(block))
    with jax.named_scope("gather_z_mid"):
        block = cat(block, z_mid(block))
    with jax.named_scope("gather_z_near"):
        block = cat(block, z_near(block))
    with jax.named_scope("gather_ring"):
        groups = [block] + [along_ring(block, -k) for k in RING[1:]]
    half = 4 * CHIP
    with jax.named_scope("tile_swap"):
        first = cat(*(g[:half] for g in groups))
        other = swap_cores(first)
        second = cat(*(g[half:] for g in groups))

    imgs = jnp.where(holds_images, first, other)[:, :width]
    coded = jnp.where(holds_images, other, second)
    txts = coded[:, :width]
    numbers = coded[:, width].astype(jnp.int32) * 128 + coded[:, width + 1].astype(jnp.int32)

    logits = (
        logit_multiplier
        * jnp.einsum("jd,id->ji", txts, imgs, preferred_element_type=jnp.float32)
        + logit_offset
    )
    sign = jnp.where(numbers[:, None] == image_ids(z, x, y)[None, :], 1.0, -1.0).astype(jnp.float32)
    weights = (logit_multiplier * -sign * jax.nn.sigmoid(-sign * logits)).astype(jnp.bfloat16)
    txt_part = jnp.dot(weights, imgs, preferred_element_type=jnp.float32)
    img_part = jnp.einsum("ji,jd->id", weights, txts, preferred_element_type=jnp.float32)

    with jax.named_scope("tile_sum"):
        away = jnp.where(holds_images, txt_part, img_part).astype(jnp.bfloat16)
        home = jnp.where(holds_images, img_part, jnp.zeros_like(img_part))
        first = home + swap_cores(away).astype(jnp.float32)
    with jax.named_scope("ring_sum"):
        total = cat(first[:half], txt_part[:half])
        for g in (1, 2, 3):
            rows = slice(g * half, (g + 1) * half)
            part = cat(first[rows], txt_part[rows]).astype(jnp.bfloat16)
            total = total + along_ring(part, RING[g]).astype(jnp.float32)
    for name, swap in (("z_near_sum", z_near), ("z_mid_sum", z_mid), ("z_far_sum", z_far)):
        with jax.named_scope(name):
            rows = total.shape[0] // 2
            total = total[:rows] + swap(total[rows:].astype(jnp.bfloat16)).astype(jnp.float32)
    with jax.named_scope("pair_return"):
        kept, given = total[:OWN], swap_cores(total[OWN:])
    return (
        back_through(img_unit, img_scale, jnp.where(holds_images, kept, given)),
        back_through(txt_unit, txt_scale, jnp.where(holds_images, given, kept)),
    )


def solution(mesh):
    placed = (P(("row", "col"), None), P(("row", "col"), None), P(("row", "col")), P(), P())
    return jax.shard_map(
        shards,
        mesh=mesh,
        in_specs=placed,
        out_specs=(P(("row", "col"), None), P(("row", "col"), None)),
        check_vma=False,
    )
```

time: 1050 us -> 147 us (0.14)
  the two profiles are of different devices: /device:TPU:960 before, /device:TPU:1 now
where the time goes in v2:
time: 147 us; the launch traced here: 145 us
  starting transfers between devices  76 us (52%)
  waiting for transfers between devices  57.7 us (39%)
  other arithmetic  5.67 us (4%)
  between operations  2.27 us (2%)
  matrix products  2.2 us (1%)
    ppermute x12, starting transfers between devices, permute(): return lax.ppermute(value, BOTH, pairs)  54 us
    ppermute x12, waiting for transfers between devices, permute(): return lax.ppermute(value, BOTH, pairs)  52.4 us
    ppermute x4, starting transfers between devices, swap_cores(): return lax.ppermute(value, BOTH, [(d, d ^ 1) for d in range(n)])  22 us
    ppermute x4, waiting for transfers between devices, swap_cores(): return lax.ppermute(value, BOTH, [(d, d ^ 1) for d in range(n)])  5.37 us
  transfers between devices with their start and end apart: 16, of which 15 were waited for; matrix products, arithmetic and copies ran while one was open for 0% of the time, Pallas kernels for 0%

profile of v2, /device:TPU:1, one launch (start us, length us, event | category | flops | bytes accessed | tf_op | source)
XLA Modules:
  0.0 145.0 jit_solution(18289302538589158284)
XLA Ops:
  4.1 16.1 %collective-permute-start = (bf16[12,1280]{1,0:T(8,128)(2,1)S(1)}, bf16[12,1280]{1,0:T(8,128)(2,1)S(1)}, u32[]{:S(2)}, u32[]{:S(2)}) collective-permute-start(bf16[12,1280]{1,0:T(8,128)(2,1)S(1)} %get-tuple-element.20), channel_id=1, source_target_pairs={{0,1},{1,0},{2,3},{3,2},{4,5},{5,4},{6,7},{7,6},{8,9},{9,8},{10,11... | collective-permute-start | bytes 92168 | tf_op jit(solution)/shard_map/pair_swap/ppermute | solution.py:55
  21.1 10.1 %collective-permute-start.1 = (bf16[24,1280]{1,0:T(8,128)(2,1)S(1)}, bf16[24,1280]{1,0:T(8,128)(2,1)S(1)}, u32[]{:S(2)}, u32[]{:S(2)}) collective-permute-start(bf16[24,1280]{1,0:T(8,128)(2,1)S(1)} %pad_maximum_fusion.5), channel_id=1, source_target_pairs={{0,512},{1,545},{2,514},{3,547},{4,516},{5,549},{6,518},{7,551},{8... | collective-permute-start | bytes 184328 | tf_op jit(solution)/shard_map/gather_z_far/ppermute | solution.py:26
  31.2 3.6 %collective-permute-done.1 = bf16[24,1280]{1,0:T(8,128)(2,1)S(1)} collective-permute-done((bf16[24,1280]{1,0:T(8,128)(2,1)S(1)}, bf16[24,1280]{1,0:T(8,128)(2,1)S(1)}, u32[]{:S(2)}, u32[]{:S(2)}) %collective-permute-start.1) | collective-permute-done | bytes 61472 | tf_op jit(solution)/shard_map/gather_z_far/ppermute | solution.py:26
  34.8 2.5 %collective-permute-start.2 = (bf16[48,1280]{1,0:T(8,128)(2,1)S(1)}, bf16[48,1280]{1,0:T(8,128)(2,1)S(1)}, u32[]{:S(2)}, u32[]{:S(2)}) collective-permute-start(bf16[48,1280]{1,0:T(8,128)(2,1)S(1)} %pad_maximum_fusion.4), channel_id=1, source_target_pairs={{0,128},{1,257},{2,130},{3,259},{4,132},{5,261},{6,134},{7,263},{8... | collective-permute-start | bytes 368648 | tf_op jit(solution)/shard_map/gather_z_mid/ppermute | solution.py:26
  37.3 9.8 %collective-permute-done.2 = bf16[48,1280]{1,0:T(8,128)(2,1)S(1)} collective-permute-done((bf16[48,1280]{1,0:T(8,128)(2,1)S(1)}, bf16[48,1280]{1,0:T(8,128)(2,1)S(1)}, u32[]{:S(2)}, u32[]{:S(2)}) %collective-permute-start.2) | collective-permute-done | bytes 122912 | tf_op jit(solution)/shard_map/gather_z_mid/ppermute | solution.py:26
  47.1 1.9 %collective-permute-start.3 = (bf16[96,1280]{1,0:T(8,128)(2,1)S(1)}, bf16[96,1280]{1,0:T(8,128)(2,1)S(1)}, u32[]{:S(2)}, u32[]{:S(2)}) collective-permute-start(bf16[96,1280]{1,0:T(8,128)(2,1)S(1)} %pad_maximum_fusion.3), channel_id=1, source_target_pairs={{1,65},{3,67},{5,69},{7,71},{9,73},{11,75},{13,77},{15,79},{17,81}... | collective-permute-start | bytes 737288 | tf_op jit(solution)/shard_map/gather_z_near/ppermute | solution.py:26
  49.0 5.3 %collective-permute-done.3 = bf16[96,1280]{1,0:T(8,128)(2,1)S(1)} collective-permute-done((bf16[96,1280]{1,0:T(8,128)(2,1)S(1)}, bf16[96,1280]{1,0:T(8,128)(2,1)S(1)}, u32[]{:S(2)}, u32[]{:S(2)}) %collective-permute-start.3) | collective-permute-done | bytes 245792 | tf_op jit(solution)/shard_map/gather_z_near/ppermute | solution.py:26
  54.6 4.9 %collective-permute-start.6 = (bf16[192,1280]{1,0:T(8,128)(2,1)S(1)}, bf16[192,1280]{1,0:T(8,128)(2,1)S(1)}, u32[]{:S(2)}, u32[]{:S(2)}) collective-permute-start(bf16[192,1280]{1,0:T(8,128)(2,1)S(1)} %concatenate.44), channel_id=1, source_target_pairs={{0,16},{1,5},{2,18},{3,7},{4,20},{5,1},{6,22},{7,3},{8,24},{9,13},... | collective-permute-start | bytes 1474568 | tf_op jit(solution)/shard_map/gather_ring/ppermute | solution.py:26
  59.5 2.3 %collective-permute-start.5 = (bf16[192,1280]{1,0:T(8,128)(2,1)S(1)}, bf16[192,1280]{1,0:T(8,128)(2,1)S(1)}, u32[]{:S(2)}, u32[]{:S(2)}) collective-permute-start(bf16[192,1280]{1,0:T(8,128)(2,1)S(1)} %concatenate.44), channel_id=1, source_target_pairs={{0,8},{1,3},{2,10},{3,5},{4,12},{5,7},{6,14},{7,1},{8,16},{9,11},{... | collective-permute-start | bytes 1474568 | tf_op jit(solution)/shard_map/gather_ring/ppermute | solution.py:26
  61.8 4.2 %collective-permute-start.4 = (bf16[192,1280]{1,0:T(8,128)(2,1)S(1)}, bf16[192,1280]{1,0:T(8,128)(2,1)S(1)}, u32[]{:S(2)}, u32[]{:S(2)}) collective-permute-start(bf16[192,1280]{1,0:T(8,128)(2,1)S(1)} %concatenate.44), channel_id=1, source_target_pairs={{0,24},{1,7},{2,26},{3,1},{4,28},{5,3},{6,30},{7,5},{8,0},{9,15},{... | collective-permute-start | bytes 1474568 | tf_op jit(solution)/shard_map/gather_ring/ppermute | solution.py:26
  66.0 4.9 %collective-permute-done.5 = bf16[192,1280]{1,0:T(8,128)(2,1)S(1)} collective-permute-done((bf16[192,1280]{1,0:T(8,128)(2,1)S(1)}, bf16[192,1280]{1,0:T(8,128)(2,1)S(1)}, u32[]{:S(2)}, u32[]{:S(2)}) %collective-permute-start.5) | collective-permute-done | bytes 491552 | tf_op jit(solution)/shard_map/gather_ring/ppermute | solution.py:26
  79.4 2.0 %collective-permute-start.8 = (bf16[384,1152]{1,0:T(8,128)(2,1)S(1)}, bf16[384,1152]{1,0:T(8,128)(2,1)S(1)}, u32[]{:S(2)}, u32[]{:S(2)}) collective-permute-start(bf16[384,1152]{1,0:T(8,128)(2,1)S(1)} %get-tuple-element.24), channel_id=1, source_target_pairs={{0,1},{1,0},{2,3},{3,2},{4,5},{5,4},{6,7},{7,6},{8,9},{9,8},{10,11... | collective-permute-start | bytes 2654216 | tf_op jit(solution)/shard_map/tile_sum/ppermute | solution.py:55
  81.6 2.1 %collective-permute-done.8 = bf16[384,1152]{1,0:T(8,128)(2,1)S(1)} collective-permute-done((bf16[384,1152]{1,0:T(8,128)(2,1)S(1)}, bf16[384,1152]{1,0:T(8,128)(2,1)S(1)}, u32[]{:S(2)}, u32[]{:S(2)}) %collective-permute-start.8) | collective-permute-done | bytes 884768 | tf_op jit(solution)/shard_map/tile_sum/ppermute | solution.py:55
  84.0 5.0 %collective-permute-start.10 = (bf16[192,1152]{1,0:T(8,128)(2,1)S(1)}, bf16[192,1152]{1,0:T(8,128)(2,1)S(1)}, u32[]{:S(2)}, u32[]{:S(2)}) collective-permute-start(bf16[192,1152]{1,0:T(8,128)(2,1)S(1)} %pad_maximum_fusion.1), channel_id=1, source_target_pairs={{0,24},{1,7},{2,26},{3,1},{4,28},{5,3},{6,30},{7,5},{8,0},{9,15},{... | collective-permute-start | bytes 1327112 | tf_op jit(solution)/shard_map/ring_sum/ppermute | solution.py:26
  91.1 2.5 %collective-permute-start.9 = (bf16[192,1152]{1,0:T(8,128)(2,1)S(1)}, bf16[192,1152]{1,0:T(8,128)(2,1)S(1)}, u32[]{:S(2)}, u32[]{:S(2)}) collective-permute-start(bf16[192,1152]{1,0:T(8,128)(2,1)S(1)} %pad_maximum_fusion), channel_id=1, source_target_pairs={{0,8},{1,3},{2,10},{3,5},{4,12},{5,7},{6,14},{7,1},{8,16},{9,11},{... | collective-permute-start | bytes 1327112 | tf_op jit(solution)/shard_map/ring_sum/ppermute | solution.py:26
  93.7 5.4 %collective-permute-done.10 = bf16[192,1152]{1,0:T(8,128)(2,1)S(1)} collective-permute-done((bf16[192,1152]{1,0:T(8,128)(2,1)S(1)}, bf16[192,1152]{1,0:T(8,128)(2,1)S(1)}, u32[]{:S(2)}, u32[]{:S(2)}) %collective-permute-start.10) | collective-permute-done | bytes 442400 | tf_op jit(solution)/shard_map/ring_sum/ppermute | solution.py:26
  100.0 4.7 %collective-permute-done.9 = bf16[192,1152]{1,0:T(8,128)(2,1)S(1)} collective-permute-done((bf16[192,1152]{1,0:T(8,128)(2,1)S(1)}, bf16[192,1152]{1,0:T(8,128)(2,1)S(1)}, u32[]{:S(2)}, u32[]{:S(2)}) %collective-permute-start.9) | collective-permute-done | bytes 442400 | tf_op jit(solution)/shard_map/ring_sum/ppermute | solution.py:26
  105.0 3.4 %collective-permute-start.12 = (bf16[96,1152]{1,0:T(8,128)(2,1)S(1)}, bf16[96,1152]{1,0:T(8,128)(2,1)S(1)}, u32[]{:S(2)}, u32[]{:S(2)}) collective-permute-start(bf16[96,1152]{1,0:T(8,128)(2,1)S(1)} %slice.168), channel_id=1, source_target_pairs={{1,65},{3,67},{5,69},{7,71},{9,73},{11,75},{13,77},{15,79},{17,81}... | collective-permute-start | bytes 663560 | tf_op jit(solution)/shard_map/z_near_sum/ppermute | solution.py:26
  108.4 3.6 %collective-permute-done.12 = bf16[96,1152]{1,0:T(8,128)(2,1)S(1)} collective-permute-done((bf16[96,1152]{1,0:T(8,128)(2,1)S(1)}, bf16[96,1152]{1,0:T(8,128)(2,1)S(1)}, u32[]{:S(2)}, u32[]{:S(2)}) %collective-permute-start.12) | collective-permute-done | bytes 221216 | tf_op jit(solution)/shard_map/z_near_sum/ppermute | solution.py:26
  112.1 1.9 %collective-permute-start.13 = (bf16[48,1152]{1,0:T(8,128)(2,1)S(1)}, bf16[48,1152]{1,0:T(8,128)(2,1)S(1)}, u32[]{:S(2)}, u32[]{:S(2)}) collective-permute-start(bf16[48,1152]{1,0:T(8,128)(2,1)S(1)} %slice.169), channel_id=1, source_target_pairs={{0,128},{1,257},{2,130},{3,259},{4,132},{5,261},{6,134},{7,263},{8... | collective-permute-start | bytes 331784 | tf_op jit(solution)/shard_map/z_mid_sum/ppermute | solution.py:26
  114.0 11.0 %collective-permute-done.13 = bf16[48,1152]{1,0:T(8,128)(2,1)S(1)} collective-permute-done((bf16[48,1152]{1,0:T(8,128)(2,1)S(1)}, bf16[48,1152]{1,0:T(8,128)(2,1)S(1)}, u32[]{:S(2)}, u32[]{:S(2)}) %collective-permute-start.13) | collective-permute-done | bytes 110624 | tf_op jit(solution)/shard_map/z_mid_sum/ppermute | solution.py:26
  125.1 13.4 %collective-permute-start.14 = (bf16[24,1152]{1,0:T(8,128)(2,1)S(1)}, bf16[24,1152]{1,0:T(8,128)(2,1)S(1)}, u32[]{:S(2)}, u32[]{:S(2)}) collective-permute-start(bf16[24,1152]{1,0:T(8,128)(2,1)S(1)} %slice.170), channel_id=1, source_target_pairs={{0,512},{1,545},{2,514},{3,547},{4,516},{5,549},{6,518},{7,551},{8... | collective-permute-start | bytes 165896 | tf_op jit(solution)/shard_map/z_far_sum/ppermute | solution.py:26
  138.5 2.3 %collective-permute-done.14 = bf16[24,1152]{1,0:T(8,128)(2,1)S(1)} collective-permute-done((bf16[24,1152]{1,0:T(8,128)(2,1)S(1)}, bf16[24,1152]{1,0:T(8,128)(2,1)S(1)}, u32[]{:S(2)}, u32[]{:S(2)}) %collective-permute-start.14) | collective-permute-done | bytes 55328 | tf_op jit(solution)/shard_map/z_far_sum/ppermute | solution.py:26
  140.8 1.9 %collective-permute-start.15 = (f32[12,1152]{1,0:T(8,128)S(1)}, f32[12,1152]{1,0:T(8,128)S(1)}, u32[]{:S(2)}, u32[]{:S(2)}) collective-permute-start(f32[12,1152]{1,0:T(8,128)S(1)} %slice.139), channel_id=1, source_target_pairs={{0,1},{1,0},{2,3},{3,2},{4,5},{5,4},{6,7},{7,6},{8,9},{9,8},{10,11... | collective-permute-start | bytes 165896 | tf_op jit(solution)/shard_map/pair_return/ppermute | solution.py:55
  (54 shorter events, 17.8 us)
Async XLA Ops:
  4.1 16.9 %collective-permute-start = (bf16[12,1280]{1,0:T(8,128)(2,1)S(1)}, bf16[12,1280]{1,0:T(8,128)(2,1)S(1)}, u32[]{:S(2)}, u32[]{:S(2)}) collective-permute-start(bf16[12,1280]{1,0:T(8,128)(2,1)S(1)} %get-tuple-element.20), channel_id=1, source_target_pairs={{0,1},{1,0},{2,3},{3,2},{4,5},{5,4},{6,7},{7,6},{8,9},{9,8},{10,11... | collective-permute-start | bytes 92168 | tf_op jit(solution)/shard_map/pair_swap/ppermute | solution.py:55
  21.1 13.7 %collective-permute-start.1 = (bf16[24,1280]{1,0:T(8,128)(2,1)S(1)}, bf16[24,1280]{1,0:T(8,128)(2,1)S(1)}, u32[]{:S(2)}, u32[]{:S(2)}) collective-permute-start(bf16[24,1280]{1,0:T(8,128)(2,1)S(1)} %pad_maximum_fusion.5), channel_id=1, source_target_pairs={{0,512},{1,545},{2,514},{3,547},{4,516},{5,549},{6,518},{7,551},{8... | collective-permute-start | bytes 184328 | tf_op jit(solution)/shard_map/gather_z_far/ppermute | solution.py:26
  34.8 12.3 %collective-permute-start.2 = (bf16[48,1280]{1,0:T(8,128)(2,1)S(1)}, bf16[48,1280]{1,0:T(8,128)(2,1)S(1)}, u32[]{:S(2)}, u32[]{:S(2)}) collective-permute-start(bf16[48,1280]{1,0:T(8,128)(2,1)S(1)} %pad_maximum_fusion.4), channel_id=1, source_target_pairs={{0,128},{1,257},{2,130},{3,259},{4,132},{5,261},{6,134},{7,263},{8... | collective-permute-start | bytes 368648 | tf_op jit(solution)/shard_map/gather_z_mid/ppermute | solution.py:26
  47.1 7.2 %collective-permute-start.3 = (bf16[96,1280]{1,0:T(8,128)(2,1)S(1)}, bf16[96,1280]{1,0:T(8,128)(2,1)S(1)}, u32[]{:S(2)}, u32[]{:S(2)}) collective-permute-start(bf16[96,1280]{1,0:T(8,128)(2,1)S(1)} %pad_maximum_fusion.3), channel_id=1, source_target_pairs={{1,65},{3,67},{5,69},{7,71},{9,73},{11,75},{13,77},{15,79},{17,81}... | collective-permute-start | bytes 737288 | tf_op jit(solution)/shard_map/gather_z_near/ppermute | solution.py:26
  54.6 11.4 %collective-permute-start.6 = (bf16[192,1280]{1,0:T(8,128)(2,1)S(1)}, bf16[192,1280]{1,0:T(8,128)(2,1)S(1)}, u32[]{:S(2)}, u32[]{:S(2)}) collective-permute-start(bf16[192,1280]{1,0:T(8,128)(2,1)S(1)} %concatenate.44), channel_id=1, source_target_pairs={{0,16},{1,5},{2,18},{3,7},{4,20},{5,1},{6,22},{7,3},{8,24},{9,13},... | collective-permute-start | bytes 1474568 | tf_op jit(solution)/shard_map/gather_ring/ppermute | solution.py:26
  59.5 11.5 %collective-permute-start.5 = (bf16[192,1280]{1,0:T(8,128)(2,1)S(1)}, bf16[192,1280]{1,0:T(8,128)(2,1)S(1)}, u32[]{:S(2)}, u32[]{:S(2)}) collective-permute-start(bf16[192,1280]{1,0:T(8,128)(2,1)S(1)} %concatenate.44), channel_id=1, source_target_pairs={{0,8},{1,3},{2,10},{3,5},{4,12},{5,7},{6,14},{7,1},{8,16},{9,11},{... | collective-permute-start | bytes 1474568 | tf_op jit(solution)/shard_map/gather_ring/ppermute | solution.py:26
  61.8 9.9 %collective-permute-start.4 = (bf16[192,1280]{1,0:T(8,128)(2,1)S(1)}, bf16[192,1280]{1,0:T(8,128)(2,1)S(1)}, u32[]{:S(2)}, u32[]{:S(2)}) collective-permute-start(bf16[192,1280]{1,0:T(8,128)(2,1)S(1)} %concatenate.44), channel_id=1, source_target_pairs={{0,24},{1,7},{2,26},{3,1},{4,28},{5,3},{6,30},{7,5},{8,0},{9,15},{... | collective-permute-start | bytes 1474568 | tf_op jit(solution)/shard_map/gather_ring/ppermute | solution.py:26
  72.2 4.5 %collective-permute-start.7 = (bf16[384,1280]{1,0:T(8,128)(2,1)S(1)}, bf16[384,1280]{1,0:T(8,128)(2,1)S(1)}, u32[]{:S(2)}, u32[]{:S(2)}) collective-permute-start(bf16[384,1280]{1,0:T(8,128)(2,1)S(1)} %concatenate.45), channel_id=1, source_target_pairs={{0,1},{1,0},{2,3},{3,2},{4,5},{5,4},{6,7},{7,6},{8,9},{9,8},{10,11... | collective-permute-start | bytes 2949128 | tf_op jit(solution)/shard_map/tile_swap/ppermute | solution.py:55
  79.4 4.3 %collective-permute-start.8 = (bf16[384,1152]{1,0:T(8,128)(2,1)S(1)}, bf16[384,1152]{1,0:T(8,128)(2,1)S(1)}, u32[]{:S(2)}, u32[]{:S(2)}) collective-permute-start(bf16[384,1152]{1,0:T(8,128)(2,1)S(1)} %get-tuple-element.24), channel_id=1, source_target_pairs={{0,1},{1,0},{2,3},{3,2},{4,5},{5,4},{6,7},{7,6},{8,9},{9,8},{10,11... | collective-permute-start | bytes 2654216 | tf_op jit(solution)/shard_map/tile_sum/ppermute | solution.py:55
  84.0 15.0 %collective-permute-start.10 = (bf16[192,1152]{1,0:T(8,128)(2,1)S(1)}, bf16[192,1152]{1,0:T(8,128)(2,1)S(1)}, u32[]{:S(2)}, u32[]{:S(2)}) collective-permute-start(bf16[192,1152]{1,0:T(8,128)(2,1)S(1)} %pad_maximum_fusion.1), channel_id=1, source_target_pairs={{0,24},{1,7},{2,26},{3,1},{4,28},{5,3},{6,30},{7,5},{8,0},{9,15},{... | collective-permute-start | bytes 1327112 | tf_op jit(solution)/shard_map/ring_sum/ppermute | solution.py:26
  89.1 10.9 %collective-permute-start.11 = (bf16[192,1152]{1,0:T(8,128)(2,1)S(1)}, bf16[192,1152]{1,0:T(8,128)(2,1)S(1)}, u32[]{:S(2)}, u32[]{:S(2)}) collective-permute-start(bf16[192,1152]{1,0:T(8,128)(2,1)S(1)} %pad_maximum_fusion.2), channel_id=1, source_target_pairs={{0,16},{1,5},{2,18},{3,7},{4,20},{5,1},{6,22},{7,3},{8,24},{9,13},... | collective-permute-start | bytes 1327112 | tf_op jit(solution)/shard_map/ring_sum/ppermute | solution.py:26
  91.1 13.6 %collective-permute-start.9 = (bf16[192,1152]{1,0:T(8,128)(2,1)S(1)}, bf16[192,1152]{1,0:T(8,128)(2,1)S(1)}, u32[]{:S(2)}, u32[]{:S(2)}) collective-permute-start(bf16[192,1152]{1,0:T(8,128)(2,1)S(1)} %pad_maximum_fusion), channel_id=1, source_target_pairs={{0,8},{1,3},{2,10},{3,5},{4,12},{5,7},{6,14},{7,1},{8,16},{9,11},{... | collective-permute-start | bytes 1327112 | tf_op jit(solution)/shard_map/ring_sum/ppermute | solution.py:26
  104.9 39.1 %copy-start = (bf16[12,1152]{1,0:T(8,128)(2,1)S(1)}, bf16[12,1152]{1,0:T(8,128)(2,1)}, u32[]{:S(2)}) copy-start(bf16[12,1152]{1,0:T(8,128)(2,1)} %param.6) | copy-start | bytes 82948
  104.9 39.1 %copy-start.1 = (bf16[12,1152]{1,0:T(8,128)(2,1)S(1)}, bf16[12,1152]{1,0:T(8,128)(2,1)}, u32[]{:S(2)}) copy-start(bf16[12,1152]{1,0:T(8,128)(2,1)} %param.5) | copy-start | bytes 82948
  105.0 7.0 %collective-permute-start.12 = (bf16[96,1152]{1,0:T(8,128)(2,1)S(1)}, bf16[96,1152]{1,0:T(8,128)(2,1)S(1)}, u32[]{:S(2)}, u32[]{:S(2)}) collective-permute-start(bf16[96,1152]{1,0:T(8,128)(2,1)S(1)} %slice.168), channel_id=1, source_target_pairs={{1,65},{3,67},{5,69},{7,71},{9,73},{11,75},{13,77},{15,79},{17,81}... | collective-permute-start | bytes 663560 | tf_op jit(solution)/shard_map/z_near_sum/ppermute | solution.py:26
  112.1 13.0 %collective-permute-start.13 = (bf16[48,1152]{1,0:T(8,128)(2,1)S(1)}, bf16[48,1152]{1,0:T(8,128)(2,1)S(1)}, u32[]{:S(2)}, u32[]{:S(2)}) collective-permute-start(bf16[48,1152]{1,0:T(8,128)(2,1)S(1)} %slice.169), channel_id=1, source_target_pairs={{0,128},{1,257},{2,130},{3,259},{4,132},{5,261},{6,134},{7,263},{8... | collective-permute-start | bytes 331784 | tf_op jit(solution)/shard_map/z_mid_sum/ppermute | solution.py:26
  125.1 15.7 %collective-permute-start.14 = (bf16[24,1152]{1,0:T(8,128)(2,1)S(1)}, bf16[24,1152]{1,0:T(8,128)(2,1)S(1)}, u32[]{:S(2)}, u32[]{:S(2)}) collective-permute-start(bf16[24,1152]{1,0:T(8,128)(2,1)S(1)} %slice.170), channel_id=1, source_target_pairs={{0,512},{1,545},{2,514},{3,547},{4,516},{5,549},{6,518},{7,551},{8... | collective-permute-start | bytes 165896 | tf_op jit(solution)/shard_map/z_far_sum/ppermute | solution.py:26
  140.8 3.2 %collective-permute-start.15 = (f32[12,1152]{1,0:T(8,128)S(1)}, f32[12,1152]{1,0:T(8,128)S(1)}, u32[]{:S(2)}, u32[]{:S(2)}) collective-permute-start(f32[12,1152]{1,0:T(8,128)S(1)} %slice.139), channel_id=1, source_target_pairs={{0,1},{1,0},{2,3},{3,2},{4,5},{5,4},{6,7},{7,6},{8,9},{9,8},{10,11... | collective-permute-start | bytes 165896 | tf_op jit(solution)/shard_map/pair_return/ppermute | solution.py:55

commit v3 on v2

--- a/solution.py
+++ b/solution.py
@@ -38,10 +38,6 @@
     return permute(value, lambda z, x, y: (z ^ 2, x, y), lambda z, x, y: (z ^ 4, x, y))
 
 
-def z_near(value):
-    return permute(value, None, lambda z, x, y: (z ^ 1, x, y))
-
-
 def along_ring(value, shift):
     return permute(
         value,
@@ -53,6 +49,16 @@
 def swap_cores(value):
     n = NZ * NX * NY * 2
     return lax.ppermute(value, BOTH, [(d, d ^ 1) for d in range(n)])
+
+
+def cross(value, back=False):
+    pairs = []
+    for z in range(NZ):
+        for x in range(NX):
+            for y in range(NY):
+                pairs.append((device_at(z, x, y, 1), device_at(z, x, y, 0)))
+                pairs.append((device_at(z, x, y, 0), device_at(z ^ 1, x, y, 1)))
+    return lax.ppermute(value, BOTH, [(b, a) for a, b in pairs] if back else pairs)
 
 
 def unit_rows(raw):
@@ -102,42 +108,41 @@
         block = cat(block, z_far(block))
     with jax.named_scope("gather_z_mid"):
         block = cat(block, z_mid(block))
-    with jax.named_scope("gather_z_near"):
-        block = cat(block, z_near(block))
     with jax.named_scope("gather_ring"):
         groups = [block] + [along_ring(block, -k) for k in RING[1:]]
-    half = 4 * CHIP
-    with jax.named_scope("tile_swap"):
-        first = cat(*(g[:half] for g in groups))
-        other = swap_cores(first)
-        second = cat(*(g[half:] for g in groups))
+    with jax.named_scope("tile_cross"):
+        crossed = cat(*(cross(g) for g in groups))
+        held = cat(*groups)
 
-    imgs = jnp.where(holds_images, first, other)[:, :width]
-    coded = jnp.where(holds_images, other, second)
+    imgs = jnp.where(holds_images, held, crossed)[:, :width]
+    coded = jnp.where(holds_images, crossed, held)
     txts = coded[:, :width]
     numbers = coded[:, width].astype(jnp.int32) * 128 + coded[:, width + 1].astype(jnp.int32)
+    img_z = jnp.where(holds_images, z, z ^ 1)
 
     logits = (
         logit_multiplier
         * jnp.einsum("jd,id->ji", txts, imgs, preferred_element_type=jnp.float32)
         + logit_offset
     )
-    sign = jnp.where(numbers[:, None] == image_ids(z, x, y)[None, :], 1.0, -1.0).astype(jnp.float32)
+    sign = jnp.where(numbers[:, None] == image_ids(img_z, x, y)[None, :], 1.0, -1.0).astype(jnp.float32)
     weights = (logit_multiplier * -sign * jax.nn.sigmoid(-sign * logits)).astype(jnp.bfloat16)
     txt_part = jnp.dot(weights, imgs, preferred_element_type=jnp.float32)
     img_part = jnp.einsum("ji,jd->id", weights, txts, preferred_element_type=jnp.float32)
 
-    with jax.named_scope("tile_sum"):
-        away = jnp.where(holds_images, txt_part, img_part).astype(jnp.bfloat16)
-        home = jnp.where(holds_images, img_part, jnp.zeros_like(img_part))
-        first = home + swap_cores(away).astype(jnp.float32)
+    half = 4 * CHIP
+    away = jnp.where(holds_images, txt_part, img_part).astype(jnp.bfloat16)
+    home = jnp.where(holds_images, img_part, txt_part)
+    sums = []
+    for g in range(4):
+        with jax.named_scope("tile_sum"):
+            rows = slice(g * half, (g + 1) * half)
+            sums.append(home[rows] + cross(away[rows], back=True).astype(jnp.float32))
     with jax.named_scope("ring_sum"):
-        total = cat(first[:half], txt_part[:half])
+        total = sums[0]
         for g in (1, 2, 3):
-            rows = slice(g * half, (g + 1) * half)
-            part = cat(first[rows], txt_part[rows]).astype(jnp.bfloat16)
-            total = total + along_ring(part, RING[g]).astype(jnp.float32)
-    for name, swap in (("z_near_sum", z_near), ("z_mid_sum", z_mid), ("z_far_sum", z_far)):
+            total = total + along_ring(sums[g].astype(jnp.bfloat16), RING[g]).astype(jnp.float32)
+    for name, swap in (("z_mid_sum", z_mid), ("z_far_sum", z_far)):
         with jax.named_scope(name):
             rows = total.shape[0] // 2
             total = total[:rows] + swap(total[rows:].astype(jnp.bfloat16)).astype(jnp.float32)

time: 147 us -> 138 us (0.939)
  waiting for transfers between devices: 57.7 us -> 38.7 us
  starting transfers between devices: 76 us -> 86.8 us
    ppermute x0 -> x8, starting transfers between devices: none -> 21.8 us  [cross(): lax.ppermute(value, BOTH, [(b, a) for a, b in pairs] if back else pairs)]
    ppermute x12 -> x10, waiting for transfers between devices: 52.4 us -> 31.1 us  [permute(): return lax.ppermute(value, BOTH, pairs)]
    ppermute x12 -> x10, starting transfers between devices: 54 us -> 44.4 us  [permute(): return lax.ppermute(value, BOTH, pairs)]
    ppermute x0 -> x8, waiting for transfers between devices: none -> 5.87 us  [cross(): lax.ppermute(value, BOTH, [(b, a) for a, b in pairs] if back else pairs)]
    ppermute x4 -> x2, waiting for transfers between devices: 5.37 us -> 1.74 us  [swap_cores(): return lax.ppermute(value, BOTH, [(d, d ^ 1) for d in range(n)])]
    ppermute x4 -> x2, starting transfers between devices: 22 us -> 20.7 us  [swap_cores(): return lax.ppermute(value, BOTH, [(d, d ^ 1) for d in range(n)])]
  transfers between devices with their start and end apart: 16 -> 20, of which waited for: 15 -> 9; matrix products, arithmetic and copies ran while one was open for 0% -> 1% of each run, Pallas kernels for 0% -> 0%
where the time goes in v3:
time: 138 us; the launch traced here: 137 us
  starting transfers between devices  86.8 us (63%)
  waiting for transfers between devices  38.7 us (28%)
  other arithmetic  5.29 us (4%)
  between operations  2.35 us (2%)
  matrix products  2.15 us (2%)
  local copies, waits for them, and re-layouts  1.69 us (1%)
    ppermute x10, starting transfers between devices, permute(): return lax.ppermute(value, BOTH, pairs)  44.4 us
    ppermute x10, waiting for transfers between devices, permute(): return lax.ppermute(value, BOTH, pairs)  31.1 us
    ppermute x8, starting transfers between devices, cross(): lax.ppermute(value, BOTH, [(b, a) for a, b in pairs] if back else pairs)  21.8 us
    ppermute x2, starting transfers between devices, swap_cores(): return lax.ppermute(value, BOTH, [(d, d ^ 1) for d in range(n)])  20.7 us
    ppermute x8, waiting for transfers between devices, cross(): lax.ppermute(value, BOTH, [(b, a) for a, b in pairs] if back else pairs)  5.87 us
  transfers between devices with their start and end apart: 20, of which 9 were waited for; matrix products, arithmetic and copies ran while one was open for 1% of the time, Pallas kernels for 0%

profile of v3, /device:TPU:1, one launch (start us, length us, event | category | flops | bytes accessed | tf_op | source)
XLA Modules:
  0.0 137.0 jit_solution(13565715611298279328)
XLA Ops:
  4.1 16.1 %collective-permute-start = (bf16[12,1280]{1,0:T(8,128)(2,1)S(1)}, bf16[12,1280]{1,0:T(8,128)(2,1)S(1)}, u32[]{:S(2)}, u32[]{:S(2)}) collective-permute-start(bf16[12,1280]{1,0:T(8,128)(2,1)S(1)} %get-tuple-element.14), channel_id=1, source_target_pairs={{0,1},{1,0},{2,3},{3,2},{4,5},{5,4},{6,7},{7,6},{8,9},{9,8},{10,11... | collective-permute-start | bytes 92168 | tf_op jit(solution)/shard_map/pair_swap/ppermute | solution.py:51
  21.1 10.1 %collective-permute-start.1 = (bf16[24,1280]{1,0:T(8,128)(2,1)S(1)}, bf16[24,1280]{1,0:T(8,128)(2,1)S(1)}, u32[]{:S(2)}, u32[]{:S(2)}) collective-permute-start(bf16[24,1280]{1,0:T(8,128)(2,1)S(1)} %pad_maximum_fusion.2), channel_id=1, source_target_pairs={{0,512},{1,545},{2,514},{3,547},{4,516},{5,549},{6,518},{7,551},{8... | collective-permute-start | bytes 184328 | tf_op jit(solution)/shard_map/gather_z_far/ppermute | solution.py:26
  31.2 3.6 %collective-permute-done.1 = bf16[24,1280]{1,0:T(8,128)(2,1)S(1)} collective-permute-done((bf16[24,1280]{1,0:T(8,128)(2,1)S(1)}, bf16[24,1280]{1,0:T(8,128)(2,1)S(1)}, u32[]{:S(2)}, u32[]{:S(2)}) %collective-permute-start.1) | collective-permute-done | bytes 61472 | tf_op jit(solution)/shard_map/gather_z_far/ppermute | solution.py:26
  34.8 2.5 %collective-permute-start.2 = (bf16[48,1280]{1,0:T(8,128)(2,1)S(1)}, bf16[48,1280]{1,0:T(8,128)(2,1)S(1)}, u32[]{:S(2)}, u32[]{:S(2)}) collective-permute-start(bf16[48,1280]{1,0:T(8,128)(2,1)S(1)} %pad_maximum_fusion.1), channel_id=1, source_target_pairs={{0,128},{1,257},{2,130},{3,259},{4,132},{5,261},{6,134},{7,263},{8... | collective-permute-start | bytes 368648 | tf_op jit(solution)/shard_map/gather_z_mid/ppermute | solution.py:26
  37.3 9.8 %collective-permute-done.2 = bf16[48,1280]{1,0:T(8,128)(2,1)S(1)} collective-permute-done((bf16[48,1280]{1,0:T(8,128)(2,1)S(1)}, bf16[48,1280]{1,0:T(8,128)(2,1)S(1)}, u32[]{:S(2)}, u32[]{:S(2)}) %collective-permute-start.2) | collective-permute-done | bytes 122912 | tf_op jit(solution)/shard_map/gather_z_mid/ppermute | solution.py:26
  47.1 1.9 %collective-permute-start.4 = (bf16[96,1280]{1,0:T(8,128)(2,1)S(1)}, bf16[96,1280]{1,0:T(8,128)(2,1)S(1)}, u32[]{:S(2)}, u32[]{:S(2)}) collective-permute-start(bf16[96,1280]{1,0:T(8,128)(2,1)S(1)} %pad_maximum_fusion), channel_id=1, source_target_pairs={{0,24},{1,7},{2,26},{3,1},{4,28},{5,3},{6,30},{7,5},{8,0},{9,15},{... | collective-permute-start | bytes 737288 | tf_op jit(solution)/shard_map/gather_ring/ppermute | solution.py:26
  49.0 1.9 %collective-permute-start.8 = (bf16[96,1280]{1,0:T(8,128)(2,1)S(1)}, bf16[96,1280]{1,0:T(8,128)(2,1)S(1)}, u32[]{:S(2)}, u32[]{:S(2)}) collective-permute-start(bf16[96,1280]{1,0:T(8,128)(2,1)S(1)} %pad_maximum_fusion), channel_id=1, source_target_pairs={{0,16},{1,5},{2,18},{3,7},{4,20},{5,1},{6,22},{7,3},{8,24},{9,13},... | collective-permute-start | bytes 737288 | tf_op jit(solution)/shard_map/gather_ring/ppermute | solution.py:26
  50.9 3.4 %collective-permute-start.6 = (bf16[96,1280]{1,0:T(8,128)(2,1)S(1)}, bf16[96,1280]{1,0:T(8,128)(2,1)S(1)}, u32[]{:S(2)}, u32[]{:S(2)}) collective-permute-start(bf16[96,1280]{1,0:T(8,128)(2,1)S(1)} %pad_maximum_fusion), channel_id=1, source_target_pairs={{0,8},{1,3},{2,10},{3,5},{4,12},{5,7},{6,14},{7,1},{8,16},{9,11},{... | collective-permute-start | bytes 737288 | tf_op jit(solution)/shard_map/gather_ring/ppermute | solution.py:26
  56.3 6.1 %collective-permute-start.5 = (bf16[96,1280]{1,0:T(8,128)(2,1)S(1)}, bf16[96,1280]{1,0:T(8,128)(2,1)S(1)}, u32[]{:S(2)}, u32[]{:S(2)}) collective-permute-start(bf16[96,1280]{1,0:T(8,128)(2,1)S(1)} %collective-permute-done.4), channel_id=1, source_target_pairs={{1,0},{0,65},{3,2},{2,67},{5,4},{4,69},{7,6},{6,71},{9,8},{8,73},{... | collective-permute-start | bytes 737288 | tf_op jit(solution)/shard_map/tile_cross/ppermute | solution.py:61
  65.7 1.9 %collective-permute-start.7 = (bf16[96,1280]{1,0:T(8,128)(2,1)S(1)}, bf16[96,1280]{1,0:T(8,128)(2,1)}, u32[]{:S(2)}, u32[]{:S(2)}) collective-permute-start(bf16[96,1280]{1,0:T(8,128)(2,1)S(1)} %collective-permute-done.6), channel_id=1, source_target_pairs={{1,0},{0,65},{3,2},{2,67},{5,4},{4,69},{7,6},{6,71},{9,8},{8,73},{... | collective-permute-start | bytes 737288 | tf_op jit(solution)/shard_map/tile_cross/ppermute | solution.py:61
  68.1 5.8 %collective-permute-done.7 = bf16[96,1280]{1,0:T(8,128)(2,1)} collective-permute-done((bf16[96,1280]{1,0:T(8,128)(2,1)S(1)}, bf16[96,1280]{1,0:T(8,128)(2,1)}, u32[]{:S(2)}, u32[]{:S(2)}) %collective-permute-start.7) | collective-permute-done | bytes 245792 | tf_op jit(solution)/shard_map/tile_cross/ppermute | solution.py:61
  77.8 1.9 %collective-permute-start.15 = (bf16[96,1152]{1,0:T(8,128)(2,1)S(1)}, bf16[96,1152]{1,0:T(8,128)(2,1)S(1)}, u32[]{:S(2)}, u32[]{:S(2)}) collective-permute-start(bf16[96,1152]{1,0:T(8,128)(2,1)S(1)} %get-tuple-element.8), channel_id=1, source_target_pairs={{0,1},{65,0},{2,3},{67,2},{4,5},{69,4},{6,7},{71,6},{8,9},{73,8},{... | collective-permute-start | bytes 663560 | tf_op jit(solution)/shard_map/tile_sum/ppermute | solution.py:61
  79.7 2.0 %collective-permute-start.13 = (bf16[96,1152]{1,0:T(8,128)(2,1)S(1)}, bf16[96,1152]{1,0:T(8,128)(2,1)S(1)}, u32[]{:S(2)}, u32[]{:S(2)}) collective-permute-start(bf16[96,1152]{1,0:T(8,128)(2,1)S(1)} %get-tuple-element.9), channel_id=1, source_target_pairs={{0,1},{65,0},{2,3},{67,2},{4,5},{69,4},{6,7},{71,6},{8,9},{73,8},{... | collective-permute-start | bytes 663560 | tf_op jit(solution)/shard_map/tile_sum/ppermute | solution.py:61
  83.6 4.1 %collective-permute-start.10 = (bf16[96,1152]{1,0:T(8,128)(2,1)S(1)}, bf16[96,1152]{1,0:T(8,128)(2,1)S(1)}, u32[]{:S(2)}, u32[]{:S(2)}) collective-permute-start(bf16[96,1152]{1,0:T(8,128)(2,1)S(1)} %get-tuple-element.7), channel_id=1, source_target_pairs={{0,1},{65,0},{2,3},{67,2},{4,5},{69,4},{6,7},{71,6},{8,9},{73,8},{... | collective-permute-start | bytes 663560 | tf_op jit(solution)/shard_map/tile_sum/ppermute | solution.py:61
  87.9 3.7 %collective-permute-start.12 = (bf16[96,1152]{1,0:T(8,128)(2,1)S(1)}, bf16[96,1152]{1,0:T(8,128)(2,1)S(1)}, u32[]{:S(2)}, u32[]{:S(2)}) collective-permute-start(bf16[96,1152]{1,0:T(8,128)(2,1)S(1)} %get-tuple-element.4), channel_id=1, source_target_pairs={{0,8},{1,3},{2,10},{3,5},{4,12},{5,7},{6,14},{7,1},{8,16},{9,11},{... | collective-permute-start | bytes 663560 | tf_op jit(solution)/shard_map/ring_sum/ppermute | solution.py:26
  91.6 3.5 %collective-permute-start.16 = (bf16[96,1152]{1,0:T(8,128)(2,1)S(1)}, bf16[96,1152]{1,0:T(8,128)(2,1)S(1)}, u32[]{:S(2)}, u32[]{:S(2)}) collective-permute-start(bf16[96,1152]{1,0:T(8,128)(2,1)S(1)} %get-tuple-element.5), channel_id=1, source_target_pairs={{0,16},{1,5},{2,18},{3,7},{4,20},{5,1},{6,22},{7,3},{8,24},{9,13},... | collective-permute-start | bytes 663560 | tf_op jit(solution)/shard_map/ring_sum/ppermute | solution.py:26
  95.0 2.8 %collective-permute-start.14 = (bf16[96,1152]{1,0:T(8,128)(2,1)S(1)}, bf16[96,1152]{1,0:T(8,128)(2,1)S(1)}, u32[]{:S(2)}, u32[]{:S(2)}) collective-permute-start(bf16[96,1152]{1,0:T(8,128)(2,1)S(1)} %get-tuple-element.6), channel_id=1, source_target_pairs={{0,24},{1,7},{2,26},{3,1},{4,28},{5,3},{6,30},{7,5},{8,0},{9,15},{... | collective-permute-start | bytes 663560 | tf_op jit(solution)/shard_map/ring_sum/ppermute | solution.py:26
  97.8 1.9 %collective-permute-done.16 = bf16[96,1152]{1,0:T(8,128)(2,1)S(1)} collective-permute-done((bf16[96,1152]{1,0:T(8,128)(2,1)S(1)}, bf16[96,1152]{1,0:T(8,128)(2,1)S(1)}, u32[]{:S(2)}, u32[]{:S(2)}) %collective-permute-start.16) | collective-permute-done | bytes 221216 | tf_op jit(solution)/shard_map/ring_sum/ppermute | solution.py:26
  99.7 2.3 %collective-permute-done.14 = bf16[96,1152]{1,0:T(8,128)(2,1)S(1)} collective-permute-done((bf16[96,1152]{1,0:T(8,128)(2,1)S(1)}, bf16[96,1152]{1,0:T(8,128)(2,1)S(1)}, u32[]{:S(2)}, u32[]{:S(2)}) %collective-permute-start.14) | collective-permute-done | bytes 221216 | tf_op jit(solution)/shard_map/ring_sum/ppermute | solution.py:26
  102.2 1.9 %collective-permute-start.17 = (bf16[48,1152]{1,0:T(8,128)(2,1)S(1)}, bf16[48,1152]{1,0:T(8,128)(2,1)S(1)}, u32[]{:S(2)}, u32[]{:S(2)}) collective-permute-start(bf16[48,1152]{1,0:T(8,128)(2,1)S(1)} %slice.135), channel_id=1, source_target_pairs={{0,128},{1,257},{2,130},{3,259},{4,132},{5,261},{6,134},{7,263},{8... | collective-permute-start | bytes 331784 | tf_op jit(solution)/shard_map/z_mid_sum/ppermute | solution.py:26
  104.1 11.1 %collective-permute-done.17 = bf16[48,1152]{1,0:T(8,128)(2,1)S(1)} collective-permute-done((bf16[48,1152]{1,0:T(8,128)(2,1)S(1)}, bf16[48,1152]{1,0:T(8,128)(2,1)S(1)}, u32[]{:S(2)}, u32[]{:S(2)}) %collective-permute-start.17) | collective-permute-done | bytes 110624 | tf_op jit(solution)/shard_map/z_mid_sum/ppermute | solution.py:26
  115.3 12.8 %collective-permute-start.18 = (bf16[24,1152]{1,0:T(8,128)(2,1)S(1)}, bf16[24,1152]{1,0:T(8,128)(2,1)S(1)}, u32[]{:S(2)}, u32[]{:S(2)}) collective-permute-start(bf16[24,1152]{1,0:T(8,128)(2,1)S(1)} %slice.136), channel_id=1, source_target_pairs={{0,512},{1,545},{2,514},{3,547},{4,516},{5,549},{6,518},{7,551},{8... | collective-permute-start | bytes 165896 | tf_op jit(solution)/shard_map/z_far_sum/ppermute | solution.py:26
  128.1 2.4 %collective-permute-done.18 = bf16[24,1152]{1,0:T(8,128)(2,1)S(1)} collective-permute-done((bf16[24,1152]{1,0:T(8,128)(2,1)S(1)}, bf16[24,1152]{1,0:T(8,128)(2,1)S(1)}, u32[]{:S(2)}, u32[]{:S(2)}) %collective-permute-start.18) | collective-permute-done | bytes 55328 | tf_op jit(solution)/shard_map/z_far_sum/ppermute | solution.py:26
  130.5 4.6 %collective-permute-start.19 = (f32[12,1152]{1,0:T(8,128)S(1)}, f32[12,1152]{1,0:T(8,128)S(1)}, u32[]{:S(2)}, u32[]{:S(2)}) collective-permute-start(f32[12,1152]{1,0:T(8,128)S(1)} %slice.92), channel_id=1, source_target_pairs={{0,1},{1,0},{2,3},{3,2},{4,5},{5,4},{6,7},{7,6},{8,9},{9,8},{10,11... | collective-permute-start | bytes 165896 | tf_op jit(solution)/shard_map/pair_return/ppermute | solution.py:51
  (54 shorter events, 16.7 us)
Async XLA Ops:
  4.1 16.9 %collective-permute-start = (bf16[12,1280]{1,0:T(8,128)(2,1)S(1)}, bf16[12,1280]{1,0:T(8,128)(2,1)S(1)}, u32[]{:S(2)}, u32[]{:S(2)}) collective-permute-start(bf16[12,1280]{1,0:T(8,128)(2,1)S(1)} %get-tuple-element.14), channel_id=1, source_target_pairs={{0,1},{1,0},{2,3},{3,2},{4,5},{5,4},{6,7},{7,6},{8,9},{9,8},{10,11... | collective-permute-start | bytes 92168 | tf_op jit(solution)/shard_map/pair_swap/ppermute | solution.py:51
  21.1 13.7 %collective-permute-start.1 = (bf16[24,1280]{1,0:T(8,128)(2,1)S(1)}, bf16[24,1280]{1,0:T(8,128)(2,1)S(1)}, u32[]{:S(2)}, u32[]{:S(2)}) collective-permute-start(bf16[24,1280]{1,0:T(8,128)(2,1)S(1)} %pad_maximum_fusion.2), channel_id=1, source_target_pairs={{0,512},{1,545},{2,514},{3,547},{4,516},{5,549},{6,518},{7,551},{8... | collective-permute-start | bytes 184328 | tf_op jit(solution)/shard_map/gather_z_far/ppermute | solution.py:26
  34.8 12.3 %collective-permute-start.2 = (bf16[48,1280]{1,0:T(8,128)(2,1)S(1)}, bf16[48,1280]{1,0:T(8,128)(2,1)S(1)}, u32[]{:S(2)}, u32[]{:S(2)}) collective-permute-start(bf16[48,1280]{1,0:T(8,128)(2,1)S(1)} %pad_maximum_fusion.1), channel_id=1, source_target_pairs={{0,128},{1,257},{2,130},{3,259},{4,132},{5,261},{6,134},{7,263},{8... | collective-permute-start | bytes 368648 | tf_op jit(solution)/shard_map/gather_z_mid/ppermute | solution.py:26
  47.1 9.2 %collective-permute-start.4 = (bf16[96,1280]{1,0:T(8,128)(2,1)S(1)}, bf16[96,1280]{1,0:T(8,128)(2,1)S(1)}, u32[]{:S(2)}, u32[]{:S(2)}) collective-permute-start(bf16[96,1280]{1,0:T(8,128)(2,1)S(1)} %pad_maximum_fusion), channel_id=1, source_target_pairs={{0,24},{1,7},{2,26},{3,1},{4,28},{5,3},{6,30},{7,5},{8,0},{9,15},{... | collective-permute-start | bytes 737288 | tf_op jit(solution)/shard_map/gather_ring/ppermute | solution.py:26
  49.0 14.7 %collective-permute-start.8 = (bf16[96,1280]{1,0:T(8,128)(2,1)S(1)}, bf16[96,1280]{1,0:T(8,128)(2,1)S(1)}, u32[]{:S(2)}, u32[]{:S(2)}) collective-permute-start(bf16[96,1280]{1,0:T(8,128)(2,1)S(1)} %pad_maximum_fusion), channel_id=1, source_target_pairs={{0,16},{1,5},{2,18},{3,7},{4,20},{5,1},{6,22},{7,3},{8,24},{9,13},... | collective-permute-start | bytes 737288 | tf_op jit(solution)/shard_map/gather_ring/ppermute | solution.py:26
  50.9 14.7 %collective-permute-start.6 = (bf16[96,1280]{1,0:T(8,128)(2,1)S(1)}, bf16[96,1280]{1,0:T(8,128)(2,1)S(1)}, u32[]{:S(2)}, u32[]{:S(2)}) collective-permute-start(bf16[96,1280]{1,0:T(8,128)(2,1)S(1)} %pad_maximum_fusion), channel_id=1, source_target_pairs={{0,8},{1,3},{2,10},{3,5},{4,12},{5,7},{6,14},{7,1},{8,16},{9,11},{... | collective-permute-start | bytes 737288 | tf_op jit(solution)/shard_map/gather_ring/ppermute | solution.py:26
  54.3 13.3 %collective-permute-start.3 = (bf16[96,1280]{1,0:T(8,128)(2,1)S(1)}, bf16[96,1280]{1,0:T(8,128)(2,1)S(1)}, u32[]{:S(2)}, u32[]{:S(2)}) collective-permute-start(bf16[96,1280]{1,0:T(8,128)(2,1)S(1)} %pad_maximum_fusion), channel_id=1, source_target_pairs={{1,0},{0,65},{3,2},{2,67},{5,4},{4,69},{7,6},{6,71},{9,8},{8,73},{... | collective-permute-start | bytes 737288 | tf_op jit(solution)/shard_map/tile_cross/ppermute | solution.py:61
  56.3 11.8 %collective-permute-start.5 = (bf16[96,1280]{1,0:T(8,128)(2,1)S(1)}, bf16[96,1280]{1,0:T(8,128)(2,1)S(1)}, u32[]{:S(2)}, u32[]{:S(2)}) collective-permute-start(bf16[96,1280]{1,0:T(8,128)(2,1)S(1)} %collective-permute-done.4), channel_id=1, source_target_pairs={{1,0},{0,65},{3,2},{2,67},{5,4},{4,69},{7,6},{6,71},{9,8},{8,73},{... | collective-permute-start | bytes 737288 | tf_op jit(solution)/shard_map/tile_cross/ppermute | solution.py:61
  63.7 11.2 %collective-permute-start.9 = (bf16[96,1280]{1,0:T(8,128)(2,1)S(1)}, bf16[96,1280]{1,0:T(8,128)(2,1)S(1)}, u32[]{:S(2)}, u32[]{:S(2)}) collective-permute-start(bf16[96,1280]{1,0:T(8,128)(2,1)S(1)} %collective-permute-done.8), channel_id=1, source_target_pairs={{1,0},{0,65},{3,2},{2,67},{5,4},{4,69},{7,6},{6,71},{9,8},{8,73},{... | collective-permute-start | bytes 737288 | tf_op jit(solution)/shard_map/tile_cross/ppermute | solution.py:61
  65.7 8.3 %collective-permute-start.7 = (bf16[96,1280]{1,0:T(8,128)(2,1)S(1)}, bf16[96,1280]{1,0:T(8,128)(2,1)}, u32[]{:S(2)}, u32[]{:S(2)}) collective-permute-start(bf16[96,1280]{1,0:T(8,128)(2,1)S(1)} %collective-permute-done.6), channel_id=1, source_target_pairs={{1,0},{0,65},{3,2},{2,67},{5,4},{4,69},{7,6},{6,71},{9,8},{8,73},{... | collective-permute-start | bytes 737288 | tf_op jit(solution)/shard_map/tile_cross/ppermute | solution.py:61
  77.8 9.9 %collective-permute-start.15 = (bf16[96,1152]{1,0:T(8,128)(2,1)S(1)}, bf16[96,1152]{1,0:T(8,128)(2,1)S(1)}, u32[]{:S(2)}, u32[]{:S(2)}) collective-permute-start(bf16[96,1152]{1,0:T(8,128)(2,1)S(1)} %get-tuple-element.8), channel_id=1, source_target_pairs={{0,1},{65,0},{2,3},{67,2},{4,5},{69,4},{6,7},{71,6},{8,9},{73,8},{... | collective-permute-start | bytes 663560 | tf_op jit(solution)/shard_map/tile_sum/ppermute | solution.py:61
  79.7 8.0 %collective-permute-start.13 = (bf16[96,1152]{1,0:T(8,128)(2,1)S(1)}, bf16[96,1152]{1,0:T(8,128)(2,1)S(1)}, u32[]{:S(2)}, u32[]{:S(2)}) collective-permute-start(bf16[96,1152]{1,0:T(8,128)(2,1)S(1)} %get-tuple-element.9), channel_id=1, source_target_pairs={{0,1},{65,0},{2,3},{67,2},{4,5},{69,4},{6,7},{71,6},{8,9},{73,8},{... | collective-permute-start | bytes 663560 | tf_op jit(solution)/shard_map/tile_sum/ppermute | solution.py:61
  81.6 6.0 %collective-permute-start.11 = (bf16[96,1152]{1,0:T(8,128)(2,1)S(1)}, bf16[96,1152]{1,0:T(8,128)(2,1)S(1)}, u32[]{:S(2)}, u32[]{:S(2)}) collective-permute-start(bf16[96,1152]{1,0:T(8,128)(2,1)S(1)} %get-tuple-element.10), channel_id=1, source_target_pairs={{0,1},{65,0},{2,3},{67,2},{4,5},{69,4},{6,7},{71,6},{8,9},{73,8},{... | collective-permute-start | bytes 663560 | tf_op jit(solution)/shard_map/tile_sum/ppermute | solution.py:61
  83.6 14.2 %collective-permute-start.10 = (bf16[96,1152]{1,0:T(8,128)(2,1)S(1)}, bf16[96,1152]{1,0:T(8,128)(2,1)S(1)}, u32[]{:S(2)}, u32[]{:S(2)}) collective-permute-start(bf16[96,1152]{1,0:T(8,128)(2,1)S(1)} %get-tuple-element.7), channel_id=1, source_target_pairs={{0,1},{65,0},{2,3},{67,2},{4,5},{69,4},{6,7},{71,6},{8,9},{73,8},{... | collective-permute-start | bytes 663560 | tf_op jit(solution)/shard_map/tile_sum/ppermute | solution.py:61
  87.9 48.2 %copy-start = (bf16[12,1152]{1,0:T(8,128)(2,1)S(1)}, bf16[12,1152]{1,0:T(8,128)(2,1)}, u32[]{:S(2)}) copy-start(bf16[12,1152]{1,0:T(8,128)(2,1)} %param.6) | copy-start | bytes 82948
  87.9 48.2 %copy-start.1 = (bf16[12,1152]{1,0:T(8,128)(2,1)S(1)}, bf16[12,1152]{1,0:T(8,128)(2,1)}, u32[]{:S(2)}) copy-start(bf16[12,1152]{1,0:T(8,128)(2,1)} %param.5) | copy-start | bytes 82948
  87.9 9.9 %collective-permute-start.12 = (bf16[96,1152]{1,0:T(8,128)(2,1)S(1)}, bf16[96,1152]{1,0:T(8,128)(2,1)S(1)}, u32[]{:S(2)}, u32[]{:S(2)}) collective-permute-start(bf16[96,1152]{1,0:T(8,128)(2,1)S(1)} %get-tuple-element.4), channel_id=1, source_target_pairs={{0,8},{1,3},{2,10},{3,5},{4,12},{5,7},{6,14},{7,1},{8,16},{9,11},{... | collective-permute-start | bytes 663560 | tf_op jit(solution)/shard_map/ring_sum/ppermute | solution.py:26
  91.6 8.2 %collective-permute-start.16 = (bf16[96,1152]{1,0:T(8,128)(2,1)S(1)}, bf16[96,1152]{1,0:T(8,128)(2,1)S(1)}, u32[]{:S(2)}, u32[]{:S(2)}) collective-permute-start(bf16[96,1152]{1,0:T(8,128)(2,1)S(1)} %get-tuple-element.5), channel_id=1, source_target_pairs={{0,16},{1,5},{2,18},{3,7},{4,20},{5,1},{6,22},{7,3},{8,24},{9,13},... | collective-permute-start | bytes 663560 | tf_op jit(solution)/shard_map/ring_sum/ppermute | solution.py:26
  95.0 7.0 %collective-permute-start.14 = (bf16[96,1152]{1,0:T(8,128)(2,1)S(1)}, bf16[96,1152]{1,0:T(8,128)(2,1)S(1)}, u32[]{:S(2)}, u32[]{:S(2)}) collective-permute-start(bf16[96,1152]{1,0:T(8,128)(2,1)S(1)} %get-tuple-element.6), channel_id=1, source_target_pairs={{0,24},{1,7},{2,26},{3,1},{4,28},{5,3},{6,30},{7,5},{8,0},{9,15},{... | collective-permute-start | bytes 663560 | tf_op jit(solution)/shard_map/ring_sum/ppermute | solution.py:26
  102.2 13.1 %collective-permute-start.17 = (bf16[48,1152]{1,0:T(8,128)(2,1)S(1)}, bf16[48,1152]{1,0:T(8,128)(2,1)S(1)}, u32[]{:S(2)}, u32[]{:S(2)}) collective-permute-start(bf16[48,1152]{1,0:T(8,128)(2,1)S(1)} %slice.135), channel_id=1, source_target_pairs={{0,128},{1,257},{2,130},{3,259},{4,132},{5,261},{6,134},{7,263},{8... | collective-permute-start | bytes 331784 | tf_op jit(solution)/shard_map/z_mid_sum/ppermute | solution.py:26
  115.3 15.2 %collective-permute-start.18 = (bf16[24,1152]{1,0:T(8,128)(2,1)S(1)}, bf16[24,1152]{1,0:T(8,128)(2,1)S(1)}, u32[]{:S(2)}, u32[]{:S(2)}) collective-permute-start(bf16[24,1152]{1,0:T(8,128)(2,1)S(1)} %slice.136), channel_id=1, source_target_pairs={{0,512},{1,545},{2,514},{3,547},{4,516},{5,549},{6,518},{7,551},{8... | collective-permute-start | bytes 165896 | tf_op jit(solution)/shard_map/z_far_sum/ppermute | solution.py:26
  130.5 5.5 %collective-permute-start.19 = (f32[12,1152]{1,0:T(8,128)S(1)}, f32[12,1152]{1,0:T(8,128)S(1)}, u32[]{:S(2)}, u32[]{:S(2)}) collective-permute-start(f32[12,1152]{1,0:T(8,128)S(1)} %slice.92), channel_id=1, source_target_pairs={{0,1},{1,0},{2,3},{3,2},{4,5},{5,4},{6,7},{7,6},{8,9},{9,8},{10,11... | collective-permute-start | bytes 165896 | tf_op jit(solution)/shard_map/pair_return/ppermute | solution.py:51

commit v4 on v3

--- a/solution.py
+++ b/solution.py
@@ -111,7 +111,11 @@
     with jax.named_scope("gather_ring"):
         groups = [block] + [along_ring(block, -k) for k in RING[1:]]
     with jax.named_scope("tile_cross"):
-        crossed = cat(*(cross(g) for g in groups))
+        parts = [cross(groups[0])]
+        for g in groups[1:]:
+            g, parts[0] = lax.optimization_barrier((g, parts[0]))
+            parts.append(cross(g))
+        crossed = cat(*parts)
         held = cat(*groups)
 
     imgs = jnp.where(holds_images, held, crossed)[:, :width]
@@ -133,15 +137,18 @@
     half = 4 * CHIP
     away = jnp.where(holds_images, txt_part, img_part).astype(jnp.bfloat16)
     home = jnp.where(holds_images, img_part, txt_part)
-    sums = []
-    for g in range(4):
-        with jax.named_scope("tile_sum"):
-            rows = slice(g * half, (g + 1) * half)
-            sums.append(home[rows] + cross(away[rows], back=True).astype(jnp.float32))
+    with jax.named_scope("tile_sum"):
+        crossed = [cross(away[g * half : (g + 1) * half], back=True) for g in range(4)]
     with jax.named_scope("ring_sum"):
-        total = sums[0]
+        arrived = []
         for g in (1, 2, 3):
-            total = total + along_ring(sums[g].astype(jnp.bfloat16), RING[g]).astype(jnp.float32)
+            part = (home[g * half : (g + 1) * half] + crossed[g].astype(jnp.float32)).astype(jnp.bfloat16)
+            part, home, early = lax.optimization_barrier((part, home, arrived[:1] if g == 3 else []))
+            arrived[: len(early)] = early
+            arrived.append(along_ring(part, RING[g]))
+        total = home[:half] + crossed[0].astype(jnp.float32)
+        for part in arrived:
+            total = total + part.astype(jnp.float32)
     for name, swap in (("z_mid_sum", z_mid), ("z_far_sum", z_far)):
         with jax.named_scope(name):
             rows = total.shape[0] // 2

time: 138 us -> 150 us (1.087)
  waiting for transfers between devices: 38.7 us -> 51 us
    ppermute x10, waiting for transfers between devices: 31.1 us -> 41 us  [permute(): return lax.ppermute(value, BOTH, pairs)]
    ppermute x8, starting transfers between devices: 21.8 us -> 25.5 us  [cross(): lax.ppermute(value, BOTH, [(b, a) for a, b in pairs] if back else pairs)]
    ppermute x2, starting transfers between devices: 20.7 us -> 18 us  [swap_cores(): return lax.ppermute(value, BOTH, [(d, d ^ 1) for d in range(n)])]
    ppermute x8, waiting for transfers between devices: 5.87 us -> 7.95 us  [cross(): lax.ppermute(value, BOTH, [(b, a) for a, b in pairs] if back else pairs)]
  transfers between devices with their start and end apart: 20 -> 20, of which waited for: 9 -> 11; matrix products, arithmetic and copies ran while one was open for 1% -> 1% of each run, Pallas kernels for 0% -> 0%
where the time goes in v4:
time: 150 us; the launch traced here: 149 us
  starting transfers between devices  87 us (58%)
  waiting for transfers between devices  51 us (34%)
  other arithmetic  5.27 us (4%)
  between operations  2.34 us (2%)
  matrix products  2.17 us (1%)
  local copies, waits for them, and re-layouts  1.68 us (1%)
    ppermute x10, starting transfers between devices, permute(): return lax.ppermute(value, BOTH, pairs)  43.5 us
    ppermute x10, waiting for transfers between devices, permute(): return lax.ppermute(value, BOTH, pairs)  41 us
    ppermute x8, starting transfers between devices, cross(): lax.ppermute(value, BOTH, [(b, a) for a, b in pairs] if back else pairs)  25.5 us
    ppermute x2, starting transfers between devices, swap_cores(): return lax.ppermute(value, BOTH, [(d, d ^ 1) for d in range(n)])  18 us
    ppermute x8, waiting for transfers between devices, cross(): lax.ppermute(value, BOTH, [(b, a) for a, b in pairs] if back else pairs)  7.95 us
  transfers between devices with their start and end apart: 20, of which 11 were waited for; matrix products, arithmetic and copies ran while one was open for 1% of the time, Pallas kernels for 0%

profile of v4, /device:TPU:1, one launch (start us, length us, event | category | flops | bytes accessed | tf_op | source)
XLA Modules:
  0.0 149.5 jit_solution(11052495647807749542)
XLA Ops:
  4.1 16.1 %collective-permute-start = (bf16[12,1280]{1,0:T(8,128)(2,1)S(1)}, bf16[12,1280]{1,0:T(8,128)(2,1)S(1)}, u32[]{:S(2)}, u32[]{:S(2)}) collective-permute-start(bf16[12,1280]{1,0:T(8,128)(2,1)S(1)} %get-tuple-element.37), channel_id=1, source_target_pairs={{0,1},{1,0},{2,3},{3,2},{4,5},{5,4},{6,7},{7,6},{8,9},{9,8},{10,11... | collective-permute-start | bytes 92168 | tf_op jit(solution)/shard_map/pair_swap/ppermute | solution.py:51
  21.1 10.1 %collective-permute-start.1 = (bf16[24,1280]{1,0:T(8,128)(2,1)S(1)}, bf16[24,1280]{1,0:T(8,128)(2,1)S(1)}, u32[]{:S(2)}, u32[]{:S(2)}) collective-permute-start(bf16[24,1280]{1,0:T(8,128)(2,1)S(1)} %pad_maximum_fusion.2), channel_id=1, source_target_pairs={{0,512},{1,545},{2,514},{3,547},{4,516},{5,549},{6,518},{7,551},{8... | collective-permute-start | bytes 184328 | tf_op jit(solution)/shard_map/gather_z_far/ppermute | solution.py:26
  31.2 3.6 %collective-permute-done.1 = bf16[24,1280]{1,0:T(8,128)(2,1)S(1)} collective-permute-done((bf16[24,1280]{1,0:T(8,128)(2,1)S(1)}, bf16[24,1280]{1,0:T(8,128)(2,1)S(1)}, u32[]{:S(2)}, u32[]{:S(2)}) %collective-permute-start.1) | collective-permute-done | bytes 61472 | tf_op jit(solution)/shard_map/gather_z_far/ppermute | solution.py:26
  34.8 2.5 %collective-permute-start.2 = (bf16[48,1280]{1,0:T(8,128)(2,1)S(1)}, bf16[48,1280]{1,0:T(8,128)(2,1)S(1)}, u32[]{:S(2)}, u32[]{:S(2)}) collective-permute-start(bf16[48,1280]{1,0:T(8,128)(2,1)S(1)} %pad_maximum_fusion.1), channel_id=1, source_target_pairs={{0,128},{1,257},{2,130},{3,259},{4,132},{5,261},{6,134},{7,263},{8... | collective-permute-start | bytes 368648 | tf_op jit(solution)/shard_map/gather_z_mid/ppermute | solution.py:26
  37.3 9.8 %collective-permute-done.2 = bf16[48,1280]{1,0:T(8,128)(2,1)S(1)} collective-permute-done((bf16[48,1280]{1,0:T(8,128)(2,1)S(1)}, bf16[48,1280]{1,0:T(8,128)(2,1)S(1)}, u32[]{:S(2)}, u32[]{:S(2)}) %collective-permute-start.2) | collective-permute-done | bytes 122912 | tf_op jit(solution)/shard_map/gather_z_mid/ppermute | solution.py:26
  47.1 1.9 %collective-permute-start.6 = (bf16[96,1280]{1,0:T(8,128)(2,1)S(1)}, bf16[96,1280]{1,0:T(8,128)(2,1)S(1)}, u32[]{:S(2)}, u32[]{:S(2)}) collective-permute-start(bf16[96,1280]{1,0:T(8,128)(2,1)S(1)} %pad_maximum_fusion), channel_id=1, source_target_pairs={{1,0},{0,65},{3,2},{2,67},{5,4},{4,69},{7,6},{6,71},{9,8},{8,73},{... | collective-permute-start | bytes 737288 | tf_op jit(solution)/shard_map/tile_cross/ppermute | solution.py:61
  50.9 3.4 %collective-permute-start.4 = (bf16[96,1280]{1,0:T(8,128)(2,1)S(1)}, bf16[96,1280]{1,0:T(8,128)(2,1)S(1)}, u32[]{:S(2)}, u32[]{:S(2)}) collective-permute-start(bf16[96,1280]{1,0:T(8,128)(2,1)S(1)} %pad_maximum_fusion), channel_id=1, source_target_pairs={{0,8},{1,3},{2,10},{3,5},{4,12},{5,7},{6,14},{7,1},{8,16},{9,11},{... | collective-permute-start | bytes 737288 | tf_op jit(solution)/shard_map/gather_ring/ppermute | solution.py:26
  56.3 7.4 %collective-permute-start.7 = (bf16[96,1280]{1,0:T(8,128)(2,1)S(1)}, bf16[96,1280]{1,0:T(8,128)(2,1)S(1)}, u32[]{:S(2)}, u32[]{:S(2)}) collective-permute-start(bf16[96,1280]{1,0:T(8,128)(2,1)S(1)} %collective-permute-done.5), channel_id=1, source_target_pairs={{1,0},{0,65},{3,2},{2,67},{5,4},{4,69},{7,6},{6,71},{9,8},{8,73},{... | collective-permute-start | bytes 737288 | tf_op jit(solution)/shard_map/tile_cross/ppermute | solution.py:61
  65.0 4.4 %collective-permute-start.8 = (bf16[96,1280]{1,0:T(8,128)(2,1)S(1)}, bf16[96,1280]{1,0:T(8,128)(2,1)S(1)}, u32[]{:S(2)}, u32[]{:S(2)}) collective-permute-start(bf16[96,1280]{1,0:T(8,128)(2,1)S(1)} %collective-permute-done.4), channel_id=1, source_target_pairs={{1,0},{0,65},{3,2},{2,67},{5,4},{4,69},{7,6},{6,71},{9,8},{8,73},{... | collective-permute-start | bytes 737288 | tf_op jit(solution)/shard_map/tile_cross/ppermute | solution.py:61
  69.4 1.9 %collective-permute-start.9 = (bf16[96,1280]{1,0:T(8,128)(2,1)S(1)}, bf16[96,1280]{1,0:T(8,128)(2,1)}, u32[]{:S(2)}, u32[]{:S(2)}) collective-permute-start(bf16[96,1280]{1,0:T(8,128)(2,1)S(1)} %collective-permute-done.3), channel_id=1, source_target_pairs={{1,0},{0,65},{3,2},{2,67},{5,4},{4,69},{7,6},{6,71},{9,8},{8,73},{... | collective-permute-start | bytes 737288 | tf_op jit(solution)/shard_map/tile_cross/ppermute | solution.py:61
  72.6 4.5 %collective-permute-done.9 = bf16[96,1280]{1,0:T(8,128)(2,1)} collective-permute-done((bf16[96,1280]{1,0:T(8,128)(2,1)S(1)}, bf16[96,1280]{1,0:T(8,128)(2,1)}, u32[]{:S(2)}, u32[]{:S(2)}) %collective-permute-start.9) | collective-permute-done | bytes 245792 | tf_op jit(solution)/shard_map/tile_cross/ppermute | solution.py:61
  80.6 1.9 %collective-permute-start.10 = (bf16[96,1152]{1,0:T(8,128)(2,1)S(1)}, bf16[96,1152]{1,0:T(8,128)(2,1)S(1)}, u32[]{:S(2)}, u32[]{:S(2)}) collective-permute-start(bf16[96,1152]{1,0:T(8,128)(2,1)S(1)} %get-tuple-element.33), channel_id=1, source_target_pairs={{0,1},{65,0},{2,3},{67,2},{4,5},{69,4},{6,7},{71,6},{8,9},{73,8},{... | collective-permute-start | bytes 663560 | tf_op jit(solution)/shard_map/tile_sum/ppermute | solution.py:61
  82.7 2.6 %collective-permute-start.14 = (bf16[96,1152]{1,0:T(8,128)(2,1)S(1)}, bf16[96,1152]{1,0:T(8,128)(2,1)S(1)}, u32[]{:S(2)}, u32[]{:S(2)}) collective-permute-start(bf16[96,1152]{1,0:T(8,128)(2,1)S(1)} %get-tuple-element.30), channel_id=1, source_target_pairs={{0,1},{65,0},{2,3},{67,2},{4,5},{69,4},{6,7},{71,6},{8,9},{73,8},{... | collective-permute-start | bytes 663560 | tf_op jit(solution)/shard_map/tile_sum/ppermute | solution.py:61
  85.4 1.9 %collective-permute-start.12 = (bf16[96,1152]{1,0:T(8,128)(2,1)S(1)}, bf16[96,1152]{1,0:T(8,128)(2,1)S(1)}, u32[]{:S(2)}, u32[]{:S(2)}) collective-permute-start(bf16[96,1152]{1,0:T(8,128)(2,1)S(1)} %get-tuple-element.31), channel_id=1, source_target_pairs={{0,1},{65,0},{2,3},{67,2},{4,5},{69,4},{6,7},{71,6},{8,9},{73,8},{... | collective-permute-start | bytes 663560 | tf_op jit(solution)/shard_map/tile_sum/ppermute | solution.py:61
  87.3 3.4 %collective-permute-start.11 = (bf16[96,1152]{1,0:T(8,128)(2,1)S(1)}, bf16[96,1152]{1,0:T(8,128)(2,1)S(1)}, u32[]{:S(2)}, u32[]{:S(2)}) collective-permute-start(bf16[96,1152]{1,0:T(8,128)(2,1)S(1)} %get-tuple-element.32), channel_id=1, source_target_pairs={{0,1},{65,0},{2,3},{67,2},{4,5},{69,4},{6,7},{71,6},{8,9},{73,8},{... | collective-permute-start | bytes 663560 | tf_op jit(solution)/shard_map/tile_sum/ppermute | solution.py:61
  90.8 2.8 %collective-permute-done.11 = bf16[96,1152]{1,0:T(8,128)(2,1)S(1)} collective-permute-done((bf16[96,1152]{1,0:T(8,128)(2,1)S(1)}, bf16[96,1152]{1,0:T(8,128)(2,1)S(1)}, u32[]{:S(2)}, u32[]{:S(2)}) %collective-permute-start.11) | collective-permute-done | bytes 221216 | tf_op jit(solution)/shard_map/tile_sum/ppermute | solution.py:61
  93.7 4.8 %collective-permute-start.15 = (bf16[96,1152]{1,0:T(8,128)(2,1)S(1)}, bf16[96,1152]{1,0:T(8,128)(2,1)S(1)}, u32[]{:S(2)}, u32[]{:S(2)}) collective-permute-start(bf16[96,1152]{1,0:T(8,128)(2,1)S(1)} %add_convert_fusion.1), channel_id=1, source_target_pairs={{0,24},{1,7},{2,26},{3,1},{4,28},{5,3},{6,30},{7,5},{8,0},{9,15},{... | collective-permute-start | bytes 663560 | tf_op jit(solution)/shard_map/ring_sum/ppermute | solution.py:26
  98.4 1.9 %collective-permute-start.13 = (bf16[96,1152]{1,0:T(8,128)(2,1)S(1)}, bf16[96,1152]{1,0:T(8,128)(2,1)S(1)}, u32[]{:S(2)}, u32[]{:S(2)}) collective-permute-start(bf16[96,1152]{1,0:T(8,128)(2,1)S(1)} %fusion.11), channel_id=1, source_target_pairs={{0,8},{1,3},{2,10},{3,5},{4,12},{5,7},{6,14},{7,1},{8,16},{9,11},{... | collective-permute-start | bytes 663560 | tf_op jit(solution)/shard_map/ring_sum/ppermute | solution.py:26
  100.4 6.2 %collective-permute-done.13 = bf16[96,1152]{1,0:T(8,128)(2,1)S(1)} collective-permute-done((bf16[96,1152]{1,0:T(8,128)(2,1)S(1)}, bf16[96,1152]{1,0:T(8,128)(2,1)S(1)}, u32[]{:S(2)}, u32[]{:S(2)}) %collective-permute-start.13) | collective-permute-done | bytes 221216 | tf_op jit(solution)/shard_map/ring_sum/ppermute | solution.py:26
  108.6 6.5 %collective-permute-done.16 = bf16[96,1152]{1,0:T(8,128)(2,1)S(1)} collective-permute-done((bf16[96,1152]{1,0:T(8,128)(2,1)S(1)}, bf16[96,1152]{1,0:T(8,128)(2,1)S(1)}, u32[]{:S(2)}, u32[]{:S(2)}) %collective-permute-start.16) | collective-permute-done | bytes 221216 | tf_op jit(solution)/shard_map/ring_sum/ppermute | solution.py:26
  117.2 10.9 %collective-permute-done.17 = bf16[48,1152]{1,0:T(8,128)(2,1)S(1)} collective-permute-done((bf16[48,1152]{1,0:T(8,128)(2,1)S(1)}, bf16[48,1152]{1,0:T(8,128)(2,1)S(1)}, u32[]{:S(2)}, u32[]{:S(2)}) %collective-permute-start.17) | collective-permute-done | bytes 110624 | tf_op jit(solution)/shard_map/z_mid_sum/ppermute | solution.py:26
  128.1 13.2 %collective-permute-start.18 = (bf16[24,1152]{1,0:T(8,128)(2,1)S(1)}, bf16[24,1152]{1,0:T(8,128)(2,1)S(1)}, u32[]{:S(2)}, u32[]{:S(2)}) collective-permute-start(bf16[24,1152]{1,0:T(8,128)(2,1)S(1)} %slice.123), channel_id=1, source_target_pairs={{0,512},{1,545},{2,514},{3,547},{4,516},{5,549},{6,518},{7,551},{8... | collective-permute-start | bytes 165896 | tf_op jit(solution)/shard_map/z_far_sum/ppermute | solution.py:26
  141.4 3.9 %collective-permute-done.18 = bf16[24,1152]{1,0:T(8,128)(2,1)S(1)} collective-permute-done((bf16[24,1152]{1,0:T(8,128)(2,1)S(1)}, bf16[24,1152]{1,0:T(8,128)(2,1)S(1)}, u32[]{:S(2)}, u32[]{:S(2)}) %collective-permute-start.18) | collective-permute-done | bytes 55328 | tf_op jit(solution)/shard_map/z_far_sum/ppermute | solution.py:26
  145.4 1.9 %collective-permute-start.19 = (f32[12,1152]{1,0:T(8,128)S(1)}, f32[12,1152]{1,0:T(8,128)S(1)}, u32[]{:S(2)}, u32[]{:S(2)}) collective-permute-start(f32[12,1152]{1,0:T(8,128)S(1)} %slice.89), channel_id=1, source_target_pairs={{0,1},{1,0},{2,3},{3,2},{4,5},{5,4},{6,7},{7,6},{8,9},{9,8},{10,11... | collective-permute-start | bytes 165896 | tf_op jit(solution)/shard_map/pair_return/ppermute | solution.py:51
  (56 shorter events, 19.5 us)
Async XLA Ops:
  4.1 16.9 %collective-permute-start = (bf16[12,1280]{1,0:T(8,128)(2,1)S(1)}, bf16[12,1280]{1,0:T(8,128)(2,1)S(1)}, u32[]{:S(2)}, u32[]{:S(2)}) collective-permute-start(bf16[12,1280]{1,0:T(8,128)(2,1)S(1)} %get-tuple-element.37), channel_id=1, source_target_pairs={{0,1},{1,0},{2,3},{3,2},{4,5},{5,4},{6,7},{7,6},{8,9},{9,8},{10,11... | collective-permute-start | bytes 92168 | tf_op jit(solution)/shard_map/pair_swap/ppermute | solution.py:51
  21.1 13.7 %collective-permute-start.1 = (bf16[24,1280]{1,0:T(8,128)(2,1)S(1)}, bf16[24,1280]{1,0:T(8,128)(2,1)S(1)}, u32[]{:S(2)}, u32[]{:S(2)}) collective-permute-start(bf16[24,1280]{1,0:T(8,128)(2,1)S(1)} %pad_maximum_fusion.2), channel_id=1, source_target_pairs={{0,512},{1,545},{2,514},{3,547},{4,516},{5,549},{6,518},{7,551},{8... | collective-permute-start | bytes 184328 | tf_op jit(solution)/shard_map/gather_z_far/ppermute | solution.py:26
  34.8 12.3 %collective-permute-start.2 = (bf16[48,1280]{1,0:T(8,128)(2,1)S(1)}, bf16[48,1280]{1,0:T(8,128)(2,1)S(1)}, u32[]{:S(2)}, u32[]{:S(2)}) collective-permute-start(bf16[48,1280]{1,0:T(8,128)(2,1)S(1)} %pad_maximum_fusion.1), channel_id=1, source_target_pairs={{0,128},{1,257},{2,130},{3,259},{4,132},{5,261},{6,134},{7,263},{8... | collective-permute-start | bytes 368648 | tf_op jit(solution)/shard_map/gather_z_mid/ppermute | solution.py:26
  47.1 9.2 %collective-permute-start.6 = (bf16[96,1280]{1,0:T(8,128)(2,1)S(1)}, bf16[96,1280]{1,0:T(8,128)(2,1)S(1)}, u32[]{:S(2)}, u32[]{:S(2)}) collective-permute-start(bf16[96,1280]{1,0:T(8,128)(2,1)S(1)} %pad_maximum_fusion), channel_id=1, source_target_pairs={{1,0},{0,65},{3,2},{2,67},{5,4},{4,69},{7,6},{6,71},{9,8},{8,73},{... | collective-permute-start | bytes 737288 | tf_op jit(solution)/shard_map/tile_cross/ppermute | solution.py:61
  49.0 7.3 %collective-permute-start.5 = (bf16[96,1280]{1,0:T(8,128)(2,1)S(1)}, bf16[96,1280]{1,0:T(8,128)(2,1)S(1)}, u32[]{:S(2)}, u32[]{:S(2)}) collective-permute-start(bf16[96,1280]{1,0:T(8,128)(2,1)S(1)} %pad_maximum_fusion), channel_id=1, source_target_pairs={{0,24},{1,7},{2,26},{3,1},{4,28},{5,3},{6,30},{7,5},{8,0},{9,15},{... | collective-permute-start | bytes 737288 | tf_op jit(solution)/shard_map/gather_ring/ppermute | solution.py:26
  50.9 14.1 %collective-permute-start.4 = (bf16[96,1280]{1,0:T(8,128)(2,1)S(1)}, bf16[96,1280]{1,0:T(8,128)(2,1)S(1)}, u32[]{:S(2)}, u32[]{:S(2)}) collective-permute-start(bf16[96,1280]{1,0:T(8,128)(2,1)S(1)} %pad_maximum_fusion), channel_id=1, source_target_pairs={{0,8},{1,3},{2,10},{3,5},{4,12},{5,7},{6,14},{7,1},{8,16},{9,11},{... | collective-permute-start | bytes 737288 | tf_op jit(solution)/shard_map/gather_ring/ppermute | solution.py:26
  54.3 15.1 %collective-permute-start.3 = (bf16[96,1280]{1,0:T(8,128)(2,1)S(1)}, bf16[96,1280]{1,0:T(8,128)(2,1)S(1)}, u32[]{:S(2)}, u32[]{:S(2)}) collective-permute-start(bf16[96,1280]{1,0:T(8,128)(2,1)S(1)} %pad_maximum_fusion), channel_id=1, source_target_pairs={{0,16},{1,5},{2,18},{3,7},{4,20},{5,1},{6,22},{7,3},{8,24},{9,13},... | collective-permute-start | bytes 737288 | tf_op jit(solution)/shard_map/gather_ring/ppermute | solution.py:26
  56.3 15.6 %collective-permute-start.7 = (bf16[96,1280]{1,0:T(8,128)(2,1)S(1)}, bf16[96,1280]{1,0:T(8,128)(2,1)S(1)}, u32[]{:S(2)}, u32[]{:S(2)}) collective-permute-start(bf16[96,1280]{1,0:T(8,128)(2,1)S(1)} %collective-permute-done.5), channel_id=1, source_target_pairs={{1,0},{0,65},{3,2},{2,67},{5,4},{4,69},{7,6},{6,71},{9,8},{8,73},{... | collective-permute-start | bytes 737288 | tf_op jit(solution)/shard_map/tile_cross/ppermute | solution.py:61
  65.0 7.5 %collective-permute-start.8 = (bf16[96,1280]{1,0:T(8,128)(2,1)S(1)}, bf16[96,1280]{1,0:T(8,128)(2,1)S(1)}, u32[]{:S(2)}, u32[]{:S(2)}) collective-permute-start(bf16[96,1280]{1,0:T(8,128)(2,1)S(1)} %collective-permute-done.4), channel_id=1, source_target_pairs={{1,0},{0,65},{3,2},{2,67},{5,4},{4,69},{7,6},{6,71},{9,8},{8,73},{... | collective-permute-start | bytes 737288 | tf_op jit(solution)/shard_map/tile_cross/ppermute | solution.py:61
  69.4 7.6 %collective-permute-start.9 = (bf16[96,1280]{1,0:T(8,128)(2,1)S(1)}, bf16[96,1280]{1,0:T(8,128)(2,1)}, u32[]{:S(2)}, u32[]{:S(2)}) collective-permute-start(bf16[96,1280]{1,0:T(8,128)(2,1)S(1)} %collective-permute-done.3), channel_id=1, source_target_pairs={{1,0},{0,65},{3,2},{2,67},{5,4},{4,69},{7,6},{6,71},{9,8},{8,73},{... | collective-permute-start | bytes 737288 | tf_op jit(solution)/shard_map/tile_cross/ppermute | solution.py:61
  80.6 10.1 %collective-permute-start.10 = (bf16[96,1152]{1,0:T(8,128)(2,1)S(1)}, bf16[96,1152]{1,0:T(8,128)(2,1)S(1)}, u32[]{:S(2)}, u32[]{:S(2)}) collective-permute-start(bf16[96,1152]{1,0:T(8,128)(2,1)S(1)} %get-tuple-element.33), channel_id=1, source_target_pairs={{0,1},{65,0},{2,3},{67,2},{4,5},{69,4},{6,7},{71,6},{8,9},{73,8},{... | collective-permute-start | bytes 663560 | tf_op jit(solution)/shard_map/tile_sum/ppermute | solution.py:61
  82.7 25.8 %collective-permute-start.14 = (bf16[96,1152]{1,0:T(8,128)(2,1)S(1)}, bf16[96,1152]{1,0:T(8,128)(2,1)S(1)}, u32[]{:S(2)}, u32[]{:S(2)}) collective-permute-start(bf16[96,1152]{1,0:T(8,128)(2,1)S(1)} %get-tuple-element.30), channel_id=1, source_target_pairs={{0,1},{65,0},{2,3},{67,2},{4,5},{69,4},{6,7},{71,6},{8,9},{73,8},{... | collective-permute-start | bytes 663560 | tf_op jit(solution)/shard_map/tile_sum/ppermute | solution.py:61
  85.4 15.0 %collective-permute-start.12 = (bf16[96,1152]{1,0:T(8,128)(2,1)S(1)}, bf16[96,1152]{1,0:T(8,128)(2,1)S(1)}, u32[]{:S(2)}, u32[]{:S(2)}) collective-permute-start(bf16[96,1152]{1,0:T(8,128)(2,1)S(1)} %get-tuple-element.31), channel_id=1, source_target_pairs={{0,1},{65,0},{2,3},{67,2},{4,5},{69,4},{6,7},{71,6},{8,9},{73,8},{... | collective-permute-start | bytes 663560 | tf_op jit(solution)/shard_map/tile_sum/ppermute | solution.py:61
  87.3 6.3 %collective-permute-start.11 = (bf16[96,1152]{1,0:T(8,128)(2,1)S(1)}, bf16[96,1152]{1,0:T(8,128)(2,1)S(1)}, u32[]{:S(2)}, u32[]{:S(2)}) collective-permute-start(bf16[96,1152]{1,0:T(8,128)(2,1)S(1)} %get-tuple-element.32), channel_id=1, source_target_pairs={{0,1},{65,0},{2,3},{67,2},{4,5},{69,4},{6,7},{71,6},{8,9},{73,8},{... | collective-permute-start | bytes 663560 | tf_op jit(solution)/shard_map/tile_sum/ppermute | solution.py:61
  93.6 54.9 %copy-start = (bf16[12,1152]{1,0:T(8,128)(2,1)S(1)}, bf16[12,1152]{1,0:T(8,128)(2,1)}, u32[]{:S(2)}) copy-start(bf16[12,1152]{1,0:T(8,128)(2,1)} %param.6) | copy-start | bytes 82948
  93.7 54.9 %copy-start.1 = (bf16[12,1152]{1,0:T(8,128)(2,1)S(1)}, bf16[12,1152]{1,0:T(8,128)(2,1)}, u32[]{:S(2)}) copy-start(bf16[12,1152]{1,0:T(8,128)(2,1)} %param.5) | copy-start | bytes 82948
  93.7 14.9 %collective-permute-start.15 = (bf16[96,1152]{1,0:T(8,128)(2,1)S(1)}, bf16[96,1152]{1,0:T(8,128)(2,1)S(1)}, u32[]{:S(2)}, u32[]{:S(2)}) collective-permute-start(bf16[96,1152]{1,0:T(8,128)(2,1)S(1)} %add_convert_fusion.1), channel_id=1, source_target_pairs={{0,24},{1,7},{2,26},{3,1},{4,28},{5,3},{6,30},{7,5},{8,0},{9,15},{... | collective-permute-start | bytes 663560 | tf_op jit(solution)/shard_map/ring_sum/ppermute | solution.py:26
  98.4 8.2 %collective-permute-start.13 = (bf16[96,1152]{1,0:T(8,128)(2,1)S(1)}, bf16[96,1152]{1,0:T(8,128)(2,1)S(1)}, u32[]{:S(2)}, u32[]{:S(2)}) collective-permute-start(bf16[96,1152]{1,0:T(8,128)(2,1)S(1)} %fusion.11), channel_id=1, source_target_pairs={{0,8},{1,3},{2,10},{3,5},{4,12},{5,7},{6,14},{7,1},{8,16},{9,11},{... | collective-permute-start | bytes 663560 | tf_op jit(solution)/shard_map/ring_sum/ppermute | solution.py:26
  106.6 8.5 %collective-permute-start.16 = (bf16[96,1152]{1,0:T(8,128)(2,1)S(1)}, bf16[96,1152]{1,0:T(8,128)(2,1)S(1)}, u32[]{:S(2)}, u32[]{:S(2)}) collective-permute-start(bf16[96,1152]{1,0:T(8,128)(2,1)S(1)} %add_convert_fusion), channel_id=1, source_target_pairs={{0,16},{1,5},{2,18},{3,7},{4,20},{5,1},{6,22},{7,3},{8,24},{9,13},... | collective-permute-start | bytes 663560 | tf_op jit(solution)/shard_map/ring_sum/ppermute | solution.py:26
  115.2 12.9 %collective-permute-start.17 = (bf16[48,1152]{1,0:T(8,128)(2,1)S(1)}, bf16[48,1152]{1,0:T(8,128)(2,1)S(1)}, u32[]{:S(2)}, u32[]{:S(2)}) collective-permute-start(bf16[48,1152]{1,0:T(8,128)(2,1)S(1)} %slice.122), channel_id=1, source_target_pairs={{0,128},{1,257},{2,130},{3,259},{4,132},{5,261},{6,134},{7,263},{8... | collective-permute-start | bytes 331784 | tf_op jit(solution)/shard_map/z_mid_sum/ppermute | solution.py:26
  128.1 17.2 %collective-permute-start.18 = (bf16[24,1152]{1,0:T(8,128)(2,1)S(1)}, bf16[24,1152]{1,0:T(8,128)(2,1)S(1)}, u32[]{:S(2)}, u32[]{:S(2)}) collective-permute-start(bf16[24,1152]{1,0:T(8,128)(2,1)S(1)} %slice.123), channel_id=1, source_target_pairs={{0,512},{1,545},{2,514},{3,547},{4,516},{5,549},{6,518},{7,551},{8... | collective-permute-start | bytes 165896 | tf_op jit(solution)/shard_map/z_far_sum/ppermute | solution.py:26
  145.4 3.2 %collective-permute-start.19 = (f32[12,1152]{1,0:T(8,128)S(1)}, f32[12,1152]{1,0:T(8,128)S(1)}, u32[]{:S(2)}, u32[]{:S(2)}) collective-permute-start(f32[12,1152]{1,0:T(8,128)S(1)} %slice.89), channel_id=1, source_target_pairs={{0,1},{1,0},{2,3},{3,2},{4,5},{5,4},{6,7},{7,6},{8,9},{9,8},{10,11... | collective-permute-start | bytes 165896 | tf_op jit(solution)/shard_map/pair_return/ppermute | solution.py:51

commit v5 on v2

v5 whole, which is shorter than its diff:
```python
import jax
import jax.numpy as jnp
from jax import lax
from jax.experimental import pallas as pl
from jax.experimental.pallas import tpu as pltpu
from jax.sharding import PartitionSpec as P

NZ, NX, NY = 32, 4, 4
OWN = 12
CHIP = 2 * OWN
LANES = 128
BOTH = ("row", "col")


def device_at(z, x, y, c):
    return (z & 15) * 64 + (z >> 4) * 32 + x * 8 + y * 2 + c


def permute(value, images=None, texts=None):
    pairs = []
    for z in range(NZ):
        for x in range(NX):
            for y in range(NY):
                for c, to in enumerate((images, texts)):
                    if to is not None:
                        pairs.append((device_at(z, x, y, c), device_at(*to(z, x, y), c)))
    return lax.ppermute(value, BOTH, pairs)


def z_far(value):
    return permute(
        value,
        lambda z, x, y: (z ^ 8, x, y),
        lambda z, x, y: ((((z + 8) % NZ) ^ 8) - 8 & (NZ - 1), x, y),
    )


def z_mid(value):
    return permute(value, lambda z, x, y: (z ^ 2, x, y), lambda z, x, y: (z ^ 4, x, y))


def eights():
    groups, seen = [], set()
    for z in range(NZ):
        for k in range(4):
            for c in range(2):
                if (z, k, c) in seen:
                    continue
                pair = (z, z ^ 1) if c else (z, (z + 1 if z % 2 else z - 1) % NZ)
                seen.update((w, k, c) for w in pair)
                groups.append([device_at(w, *((k, n) if c else (n, k)), c) for w in pair for n in range(4)])
    return groups


EIGHTS = eights()


def around(value):
    return lax.all_to_all(value, BOTH, 0, 0, axis_index_groups=EIGHTS, tiled=True)


def swap_cores(value):
    n = NZ * NX * NY * 2
    return lax.ppermute(value, BOTH, [(d, d ^ 1) for d in range(n)])


def pack_kernel(photo, sentence, ids, own, given, img_scale, txt_scale):
    width = photo.shape[1]
    holds_images = lax.axis_index("col") % 2 == 0

    def unit(raw, scale):
        values = raw[...].astype(jnp.float32)
        scale[...] = lax.rsqrt(jnp.sum(values * values, axis=1, keepdims=True) + 1e-06)
        return values * scale[...]

    img, txt = unit(photo, img_scale), unit(sentence, txt_scale)
    square = (OWN, OWN)
    diagonal = lax.broadcasted_iota(jnp.int32, square, 0) == lax.broadcasted_iota(jnp.int32, square, 1)
    spread = jnp.broadcast_to(ids[...].astype(jnp.float32), square)
    number = jnp.sum(jnp.where(diagonal, spread, 0.0), axis=1, keepdims=True)
    high = jnp.floor(number * (1 / 128))
    lane = lax.broadcasted_iota(jnp.int32, (OWN, LANES), 1)
    tail = jnp.where(lane == 0, high, jnp.where(lane == 1, number - high * 128, 0.0))
    none = jnp.zeros_like(tail)
    own[:, :width] = jnp.where(holds_images, img, txt).astype(jnp.bfloat16)
    own[:, width:] = jnp.where(holds_images, none, tail).astype(jnp.bfloat16)
    given[:, :width] = jnp.where(holds_images, txt, img).astype(jnp.bfloat16)
    given[:, width:] = jnp.where(holds_images, tail, none).astype(jnp.bfloat16)


def pack_rows(photo_features, sentence_features, ids):
    rows, width = photo_features.shape
    block = jax.ShapeDtypeStruct((rows, width + LANES), jnp.bfloat16)
    scale = jax.ShapeDtypeStruct((rows, 1), jnp.float32)
    return pl.pallas_call(
        pack_kernel,
        out_shape=(block, block, scale, scale),
        compiler_params=pltpu.CompilerParams(vmem_limit_bytes=2 << 20),
        name="pack_rows",
    )(photo_features, sentence_features, ids.reshape(1, rows))


def back_through(raw, scale, upstream):
    unit = raw.astype(jnp.float32) * scale
    inner = jnp.sum(unit * upstream, axis=1, keepdims=True)
    return scale * (upstream - unit * inner)


def cat(*parts):
    return jnp.concatenate(parts, axis=0)


def image_ids(z, y):
    row = lax.iota(jnp.int32, 16 * CHIP)
    group, zslot, r = row // (4 * CHIP), row // CHIP % 4, row % CHIP
    owner_z = z ^ jnp.where(zslot % 2 == 1, 8, 0) ^ jnp.where(zslot >= 2, 2, 0)
    owner = device_at(owner_z, group, y, r // OWN)
    return owner * OWN + r % OWN


def text_ids(tail):
    place = lax.broadcasted_iota(jnp.int32, tail.shape, 1)
    weight = jnp.where(place == 0, 128.0, jnp.where(place == 1, 1.0, 0.0))
    return jnp.sum(tail.astype(jnp.float32) * weight, axis=1).astype(jnp.int32)


def shards(
    photo_features, sentence_features, described_photo_number, logit_multiplier, logit_offset
):
    low = lax.axis_index("row")
    rest = lax.axis_index("col")
    z, y = (rest >> 5) * 16 + low, (rest >> 1) & 3
    holds_images = (rest & 1) == 0

    width = photo_features.shape[1]
    block_own, block_given, img_scale, txt_scale = pack_rows(
        photo_features, sentence_features, described_photo_number
    )

    with jax.named_scope("pair_swap"):
        block = cat(block_own, swap_cores(block_given))
    with jax.named_scope("gather_z_far"):
        block = cat(block, z_far(block))
    with jax.named_scope("gather_z_mid"):
        block = cat(block, z_mid(block))
    with jax.named_scope("gather_ring"):
        block = lax.optimization_barrier(block)
        held = around(jnp.tile(block, (8, 1)))
        first, second = held[: 16 * CHIP], held[16 * CHIP :]
    stands_first = (z == 0) | ((z % 2 == 1) & (z < NZ - 1))
    with jax.named_scope("tile_swap"):
        away_first = jnp.where(holds_images, stands_first, True)
        held = jnp.where(holds_images & stands_first, first, second)
        crossed = swap_cores(jnp.where(away_first, first, second))

    mine, other = held[:, :width], crossed[:, :width]
    img_ids = image_ids(z, y)
    mine_ids = jnp.where(holds_images, img_ids, text_ids(held[:, width:]))
    other_ids = jnp.where(holds_images, text_ids(crossed[:, width:]), img_ids)

    logits = (
        logit_multiplier
        * jnp.einsum("od,md->om", other, mine, preferred_element_type=jnp.float32)
        + logit_offset
    )
    sign = jnp.where(other_ids[:, None] == mine_ids[None, :], 1.0, -1.0).astype(jnp.float32)
    weights = (logit_multiplier * -sign * jax.nn.sigmoid(-sign * logits)).astype(jnp.bfloat16)
    away = jnp.dot(weights, mine, preferred_element_type=jnp.float32).astype(jnp.bfloat16)
    home = jnp.einsum("om,od->md", weights, other, preferred_element_type=jnp.float32)

    with jax.named_scope("tile_sum"):
        crossed = swap_cores(away).astype(jnp.float32)
        imgs, none = home + crossed, jnp.zeros_like(home)
        first = jnp.where(holds_images, jnp.where(stands_first, imgs, none), crossed)
        second = jnp.where(holds_images, jnp.where(stands_first, none, imgs), home)
    with jax.named_scope("ring_sum"):
        parts = around(cat(first.astype(jnp.bfloat16), second.astype(jnp.bfloat16)))
        total = jnp.sum(parts.reshape(8, 4 * CHIP, width).astype(jnp.float32), axis=0)
    for name, swap in (("z_mid_sum", z_mid), ("z_far_sum", z_far)):
        with jax.named_scope(name):
            rows = total.shape[0] // 2
            total = total[:rows] + swap(total[rows:].astype(jnp.bfloat16)).astype(jnp.float32)
    with jax.named_scope("pair_return"):
        kept, given = total[:OWN], swap_cores(total[OWN:])
    return (
        back_through(photo_features, img_scale, jnp.where(holds_images, kept, given)),
        back_through(sentence_features, txt_scale, jnp.where(holds_images, given, kept)),
    )


def solution(mesh):
    placed = (P(("row", "col"), None), P(("row", "col"), None), P(("row", "col")), P(), P())
    return jax.shard_map(
        shards,
        mesh=mesh,
        in_specs=placed,
        out_specs=(P(("row", "col"), None), P(("row", "col"), None)),
        check_vma=False,
    )
```

time: 147 us -> 135 us (0.918); the launches traced: 145 us -> 135 us
  blocking collectives: 0 us -> 18.3 us
  starting transfers between devices: 76 us -> 60.1 us
  waiting for transfers between devices: 57.7 us -> 44.9 us
  other arithmetic: 5.67 us -> 2.99 us
  local copies, waits for them, and re-layouts: 1.14 us -> 3.64 us
    ppermute x12 -> x4, starting transfers between devices: 54 us -> 25 us  [permute(): return lax.ppermute(value, BOTH, pairs)]
    ppermute x12 -> x4, waiting for transfers between devices: 52.4 us -> 25.6 us  [permute(): return lax.ppermute(value, BOTH, pairs)]
    all_to_all x0 -> x1, blocking collectives: none -> 18.3 us  [around(): lax.all_to_all(value, BOTH, 0, 0, axis_index_groups=EIGHTS, tiled=True)]
    all_to_all x0 -> x1, waiting for transfers between devices: none -> 14.7 us  [around(): lax.all_to_all(value, BOTH, 0, 0, axis_index_groups=EIGHTS, tiled=True)]
    ppermute x4, starting transfers between devices: 22 us -> 29.6 us  [swap_cores(): return lax.ppermute(value, BOTH, [(d, d ^ 1) for d in range(n)])]
    all_to_all x0 -> x1, starting transfers between devices: none -> 5.46 us  [around(): lax.all_to_all(value, BOTH, 0, 0, axis_index_groups=EIGHTS, tiled=True)]
    unnamed x4 -> x10, local copies, waits for them, and re-layouts: 0.01 us -> 2.19 us
  transfers between devices with their start and end apart: 16 -> 9, of which waited for: 15 -> 9; matrix products, arithmetic and copies ran while one was open for 0% -> 0% of each run, Pallas kernels for 0% -> 0%
where the time goes in v5:
time: 135 us
  starting transfers between devices  60.1 us (45%)
  waiting for transfers between devices  44.9 us (33%)
  blocking collectives  18.3 us (14%)
  local copies, waits for them, and re-layouts  3.64 us (3%)
  other arithmetic  2.99 us (2%)
  matrix products  2.29 us (2%)
  between operations  2.11 us (2%)
    ppermute x4, starting transfers between devices, swap_cores(): return lax.ppermute(value, BOTH, [(d, d ^ 1) for d in range(n)])  29.6 us
    ppermute x4, waiting for transfers between devices, permute(): return lax.ppermute(value, BOTH, pairs)  25.6 us
    ppermute x4, starting transfers between devices, permute(): return lax.ppermute(value, BOTH, pairs)  25 us
    all_to_all x1, blocking collectives, around(): lax.all_to_all(value, BOTH, 0, 0, axis_index_groups=EIGHTS, tiled=True)  18.3 us
    all_to_all x1, waiting for transfers between devices, around(): lax.all_to_all(value, BOTH, 0, 0, axis_index_groups=EIGHTS, tiled=True)  14.7 us
    all_to_all x1, starting transfers between devices, around(): lax.all_to_all(value, BOTH, 0, 0, axis_index_groups=EIGHTS, tiled=True)  5.46 us
    ppermute x4, waiting for transfers between devices, swap_cores(): return lax.ppermute(value, BOTH, [(d, d ^ 1) for d in range(n)])  4.6 us
  transfers between devices with their start and end apart: 9, of which 9 were waited for; matrix products, arithmetic and copies ran while one was open for 0% of the time, Pallas kernels for 0%

profile of v5, /device:TPU:1, one launch (start us, length us, event | category | flops | bytes accessed | tf_op | source)
XLA Modules:
  0.0 134.5 jit_solution(9280152611255803764)
XLA Ops:
  0.6 0.8 copy-done
  1.4 0.8 copy-done.2
  3.0 16.1 %collective-permute-start = (bf16[12,1280]{1,0:T(8,128)(2,1)S(1)}, bf16[12,1280]{1,0:T(8,128)(2,1)S(1)}, u32[]{:S(2)}, u32[]{:S(2)}) collective-permute-start(bf16[12,1280]{1,0:T(8,128)(2,1)S(1)} %get-tuple-element.8), channel_id=1, source_target_pairs={{0,1},{1,0},{2,3},{3,2},{4,5},{5,4},{6,7},{7,6},{8,9},{9,8},{10,11... | collective-permute-start | bytes 92168 | tf_op jit(solution)/shard_map/pair_swap/ppermute | solution.py:64
  19.1 0.8 collective-permute-done
  20.0 10.1 %collective-permute-start.1 = (bf16[24,1280]{1,0:T(8,128)(2,1)S(1)}, bf16[24,1280]{1,0:T(8,128)(2,1)S(1)}, u32[]{:S(2)}, u32[]{:S(2)}) collective-permute-start(bf16[24,1280]{1,0:T(8,128)(2,1)S(1)} %pad_maximum_fusion.3), channel_id=1, source_target_pairs={{0,512},{1,545},{2,514},{3,547},{4,516},{5,549},{6,518},{7,551},{8... | collective-permute-start | bytes 184328 | tf_op jit(solution)/shard_map/gather_z_far/ppermute | solution.py:27
  30.1 3.6 %collective-permute-done.1 = bf16[24,1280]{1,0:T(8,128)(2,1)S(1)} collective-permute-done((bf16[24,1280]{1,0:T(8,128)(2,1)S(1)}, bf16[24,1280]{1,0:T(8,128)(2,1)S(1)}, u32[]{:S(2)}, u32[]{:S(2)}) %collective-permute-start.1) | collective-permute-done | bytes 61472 | tf_op jit(solution)/shard_map/gather_z_far/ppermute | solution.py:27
  33.7 2.5 %collective-permute-start.2 = (bf16[48,1280]{1,0:T(8,128)(2,1)S(1)}, bf16[48,1280]{1,0:T(8,128)(2,1)S(1)}, u32[]{:S(2)}, u32[]{:S(2)}) collective-permute-start(bf16[48,1280]{1,0:T(8,128)(2,1)S(1)} %pad_maximum_fusion.2), channel_id=1, source_target_pairs={{0,128},{1,257},{2,130},{3,259},{4,132},{5,261},{6,134},{7,263},{8... | collective-permute-start | bytes 368648 | tf_op jit(solution)/shard_map/gather_z_mid/ppermute | solution.py:27
  36.2 9.8 %collective-permute-done.2 = bf16[48,1280]{1,0:T(8,128)(2,1)S(1)} collective-permute-done((bf16[48,1280]{1,0:T(8,128)(2,1)S(1)}, bf16[48,1280]{1,0:T(8,128)(2,1)S(1)}, u32[]{:S(2)}, u32[]{:S(2)}) %collective-permute-start.2) | collective-permute-done | bytes 122912 | tf_op jit(solution)/shard_map/gather_z_mid/ppermute | solution.py:27
  46.0 1.4 %tile.2 = bf16[8,96,1280]{2,1,0:T(8,128)(2,1)} broadcast(bf16[96,1280]{1,0:T(8,128)(2,1)S(1)} %pad_maximum_fusion.1), dimensions={1,2} | broadcast | bytes 2211840 | tf_op jit(solution)/shard_map/gather_ring/tile | solution.py:148
  47.4 5.5 %all-to-all-start = ((bf16[8,96,1280]{2,1,0:T(8,128)(2,1)}), bf16[8,96,1280]{2,1,0:T(8,128)(2,1)S(1)}, u32[]{:S(2)}, u32[]{:S(2)}) async-start(bf16[8,96,1280]{2,1,0:T(8,128)(2,1)} %tile.2), calls=%async_computation | async-start | bytes 3932160 | tf_op jit(solution)/shard_map/gather_ring/all_to_all | solution.py:59
  52.9 14.7 %all-to-all-done = bf16[8,96,1280]{2,1,0:T(8,128)(2,1)S(1)} async-done(((bf16[8,96,1280]{2,1,0:T(8,128)(2,1)}), bf16[8,96,1280]{2,1,0:T(8,128)(2,1)S(1)}, u32[]{:S(2)}, u32[]{:S(2)}) %all-to-all-start) | async-done | bytes 1966112 | tf_op jit(solution)/shard_map/gather_ring/all_to_all | solution.py:59
  67.5 1.1 broadcast_select_fusion.1
  68.6 6.6 %collective-permute-start.3 = (bf16[384,1280]{1,0:T(8,128)(2,1)}, bf16[384,1280]{1,0:T(8,128)(2,1)S(1)}, u32[]{:S(2)}, u32[]{:S(2)}) collective-permute-start(bf16[384,1280]{1,0:T(8,128)(2,1)} %bitcast.1), channel_id=1, source_target_pairs={{0,1},{1,0},{2,3},{3,2},{4,5},{5,4},{6,7},{7,6},{8,9},{9,8},{10,11... | collective-permute-start | bytes 2949128 | tf_op jit(solution)/shard_map/tile_swap/ppermute | solution.py:64
  76.6 1.1 collective-permute-done.3
  77.9 0.8 fusion.8
  79.3 2.3 %collective-permute-start.4 = (bf16[384,1152]{1,0:T(8,128)(2,1)S(1)}, bf16[384,1152]{1,0:T(8,128)(2,1)S(1)}, u32[]{:S(2)}, u32[]{:S(2)}) collective-permute-start(bf16[384,1152]{1,0:T(8,128)(2,1)S(1)} %convolution_convert_fusion), channel_id=1, source_target_pairs={{0,1},{1,0},{2,3},{3,2},{4,5},{5,4},{6,7},{7,6},{8,9},{9,8},{10,11... | collective-permute-start | bytes 2654216 | tf_op jit(solution)/shard_map/tile_sum/ppermute | solution.py:64
  81.6 2.0 %collective-permute-done.4 = bf16[384,1152]{1,0:T(8,128)(2,1)S(1)} collective-permute-done((bf16[384,1152]{1,0:T(8,128)(2,1)S(1)}, bf16[384,1152]{1,0:T(8,128)(2,1)S(1)}, u32[]{:S(2)}, u32[]{:S(2)}) %collective-permute-start.4) | collective-permute-done | bytes 884768 | tf_op jit(solution)/shard_map/tile_sum/ppermute | solution.py:64
  83.6 0.9 fusion
  84.6 18.3 %all_to_all.15 = bf16[8,96,1152]{2,1,0:T(8,128)(2,1)S(1)} all-to-all(bf16[8,96,1152]{2,1,0:T(8,128)(2,1)S(1)} %bitcast.7), channel_id=1, replica_groups={{0,8,16,24,992,1000,1008,1016},{1,3,5,7,65,67,69,71},{2,10,18,26,994,10..., dimensions={0} | all-to-all | bytes 3538944 | tf_op jit(solution)/shard_map/ring_sum/all_to_all | solution.py:59
  103.2 1.9 %collective-permute-start.5 = (bf16[48,1152]{1,0:T(8,128)(2,1)S(1)}, bf16[48,1152]{1,0:T(8,128)(2,1)S(1)}, u32[]{:S(2)}, u32[]{:S(2)}) collective-permute-start(bf16[48,1152]{1,0:T(8,128)(2,1)S(1)} %slice.92), channel_id=1, source_target_pairs={{0,128},{1,257},{2,130},{3,259},{4,132},{5,261},{6,134},{7,263},{8... | collective-permute-start | bytes 331784 | tf_op jit(solution)/shard_map/z_mid_sum/ppermute | solution.py:27
  105.1 8.7 %collective-permute-done.5 = bf16[48,1152]{1,0:T(8,128)(2,1)S(1)} collective-permute-done((bf16[48,1152]{1,0:T(8,128)(2,1)S(1)}, bf16[48,1152]{1,0:T(8,128)(2,1)S(1)}, u32[]{:S(2)}, u32[]{:S(2)}) %collective-permute-start.5) | collective-permute-done | bytes 110624 | tf_op jit(solution)/shard_map/z_mid_sum/ppermute | solution.py:27
  113.9 10.5 %collective-permute-start.6 = (bf16[24,1152]{1,0:T(8,128)(2,1)S(1)}, bf16[24,1152]{1,0:T(8,128)(2,1)S(1)}, u32[]{:S(2)}, u32[]{:S(2)}) collective-permute-start(bf16[24,1152]{1,0:T(8,128)(2,1)S(1)} %slice.93), channel_id=1, source_target_pairs={{0,512},{1,545},{2,514},{3,547},{4,516},{5,549},{6,518},{7,551},{8... | collective-permute-start | bytes 165896 | tf_op jit(solution)/shard_map/z_far_sum/ppermute | solution.py:27
  124.4 3.6 %collective-permute-done.6 = bf16[24,1152]{1,0:T(8,128)(2,1)S(1)} collective-permute-done((bf16[24,1152]{1,0:T(8,128)(2,1)S(1)}, bf16[24,1152]{1,0:T(8,128)(2,1)S(1)}, u32[]{:S(2)}, u32[]{:S(2)}) %collective-permute-start.6) | collective-permute-done | bytes 55328 | tf_op jit(solution)/shard_map/z_far_sum/ppermute | solution.py:27
  128.0 4.6 %collective-permute-start.7 = (f32[12,1152]{1,0:T(8,128)S(1)}, f32[12,1152]{1,0:T(8,128)S(1)}, u32[]{:S(2)}, u32[]{:S(2)}) collective-permute-start(f32[12,1152]{1,0:T(8,128)S(1)} %slice.63), channel_id=1, source_target_pairs={{0,1},{1,0},{2,3},{3,2},{4,5},{5,4},{6,7},{7,6},{8,9},{9,8},{10,11... | collective-permute-start | bytes 165896 | tf_op jit(solution)/shard_map/pair_return/ppermute | solution.py:64
  (29 shorter events, 4.1 us)
Async XLA Ops:
  0.6 0.8 copy-start
  1.4 0.8 copy-start.2
  2.2 0.7 copy-start.4
  3.0 16.9 %collective-permute-start = (bf16[12,1280]{1,0:T(8,128)(2,1)S(1)}, bf16[12,1280]{1,0:T(8,128)(2,1)S(1)}, u32[]{:S(2)}, u32[]{:S(2)}) collective-permute-start(bf16[12,1280]{1,0:T(8,128)(2,1)S(1)} %get-tuple-element.8), channel_id=1, source_target_pairs={{0,1},{1,0},{2,3},{3,2},{4,5},{5,4},{6,7},{7,6},{8,9},{9,8},{10,11... | collective-permute-start | bytes 92168 | tf_op jit(solution)/shard_map/pair_swap/ppermute | solution.py:64
  20.0 13.7 %collective-permute-start.1 = (bf16[24,1280]{1,0:T(8,128)(2,1)S(1)}, bf16[24,1280]{1,0:T(8,128)(2,1)S(1)}, u32[]{:S(2)}, u32[]{:S(2)}) collective-permute-start(bf16[24,1280]{1,0:T(8,128)(2,1)S(1)} %pad_maximum_fusion.3), channel_id=1, source_target_pairs={{0,512},{1,545},{2,514},{3,547},{4,516},{5,549},{6,518},{7,551},{8... | collective-permute-start | bytes 184328 | tf_op jit(solution)/shard_map/gather_z_far/ppermute | solution.py:27
  33.7 12.3 %collective-permute-start.2 = (bf16[48,1280]{1,0:T(8,128)(2,1)S(1)}, bf16[48,1280]{1,0:T(8,128)(2,1)S(1)}, u32[]{:S(2)}, u32[]{:S(2)}) collective-permute-start(bf16[48,1280]{1,0:T(8,128)(2,1)S(1)} %pad_maximum_fusion.2), channel_id=1, source_target_pairs={{0,128},{1,257},{2,130},{3,259},{4,132},{5,261},{6,134},{7,263},{8... | collective-permute-start | bytes 368648 | tf_op jit(solution)/shard_map/gather_z_mid/ppermute | solution.py:27
  47.4 20.1 %all-to-all-start = ((bf16[8,96,1280]{2,1,0:T(8,128)(2,1)}), bf16[8,96,1280]{2,1,0:T(8,128)(2,1)S(1)}, u32[]{:S(2)}, u32[]{:S(2)}) async-start(bf16[8,96,1280]{2,1,0:T(8,128)(2,1)} %tile.2), calls=%async_computation | async-start | bytes 3932160 | tf_op jit(solution)/shard_map/gather_ring/all_to_all | solution.py:59
  68.6 9.0 %collective-permute-start.3 = (bf16[384,1280]{1,0:T(8,128)(2,1)}, bf16[384,1280]{1,0:T(8,128)(2,1)S(1)}, u32[]{:S(2)}, u32[]{:S(2)}) collective-permute-start(bf16[384,1280]{1,0:T(8,128)(2,1)} %bitcast.1), channel_id=1, source_target_pairs={{0,1},{1,0},{2,3},{3,2},{4,5},{5,4},{6,7},{7,6},{8,9},{9,8},{10,11... | collective-permute-start | bytes 2949128 | tf_op jit(solution)/shard_map/tile_swap/ppermute | solution.py:64
  79.3 4.3 %collective-permute-start.4 = (bf16[384,1152]{1,0:T(8,128)(2,1)S(1)}, bf16[384,1152]{1,0:T(8,128)(2,1)S(1)}, u32[]{:S(2)}, u32[]{:S(2)}) collective-permute-start(bf16[384,1152]{1,0:T(8,128)(2,1)S(1)} %convolution_convert_fusion), channel_id=1, source_target_pairs={{0,1},{1,0},{2,3},{3,2},{4,5},{5,4},{6,7},{7,6},{8,9},{9,8},{10,11... | collective-permute-start | bytes 2654216 | tf_op jit(solution)/shard_map/tile_sum/ppermute | solution.py:64
  102.9 30.7 %copy-start.1 = (bf16[12,1152]{1,0:T(8,128)(2,1)S(1)}, bf16[12,1152]{1,0:T(8,128)(2,1)}, u32[]{:S(2)}) copy-start(bf16[12,1152]{1,0:T(8,128)(2,1)} %sentence.1) | copy-start | bytes 82948
  102.9 30.7 %copy-start.3 = (bf16[12,1152]{1,0:T(8,128)(2,1)S(1)}, bf16[12,1152]{1,0:T(8,128)(2,1)}, u32[]{:S(2)}) copy-start(bf16[12,1152]{1,0:T(8,128)(2,1)} %photo.1) | copy-start | bytes 82948
  103.2 10.7 %collective-permute-start.5 = (bf16[48,1152]{1,0:T(8,128)(2,1)S(1)}, bf16[48,1152]{1,0:T(8,128)(2,1)S(1)}, u32[]{:S(2)}, u32[]{:S(2)}) collective-permute-start(bf16[48,1152]{1,0:T(8,128)(2,1)S(1)} %slice.92), channel_id=1, source_target_pairs={{0,128},{1,257},{2,130},{3,259},{4,132},{5,261},{6,134},{7,263},{8... | collective-permute-start | bytes 331784 | tf_op jit(solution)/shard_map/z_mid_sum/ppermute | solution.py:27
  113.9 14.1 %collective-permute-start.6 = (bf16[24,1152]{1,0:T(8,128)(2,1)S(1)}, bf16[24,1152]{1,0:T(8,128)(2,1)S(1)}, u32[]{:S(2)}, u32[]{:S(2)}) collective-permute-start(bf16[24,1152]{1,0:T(8,128)(2,1)S(1)} %slice.93), channel_id=1, source_target_pairs={{0,512},{1,545},{2,514},{3,547},{4,516},{5,549},{6,518},{7,551},{8... | collective-permute-start | bytes 165896 | tf_op jit(solution)/shard_map/z_far_sum/ppermute | solution.py:27
  128.0 5.5 %collective-permute-start.7 = (f32[12,1152]{1,0:T(8,128)S(1)}, f32[12,1152]{1,0:T(8,128)S(1)}, u32[]{:S(2)}, u32[]{:S(2)}) collective-permute-start(f32[12,1152]{1,0:T(8,128)S(1)} %slice.63), channel_id=1, source_target_pairs={{0,1},{1,0},{2,3},{3,2},{4,5},{5,4},{6,7},{7,6},{8,9},{9,8},{10,11... | collective-permute-start | bytes 165896 | tf_op jit(solution)/shard_map/pair_return/ppermute | solution.py:64

commit v6 on v5

--- a/solution.py
+++ b/solution.py
@@ -64,7 +64,19 @@
     return lax.ppermute(value, BOTH, [(d, d ^ 1) for d in range(n)])
 
 
-def pack_kernel(photo, sentence, ids, own, given, img_scale, txt_scale):
+def pack_kernel(
+    photo_in, sentence_in, ids_in, own, given, img_scale, txt_scale, photo, sentence, ids, arrived
+):
+    copies = [
+        pltpu.make_async_copy(source, target, arrived.at[k])
+        for k, (source, target) in enumerate(
+            ((photo_in, photo), (sentence_in, sentence), (ids_in, ids))
+        )
+    ]
+    for copy in copies:
+        copy.start()
+    for copy in copies:
+        copy.wait()
     width = photo.shape[1]
     holds_images = lax.axis_index("col") % 2 == 0
 
@@ -95,9 +107,21 @@
     return pl.pallas_call(
         pack_kernel,
         out_shape=(block, block, scale, scale),
+        in_specs=[pl.BlockSpec(memory_space=pltpu.HBM)] * 3,
+        scratch_shapes=[
+            pltpu.VMEM((rows, width), photo_features.dtype),
+            pltpu.VMEM((rows, width), sentence_features.dtype),
+            pltpu.VMEM((1, rows), ids.dtype),
+            pltpu.SemaphoreType.DMA((3,)),
+        ],
         compiler_params=pltpu.CompilerParams(vmem_limit_bytes=2 << 20),
         name="pack_rows",
-    )(photo_features, sentence_features, ids.reshape(1, rows))
+    )(
+        *(
+            pltpu.with_memory_space_constraint(a, pltpu.HBM)
+            for a in (photo_features, sentence_features, ids.reshape(1, rows))
+        )
+    )
 
 
 def back_through(raw, scale, upstream):

time: 135 us -> 134 us (level)
  local copies, waits for them, and re-layouts: 3.64 us -> 1.45 us
    unnamed x10 -> x4, local copies, waits for them, and re-layouts: 2.19 us -> 0.01 us
where the time goes in v6:
time: 134 us; the launch traced here: 133 us
  starting transfers between devices  60.1 us (45%)
  waiting for transfers between devices  44.9 us (34%)
  blocking collectives  18.3 us (14%)
  other arithmetic  2.98 us (2%)
  matrix products  2.28 us (2%)
  between operations  2.1 us (2%)
  local copies, waits for them, and re-layouts  1.45 us (1%)
    ppermute x4, starting transfers between devices, swap_cores(): return lax.ppermute(value, BOTH, [(d, d ^ 1) for d in range(n)])  29.6 us
    ppermute x4, waiting for transfers between devices, permute(): return lax.ppermute(value, BOTH, pairs)  25.7 us
    ppermute x4, starting transfers between devices, permute(): return lax.ppermute(value, BOTH, pairs)  25 us
    all_to_all x1, blocking collectives, around(): lax.all_to_all(value, BOTH, 0, 0, axis_index_groups=EIGHTS, tiled=True)  18.3 us
    all_to_all x1, waiting for transfers between devices, around(): lax.all_to_all(value, BOTH, 0, 0, axis_index_groups=EIGHTS, tiled=True)  14.7 us
    all_to_all x1, starting transfers between devices, around(): lax.all_to_all(value, BOTH, 0, 0, axis_index_groups=EIGHTS, tiled=True)  5.46 us
    ppermute x4, waiting for transfers between devices, swap_cores(): return lax.ppermute(value, BOTH, [(d, d ^ 1) for d in range(n)])  4.59 us
  transfers between devices with their start and end apart: 9, of which 9 were waited for; matrix products, arithmetic and copies ran while one was open for 0% of the time, Pallas kernels for 0%

profile of v6, /device:TPU:1, one launch (start us, length us, event | category | flops | bytes accessed | tf_op | source)
XLA Modules:
  0.0 133.1 jit_solution(9534753778485195994)
XLA Ops:
  0.6 1.0 pack_rows.1
  1.7 16.1 %collective-permute-start = (bf16[12,1280]{1,0:T(8,128)(2,1)S(1)}, bf16[12,1280]{1,0:T(8,128)(2,1)S(1)}, u32[]{:S(2)}, u32[]{:S(2)}) collective-permute-start(bf16[12,1280]{1,0:T(8,128)(2,1)S(1)} %get-tuple-element.8), channel_id=1, source_target_pairs={{0,1},{1,0},{2,3},{3,2},{4,5},{5,4},{6,7},{7,6},{8,9},{9,8},{10,11... | collective-permute-start | bytes 92168 | tf_op jit(solution)/shard_map/pair_swap/ppermute | solution.py:64
  17.7 0.8 collective-permute-done
  18.6 10.1 %collective-permute-start.1 = (bf16[24,1280]{1,0:T(8,128)(2,1)S(1)}, bf16[24,1280]{1,0:T(8,128)(2,1)S(1)}, u32[]{:S(2)}, u32[]{:S(2)}) collective-permute-start(bf16[24,1280]{1,0:T(8,128)(2,1)S(1)} %pad_maximum_fusion.3), channel_id=1, source_target_pairs={{0,512},{1,545},{2,514},{3,547},{4,516},{5,549},{6,518},{7,551},{8... | collective-permute-start | bytes 184328 | tf_op jit(solution)/shard_map/gather_z_far/ppermute | solution.py:27
  28.7 3.6 %collective-permute-done.1 = bf16[24,1280]{1,0:T(8,128)(2,1)S(1)} collective-permute-done((bf16[24,1280]{1,0:T(8,128)(2,1)S(1)}, bf16[24,1280]{1,0:T(8,128)(2,1)S(1)}, u32[]{:S(2)}, u32[]{:S(2)}) %collective-permute-start.1) | collective-permute-done | bytes 61472 | tf_op jit(solution)/shard_map/gather_z_far/ppermute | solution.py:27
  32.3 2.5 %collective-permute-start.2 = (bf16[48,1280]{1,0:T(8,128)(2,1)S(1)}, bf16[48,1280]{1,0:T(8,128)(2,1)S(1)}, u32[]{:S(2)}, u32[]{:S(2)}) collective-permute-start(bf16[48,1280]{1,0:T(8,128)(2,1)S(1)} %pad_maximum_fusion.2), channel_id=1, source_target_pairs={{0,128},{1,257},{2,130},{3,259},{4,132},{5,261},{6,134},{7,263},{8... | collective-permute-start | bytes 368648 | tf_op jit(solution)/shard_map/gather_z_mid/ppermute | solution.py:27
  34.8 9.8 %collective-permute-done.2 = bf16[48,1280]{1,0:T(8,128)(2,1)S(1)} collective-permute-done((bf16[48,1280]{1,0:T(8,128)(2,1)S(1)}, bf16[48,1280]{1,0:T(8,128)(2,1)S(1)}, u32[]{:S(2)}, u32[]{:S(2)}) %collective-permute-start.2) | collective-permute-done | bytes 122912 | tf_op jit(solution)/shard_map/gather_z_mid/ppermute | solution.py:27
  44.6 1.4 %tile.2 = bf16[8,96,1280]{2,1,0:T(8,128)(2,1)} broadcast(bf16[96,1280]{1,0:T(8,128)(2,1)S(1)} %pad_maximum_fusion.1), dimensions={1,2} | broadcast | bytes 2211840 | tf_op jit(solution)/shard_map/gather_ring/tile | solution.py:172
  46.0 5.5 %all-to-all-start = ((bf16[8,96,1280]{2,1,0:T(8,128)(2,1)}), bf16[8,96,1280]{2,1,0:T(8,128)(2,1)S(1)}, u32[]{:S(2)}, u32[]{:S(2)}) async-start(bf16[8,96,1280]{2,1,0:T(8,128)(2,1)} %tile.2), calls=%async_computation | async-start | bytes 3932160 | tf_op jit(solution)/shard_map/gather_ring/all_to_all | solution.py:59
  51.5 14.7 %all-to-all-done = bf16[8,96,1280]{2,1,0:T(8,128)(2,1)S(1)} async-done(((bf16[8,96,1280]{2,1,0:T(8,128)(2,1)}), bf16[8,96,1280]{2,1,0:T(8,128)(2,1)S(1)}, u32[]{:S(2)}, u32[]{:S(2)}) %all-to-all-start) | async-done | bytes 1966112 | tf_op jit(solution)/shard_map/gather_ring/all_to_all | solution.py:59
  66.1 1.1 broadcast_select_fusion.1
  67.2 6.6 %collective-permute-start.3 = (bf16[384,1280]{1,0:T(8,128)(2,1)}, bf16[384,1280]{1,0:T(8,128)(2,1)S(1)}, u32[]{:S(2)}, u32[]{:S(2)}) collective-permute-start(bf16[384,1280]{1,0:T(8,128)(2,1)} %bitcast.1), channel_id=1, source_target_pairs={{0,1},{1,0},{2,3},{3,2},{4,5},{5,4},{6,7},{7,6},{8,9},{9,8},{10,11... | collective-permute-start | bytes 2949128 | tf_op jit(solution)/shard_map/tile_swap/ppermute | solution.py:64
  75.2 1.1 collective-permute-done.3
  76.5 0.8 fusion.8
  77.9 2.3 %collective-permute-start.4 = (bf16[384,1152]{1,0:T(8,128)(2,1)S(1)}, bf16[384,1152]{1,0:T(8,128)(2,1)S(1)}, u32[]{:S(2)}, u32[]{:S(2)}) collective-permute-start(bf16[384,1152]{1,0:T(8,128)(2,1)S(1)} %convolution_convert_fusion), channel_id=1, source_target_pairs={{0,1},{1,0},{2,3},{3,2},{4,5},{5,4},{6,7},{7,6},{8,9},{9,8},{10,11... | collective-permute-start | bytes 2654216 | tf_op jit(solution)/shard_map/tile_sum/ppermute | solution.py:64
  80.2 2.0 %collective-permute-done.4 = bf16[384,1152]{1,0:T(8,128)(2,1)S(1)} collective-permute-done((bf16[384,1152]{1,0:T(8,128)(2,1)S(1)}, bf16[384,1152]{1,0:T(8,128)(2,1)S(1)}, u32[]{:S(2)}, u32[]{:S(2)}) %collective-permute-start.4) | collective-permute-done | bytes 884768 | tf_op jit(solution)/shard_map/tile_sum/ppermute | solution.py:64
  82.2 0.9 fusion
  83.3 18.3 %all_to_all.15 = bf16[8,96,1152]{2,1,0:T(8,128)(2,1)S(1)} all-to-all(bf16[8,96,1152]{2,1,0:T(8,128)(2,1)S(1)} %bitcast.6), channel_id=1, replica_groups={{0,8,16,24,992,1000,1008,1016},{1,3,5,7,65,67,69,71},{2,10,18,26,994,10..., dimensions={0} | all-to-all | bytes 3538944 | tf_op jit(solution)/shard_map/ring_sum/all_to_all | solution.py:59
  101.8 1.9 %collective-permute-start.5 = (bf16[48,1152]{1,0:T(8,128)(2,1)S(1)}, bf16[48,1152]{1,0:T(8,128)(2,1)S(1)}, u32[]{:S(2)}, u32[]{:S(2)}) collective-permute-start(bf16[48,1152]{1,0:T(8,128)(2,1)S(1)} %slice.92), channel_id=1, source_target_pairs={{0,128},{1,257},{2,130},{3,259},{4,132},{5,261},{6,134},{7,263},{8... | collective-permute-start | bytes 331784 | tf_op jit(solution)/shard_map/z_mid_sum/ppermute | solution.py:27
  103.7 8.7 %collective-permute-done.5 = bf16[48,1152]{1,0:T(8,128)(2,1)S(1)} collective-permute-done((bf16[48,1152]{1,0:T(8,128)(2,1)S(1)}, bf16[48,1152]{1,0:T(8,128)(2,1)S(1)}, u32[]{:S(2)}, u32[]{:S(2)}) %collective-permute-start.5) | collective-permute-done | bytes 110624 | tf_op jit(solution)/shard_map/z_mid_sum/ppermute | solution.py:27
  112.5 10.6 %collective-permute-start.6 = (bf16[24,1152]{1,0:T(8,128)(2,1)S(1)}, bf16[24,1152]{1,0:T(8,128)(2,1)S(1)}, u32[]{:S(2)}, u32[]{:S(2)}) collective-permute-start(bf16[24,1152]{1,0:T(8,128)(2,1)S(1)} %slice.93), channel_id=1, source_target_pairs={{0,512},{1,545},{2,514},{3,547},{4,516},{5,549},{6,518},{7,551},{8... | collective-permute-start | bytes 165896 | tf_op jit(solution)/shard_map/z_far_sum/ppermute | solution.py:27
  123.0 3.6 %collective-permute-done.6 = bf16[24,1152]{1,0:T(8,128)(2,1)S(1)} collective-permute-done((bf16[24,1152]{1,0:T(8,128)(2,1)S(1)}, bf16[24,1152]{1,0:T(8,128)(2,1)S(1)}, u32[]{:S(2)}, u32[]{:S(2)}) %collective-permute-start.6) | collective-permute-done | bytes 55328 | tf_op jit(solution)/shard_map/z_far_sum/ppermute | solution.py:27
  126.6 4.6 %collective-permute-start.7 = (f32[12,1152]{1,0:T(8,128)S(1)}, f32[12,1152]{1,0:T(8,128)S(1)}, u32[]{:S(2)}, u32[]{:S(2)}) collective-permute-start(f32[12,1152]{1,0:T(8,128)S(1)} %slice.63), channel_id=1, source_target_pairs={{0,1},{1,0},{2,3},{3,2},{4,5},{5,4},{6,7},{7,6},{8,9},{9,8},{10,11... | collective-permute-start | bytes 165896 | tf_op jit(solution)/shard_map/pair_return/ppermute | solution.py:64
  132.4 0.8 subtract_multiply_fusion
  (23 shorter events, 2.5 us)
Async XLA Ops:
  1.7 16.9 %collective-permute-start = (bf16[12,1280]{1,0:T(8,128)(2,1)S(1)}, bf16[12,1280]{1,0:T(8,128)(2,1)S(1)}, u32[]{:S(2)}, u32[]{:S(2)}) collective-permute-start(bf16[12,1280]{1,0:T(8,128)(2,1)S(1)} %get-tuple-element.8), channel_id=1, source_target_pairs={{0,1},{1,0},{2,3},{3,2},{4,5},{5,4},{6,7},{7,6},{8,9},{9,8},{10,11... | collective-permute-start | bytes 92168 | tf_op jit(solution)/shard_map/pair_swap/ppermute | solution.py:64
  18.6 13.7 %collective-permute-start.1 = (bf16[24,1280]{1,0:T(8,128)(2,1)S(1)}, bf16[24,1280]{1,0:T(8,128)(2,1)S(1)}, u32[]{:S(2)}, u32[]{:S(2)}) collective-permute-start(bf16[24,1280]{1,0:T(8,128)(2,1)S(1)} %pad_maximum_fusion.3), channel_id=1, source_target_pairs={{0,512},{1,545},{2,514},{3,547},{4,516},{5,549},{6,518},{7,551},{8... | collective-permute-start | bytes 184328 | tf_op jit(solution)/shard_map/gather_z_far/ppermute | solution.py:27
  32.3 12.3 %collective-permute-start.2 = (bf16[48,1280]{1,0:T(8,128)(2,1)S(1)}, bf16[48,1280]{1,0:T(8,128)(2,1)S(1)}, u32[]{:S(2)}, u32[]{:S(2)}) collective-permute-start(bf16[48,1280]{1,0:T(8,128)(2,1)S(1)} %pad_maximum_fusion.2), channel_id=1, source_target_pairs={{0,128},{1,257},{2,130},{3,259},{4,132},{5,261},{6,134},{7,263},{8... | collective-permute-start | bytes 368648 | tf_op jit(solution)/shard_map/gather_z_mid/ppermute | solution.py:27
  46.0 20.1 %all-to-all-start = ((bf16[8,96,1280]{2,1,0:T(8,128)(2,1)}), bf16[8,96,1280]{2,1,0:T(8,128)(2,1)S(1)}, u32[]{:S(2)}, u32[]{:S(2)}) async-start(bf16[8,96,1280]{2,1,0:T(8,128)(2,1)} %tile.2), calls=%async_computation | async-start | bytes 3932160 | tf_op jit(solution)/shard_map/gather_ring/all_to_all | solution.py:59
  67.2 9.0 %collective-permute-start.3 = (bf16[384,1280]{1,0:T(8,128)(2,1)}, bf16[384,1280]{1,0:T(8,128)(2,1)S(1)}, u32[]{:S(2)}, u32[]{:S(2)}) collective-permute-start(bf16[384,1280]{1,0:T(8,128)(2,1)} %bitcast.1), channel_id=1, source_target_pairs={{0,1},{1,0},{2,3},{3,2},{4,5},{5,4},{6,7},{7,6},{8,9},{9,8},{10,11... | collective-permute-start | bytes 2949128 | tf_op jit(solution)/shard_map/tile_swap/ppermute | solution.py:64
  77.9 4.3 %collective-permute-start.4 = (bf16[384,1152]{1,0:T(8,128)(2,1)S(1)}, bf16[384,1152]{1,0:T(8,128)(2,1)S(1)}, u32[]{:S(2)}, u32[]{:S(2)}) collective-permute-start(bf16[384,1152]{1,0:T(8,128)(2,1)S(1)} %convolution_convert_fusion), channel_id=1, source_target_pairs={{0,1},{1,0},{2,3},{3,2},{4,5},{5,4},{6,7},{7,6},{8,9},{9,8},{10,11... | collective-permute-start | bytes 2654216 | tf_op jit(solution)/shard_map/tile_sum/ppermute | solution.py:64
  101.5 30.7 %copy-start = (bf16[12,1152]{1,0:T(8,128)(2,1)S(1)}, bf16[12,1152]{1,0:T(8,128)(2,1)}, u32[]{:S(2)}) copy-start(bf16[12,1152]{1,0:T(8,128)(2,1)} %sentence_in.1) | copy-start | bytes 82948
  101.5 30.7 %copy-start.1 = (bf16[12,1152]{1,0:T(8,128)(2,1)S(1)}, bf16[12,1152]{1,0:T(8,128)(2,1)}, u32[]{:S(2)}) copy-start(bf16[12,1152]{1,0:T(8,128)(2,1)} %photo_in.1) | copy-start | bytes 82948
  101.8 10.7 %collective-permute-start.5 = (bf16[48,1152]{1,0:T(8,128)(2,1)S(1)}, bf16[48,1152]{1,0:T(8,128)(2,1)S(1)}, u32[]{:S(2)}, u32[]{:S(2)}) collective-permute-start(bf16[48,1152]{1,0:T(8,128)(2,1)S(1)} %slice.92), channel_id=1, source_target_pairs={{0,128},{1,257},{2,130},{3,259},{4,132},{5,261},{6,134},{7,263},{8... | collective-permute-start | bytes 331784 | tf_op jit(solution)/shard_map/z_mid_sum/ppermute | solution.py:27
  112.5 14.1 %collective-permute-start.6 = (bf16[24,1152]{1,0:T(8,128)(2,1)S(1)}, bf16[24,1152]{1,0:T(8,128)(2,1)S(1)}, u32[]{:S(2)}, u32[]{:S(2)}) collective-permute-start(bf16[24,1152]{1,0:T(8,128)(2,1)S(1)} %slice.93), channel_id=1, source_target_pairs={{0,512},{1,545},{2,514},{3,547},{4,516},{5,549},{6,518},{7,551},{8... | collective-permute-start | bytes 165896 | tf_op jit(solution)/shard_map/z_far_sum/ppermute | solution.py:27
  126.6 5.5 %collective-permute-start.7 = (f32[12,1152]{1,0:T(8,128)S(1)}, f32[12,1152]{1,0:T(8,128)S(1)}, u32[]{:S(2)}, u32[]{:S(2)}) collective-permute-start(f32[12,1152]{1,0:T(8,128)S(1)} %slice.63), channel_id=1, source_target_pairs={{0,1},{1,0},{2,3},{3,2},{4,5},{5,4},{6,7},{7,6},{8,9},{9,8},{10,11... | collective-permute-start | bytes 165896 | tf_op jit(solution)/shard_map/pair_return/ppermute | solution.py:64

commit v7 on v6

--- a/solution.py
+++ b/solution.py
@@ -98,6 +98,22 @@
     own[:, width:] = jnp.where(holds_images, none, tail).astype(jnp.bfloat16)
     given[:, :width] = jnp.where(holds_images, txt, img).astype(jnp.bfloat16)
     given[:, width:] = jnp.where(holds_images, tail, none).astype(jnp.bfloat16)
+
+
+def copies_kernel(block, out):
+    rows = block.shape[0]
+    for k in range(out.shape[0] // rows):
+        out[k * rows : (k + 1) * rows, :] = block[...]
+
+
+def eight_copies(block):
+    rows, width = block.shape
+    return pl.pallas_call(
+        copies_kernel,
+        out_shape=jax.ShapeDtypeStruct((8 * rows, width), block.dtype),
+        compiler_params=pltpu.CompilerParams(vmem_limit_bytes=4 << 20),
+        name="eight_copies",
+    )(block)
 
 
 def pack_rows(photo_features, sentence_features, ids):
@@ -168,8 +184,7 @@
     with jax.named_scope("gather_z_mid"):
         block = cat(block, z_mid(block))
     with jax.named_scope("gather_ring"):
-        block = lax.optimization_barrier(block)
-        held = around(jnp.tile(block, (8, 1)))
+        held = around(eight_copies(block))
         first, second = held[: 16 * CHIP], held[16 * CHIP :]
     stands_first = (z == 0) | ((z % 2 == 1) & (z < NZ - 1))
     with jax.named_scope("tile_swap"):

time: 134 us -> 134 us (level)
  Pallas kernels: 1.03 us -> 2.44 us
  local copies, waits for them, and re-layouts: 1.45 us -> 0.04 us
    pallas_call x0 -> x1, Pallas kernels: none -> 1.41 us  [eight_copies(): pl.pallas_call(copies_kernel, out_shape=jax.ShapeDtypeStruct((8 * rows, w...]
    another operation x1 -> x0, local copies, waits for them, and re-layouts: 1.41 us -> none  [shards(): held = around(jnp.tile(block, (8, 1)))]
where the time goes in v7:
time: 134 us; the launch traced here: 133 us
  starting transfers between devices  60.1 us (45%)
  waiting for transfers between devices  44.9 us (34%)
  blocking collectives  18.3 us (14%)
  other arithmetic  2.98 us (2%)
  Pallas kernels  2.44 us (2%)
  matrix products  2.29 us (2%)
  between operations  2.1 us (2%)
    ppermute x4, starting transfers between devices, swap_cores(): return lax.ppermute(value, BOTH, [(d, d ^ 1) for d in range(n)])  29.6 us
    ppermute x4, waiting for transfers between devices, permute(): return lax.ppermute(value, BOTH, pairs)  25.7 us
    ppermute x4, starting transfers between devices, permute(): return lax.ppermute(value, BOTH, pairs)  25 us
    all_to_all x1, blocking collectives, around(): lax.all_to_all(value, BOTH, 0, 0, axis_index_groups=EIGHTS, tiled=True)  18.3 us
    all_to_all x1, waiting for transfers between devices, around(): lax.all_to_all(value, BOTH, 0, 0, axis_index_groups=EIGHTS, tiled=True)  14.7 us
    all_to_all x1, starting transfers between devices, around(): lax.all_to_all(value, BOTH, 0, 0, axis_index_groups=EIGHTS, tiled=True)  5.46 us
    ppermute x4, waiting for transfers between devices, swap_cores(): return lax.ppermute(value, BOTH, [(d, d ^ 1) for d in range(n)])  4.59 us
  transfers between devices with their start and end apart: 9, of which 9 were waited for; matrix products, arithmetic and copies ran while one was open for 0% of the time, Pallas kernels for 0%

profile of v7, /device:TPU:1, one launch (start us, length us, event | category | flops | bytes accessed | tf_op | source)
XLA Modules:
  0.0 133.1 jit_solution(5286024596952214542)
XLA Ops:
  0.6 1.0 pack_rows.1
  1.7 16.1 %collective-permute-start = (bf16[12,1280]{1,0:T(8,128)(2,1)S(1)}, bf16[12,1280]{1,0:T(8,128)(2,1)S(1)}, u32[]{:S(2)}, u32[]{:S(2)}) collective-permute-start(bf16[12,1280]{1,0:T(8,128)(2,1)S(1)} %get-tuple-element.8), channel_id=1, source_target_pairs={{0,1},{1,0},{2,3},{3,2},{4,5},{5,4},{6,7},{7,6},{8,9},{9,8},{10,11... | collective-permute-start | bytes 92168 | tf_op jit(solution)/shard_map/pair_swap/ppermute | solution.py:64
  17.7 0.8 collective-permute-done
  18.6 10.1 %collective-permute-start.1 = (bf16[24,1280]{1,0:T(8,128)(2,1)S(1)}, bf16[24,1280]{1,0:T(8,128)(2,1)S(1)}, u32[]{:S(2)}, u32[]{:S(2)}) collective-permute-start(bf16[24,1280]{1,0:T(8,128)(2,1)S(1)} %pad_maximum_fusion.3), channel_id=1, source_target_pairs={{0,512},{1,545},{2,514},{3,547},{4,516},{5,549},{6,518},{7,551},{8... | collective-permute-start | bytes 184328 | tf_op jit(solution)/shard_map/gather_z_far/ppermute | solution.py:27
  28.7 3.6 %collective-permute-done.1 = bf16[24,1280]{1,0:T(8,128)(2,1)S(1)} collective-permute-done((bf16[24,1280]{1,0:T(8,128)(2,1)S(1)}, bf16[24,1280]{1,0:T(8,128)(2,1)S(1)}, u32[]{:S(2)}, u32[]{:S(2)}) %collective-permute-start.1) | collective-permute-done | bytes 61472 | tf_op jit(solution)/shard_map/gather_z_far/ppermute | solution.py:27
  32.3 2.5 %collective-permute-start.2 = (bf16[48,1280]{1,0:T(8,128)(2,1)S(1)}, bf16[48,1280]{1,0:T(8,128)(2,1)S(1)}, u32[]{:S(2)}, u32[]{:S(2)}) collective-permute-start(bf16[48,1280]{1,0:T(8,128)(2,1)S(1)} %pad_maximum_fusion.2), channel_id=1, source_target_pairs={{0,128},{1,257},{2,130},{3,259},{4,132},{5,261},{6,134},{7,263},{8... | collective-permute-start | bytes 368648 | tf_op jit(solution)/shard_map/gather_z_mid/ppermute | solution.py:27
  34.8 9.8 %collective-permute-done.2 = bf16[48,1280]{1,0:T(8,128)(2,1)S(1)} collective-permute-done((bf16[48,1280]{1,0:T(8,128)(2,1)S(1)}, bf16[48,1280]{1,0:T(8,128)(2,1)S(1)}, u32[]{:S(2)}, u32[]{:S(2)}) %collective-permute-start.2) | collective-permute-done | bytes 122912 | tf_op jit(solution)/shard_map/gather_z_mid/ppermute | solution.py:27
  44.6 1.4 %eight_copies.1 = bf16[768,1280]{1,0:T(8,128)(2,1)} custom-call(bf16[96,1280]{1,0:T(8,128)(2,1)S(1)} %pad_maximum_fusion.1.block), custom_call_target="tpu_custom_call" | custom-call | tf_op jit(solution)/shard_map/gather_ring/eight_copies/pallas_call | solution.py:111
  46.0 5.5 %all-to-all-start = ((bf16[8,96,1280]{2,1,0:T(8,128)(2,1)}), bf16[8,96,1280]{2,1,0:T(8,128)(2,1)S(1)}, u32[]{:S(2)}, u32[]{:S(2)}) async-start(bf16[8,96,1280]{2,1,0:T(8,128)(2,1)} %bitcast.1), calls=%async_computation | async-start | bytes 3932160 | tf_op jit(solution)/shard_map/gather_ring/all_to_all | solution.py:59
  51.5 14.7 %all-to-all-done = bf16[8,96,1280]{2,1,0:T(8,128)(2,1)S(1)} async-done(((bf16[8,96,1280]{2,1,0:T(8,128)(2,1)}), bf16[8,96,1280]{2,1,0:T(8,128)(2,1)S(1)}, u32[]{:S(2)}, u32[]{:S(2)}) %all-to-all-start) | async-done | bytes 1966112 | tf_op jit(solution)/shard_map/gather_ring/all_to_all | solution.py:59
  66.1 1.1 broadcast_select_fusion.1
  67.2 6.6 %collective-permute-start.3 = (bf16[384,1280]{1,0:T(8,128)(2,1)}, bf16[384,1280]{1,0:T(8,128)(2,1)S(1)}, u32[]{:S(2)}, u32[]{:S(2)}) collective-permute-start(bf16[384,1280]{1,0:T(8,128)(2,1)} %bitcast.2), channel_id=1, source_target_pairs={{0,1},{1,0},{2,3},{3,2},{4,5},{5,4},{6,7},{7,6},{8,9},{9,8},{10,11... | collective-permute-start | bytes 2949128 | tf_op jit(solution)/shard_map/tile_swap/ppermute | solution.py:64
  75.2 1.1 collective-permute-done.3
  76.5 0.8 fusion.8
  77.9 2.3 %collective-permute-start.4 = (bf16[384,1152]{1,0:T(8,128)(2,1)S(1)}, bf16[384,1152]{1,0:T(8,128)(2,1)S(1)}, u32[]{:S(2)}, u32[]{:S(2)}) collective-permute-start(bf16[384,1152]{1,0:T(8,128)(2,1)S(1)} %convolution_convert_fusion), channel_id=1, source_target_pairs={{0,1},{1,0},{2,3},{3,2},{4,5},{5,4},{6,7},{7,6},{8,9},{9,8},{10,11... | collective-permute-start | bytes 2654216 | tf_op jit(solution)/shard_map/tile_sum/ppermute | solution.py:64
  80.2 2.0 %collective-permute-done.4 = bf16[384,1152]{1,0:T(8,128)(2,1)S(1)} collective-permute-done((bf16[384,1152]{1,0:T(8,128)(2,1)S(1)}, bf16[384,1152]{1,0:T(8,128)(2,1)S(1)}, u32[]{:S(2)}, u32[]{:S(2)}) %collective-permute-start.4) | collective-permute-done | bytes 884768 | tf_op jit(solution)/shard_map/tile_sum/ppermute | solution.py:64
  82.2 0.9 fusion
  83.3 18.3 %all_to_all.18 = bf16[8,96,1152]{2,1,0:T(8,128)(2,1)S(1)} all-to-all(bf16[8,96,1152]{2,1,0:T(8,128)(2,1)S(1)} %bitcast.7), channel_id=1, replica_groups={{0,8,16,24,992,1000,1008,1016},{1,3,5,7,65,67,69,71},{2,10,18,26,994,10..., dimensions={0} | all-to-all | bytes 3538944 | tf_op jit(solution)/shard_map/ring_sum/all_to_all | solution.py:59
  101.8 1.9 %collective-permute-start.5 = (bf16[48,1152]{1,0:T(8,128)(2,1)S(1)}, bf16[48,1152]{1,0:T(8,128)(2,1)S(1)}, u32[]{:S(2)}, u32[]{:S(2)}) collective-permute-start(bf16[48,1152]{1,0:T(8,128)(2,1)S(1)} %slice.92), channel_id=1, source_target_pairs={{0,128},{1,257},{2,130},{3,259},{4,132},{5,261},{6,134},{7,263},{8... | collective-permute-start | bytes 331784 | tf_op jit(solution)/shard_map/z_mid_sum/ppermute | solution.py:27
  103.7 8.7 %collective-permute-done.5 = bf16[48,1152]{1,0:T(8,128)(2,1)S(1)} collective-permute-done((bf16[48,1152]{1,0:T(8,128)(2,1)S(1)}, bf16[48,1152]{1,0:T(8,128)(2,1)S(1)}, u32[]{:S(2)}, u32[]{:S(2)}) %collective-permute-start.5) | collective-permute-done | bytes 110624 | tf_op jit(solution)/shard_map/z_mid_sum/ppermute | solution.py:27
  112.5 10.6 %collective-permute-start.6 = (bf16[24,1152]{1,0:T(8,128)(2,1)S(1)}, bf16[24,1152]{1,0:T(8,128)(2,1)S(1)}, u32[]{:S(2)}, u32[]{:S(2)}) collective-permute-start(bf16[24,1152]{1,0:T(8,128)(2,1)S(1)} %slice.93), channel_id=1, source_target_pairs={{0,512},{1,545},{2,514},{3,547},{4,516},{5,549},{6,518},{7,551},{8... | collective-permute-start | bytes 165896 | tf_op jit(solution)/shard_map/z_far_sum/ppermute | solution.py:27
  123.0 3.6 %collective-permute-done.6 = bf16[24,1152]{1,0:T(8,128)(2,1)S(1)} collective-permute-done((bf16[24,1152]{1,0:T(8,128)(2,1)S(1)}, bf16[24,1152]{1,0:T(8,128)(2,1)S(1)}, u32[]{:S(2)}, u32[]{:S(2)}) %collective-permute-start.6) | collective-permute-done | bytes 55328 | tf_op jit(solution)/shard_map/z_far_sum/ppermute | solution.py:27
  126.6 4.6 %collective-permute-start.7 = (f32[12,1152]{1,0:T(8,128)S(1)}, f32[12,1152]{1,0:T(8,128)S(1)}, u32[]{:S(2)}, u32[]{:S(2)}) collective-permute-start(f32[12,1152]{1,0:T(8,128)S(1)} %slice.63), channel_id=1, source_target_pairs={{0,1},{1,0},{2,3},{3,2},{4,5},{5,4},{6,7},{7,6},{8,9},{9,8},{10,11... | collective-permute-start | bytes 165896 | tf_op jit(solution)/shard_map/pair_return/ppermute | solution.py:64
  132.4 0.8 subtract_multiply_fusion
  (23 shorter events, 2.5 us)
Async XLA Ops:
  1.7 16.9 %collective-permute-start = (bf16[12,1280]{1,0:T(8,128)(2,1)S(1)}, bf16[12,1280]{1,0:T(8,128)(2,1)S(1)}, u32[]{:S(2)}, u32[]{:S(2)}) collective-permute-start(bf16[12,1280]{1,0:T(8,128)(2,1)S(1)} %get-tuple-element.8), channel_id=1, source_target_pairs={{0,1},{1,0},{2,3},{3,2},{4,5},{5,4},{6,7},{7,6},{8,9},{9,8},{10,11... | collective-permute-start | bytes 92168 | tf_op jit(solution)/shard_map/pair_swap/ppermute | solution.py:64
  18.6 13.7 %collective-permute-start.1 = (bf16[24,1280]{1,0:T(8,128)(2,1)S(1)}, bf16[24,1280]{1,0:T(8,128)(2,1)S(1)}, u32[]{:S(2)}, u32[]{:S(2)}) collective-permute-start(bf16[24,1280]{1,0:T(8,128)(2,1)S(1)} %pad_maximum_fusion.3), channel_id=1, source_target_pairs={{0,512},{1,545},{2,514},{3,547},{4,516},{5,549},{6,518},{7,551},{8... | collective-permute-start | bytes 184328 | tf_op jit(solution)/shard_map/gather_z_far/ppermute | solution.py:27
  32.3 12.3 %collective-permute-start.2 = (bf16[48,1280]{1,0:T(8,128)(2,1)S(1)}, bf16[48,1280]{1,0:T(8,128)(2,1)S(1)}, u32[]{:S(2)}, u32[]{:S(2)}) collective-permute-start(bf16[48,1280]{1,0:T(8,128)(2,1)S(1)} %pad_maximum_fusion.2), channel_id=1, source_target_pairs={{0,128},{1,257},{2,130},{3,259},{4,132},{5,261},{6,134},{7,263},{8... | collective-permute-start | bytes 368648 | tf_op jit(solution)/shard_map/gather_z_mid/ppermute | solution.py:27
  46.0 20.1 %all-to-all-start = ((bf16[8,96,1280]{2,1,0:T(8,128)(2,1)}), bf16[8,96,1280]{2,1,0:T(8,128)(2,1)S(1)}, u32[]{:S(2)}, u32[]{:S(2)}) async-start(bf16[8,96,1280]{2,1,0:T(8,128)(2,1)} %bitcast.1), calls=%async_computation | async-start | bytes 3932160 | tf_op jit(solution)/shard_map/gather_ring/all_to_all | solution.py:59
  67.2 9.0 %collective-permute-start.3 = (bf16[384,1280]{1,0:T(8,128)(2,1)}, bf16[384,1280]{1,0:T(8,128)(2,1)S(1)}, u32[]{:S(2)}, u32[]{:S(2)}) collective-permute-start(bf16[384,1280]{1,0:T(8,128)(2,1)} %bitcast.2), channel_id=1, source_target_pairs={{0,1},{1,0},{2,3},{3,2},{4,5},{5,4},{6,7},{7,6},{8,9},{9,8},{10,11... | collective-permute-start | bytes 2949128 | tf_op jit(solution)/shard_map/tile_swap/ppermute | solution.py:64
  77.9 4.3 %collective-permute-start.4 = (bf16[384,1152]{1,0:T(8,128)(2,1)S(1)}, bf16[384,1152]{1,0:T(8,128)(2,1)S(1)}, u32[]{:S(2)}, u32[]{:S(2)}) collective-permute-start(bf16[384,1152]{1,0:T(8,128)(2,1)S(1)} %convolution_convert_fusion), channel_id=1, source_target_pairs={{0,1},{1,0},{2,3},{3,2},{4,5},{5,4},{6,7},{7,6},{8,9},{9,8},{10,11... | collective-permute-start | bytes 2654216 | tf_op jit(solution)/shard_map/tile_sum/ppermute | solution.py:64
  101.5 30.7 %copy-start = (bf16[12,1152]{1,0:T(8,128)(2,1)S(1)}, bf16[12,1152]{1,0:T(8,128)(2,1)}, u32[]{:S(2)}) copy-start(bf16[12,1152]{1,0:T(8,128)(2,1)} %sentence_in.1) | copy-start | bytes 82948
  101.5 30.7 %copy-start.1 = (bf16[12,1152]{1,0:T(8,128)(2,1)S(1)}, bf16[12,1152]{1,0:T(8,128)(2,1)}, u32[]{:S(2)}) copy-start(bf16[12,1152]{1,0:T(8,128)(2,1)} %photo_in.1) | copy-start | bytes 82948
  101.8 10.7 %collective-permute-start.5 = (bf16[48,1152]{1,0:T(8,128)(2,1)S(1)}, bf16[48,1152]{1,0:T(8,128)(2,1)S(1)}, u32[]{:S(2)}, u32[]{:S(2)}) collective-permute-start(bf16[48,1152]{1,0:T(8,128)(2,1)S(1)} %slice.92), channel_id=1, source_target_pairs={{0,128},{1,257},{2,130},{3,259},{4,132},{5,261},{6,134},{7,263},{8... | collective-permute-start | bytes 331784 | tf_op jit(solution)/shard_map/z_mid_sum/ppermute | solution.py:27
  112.5 14.1 %collective-permute-start.6 = (bf16[24,1152]{1,0:T(8,128)(2,1)S(1)}, bf16[24,1152]{1,0:T(8,128)(2,1)S(1)}, u32[]{:S(2)}, u32[]{:S(2)}) collective-permute-start(bf16[24,1152]{1,0:T(8,128)(2,1)S(1)} %slice.93), channel_id=1, source_target_pairs={{0,512},{1,545},{2,514},{3,547},{4,516},{5,549},{6,518},{7,551},{8... | collective-permute-start | bytes 165896 | tf_op jit(solution)/shard_map/z_far_sum/ppermute | solution.py:27
  126.6 5.5 %collective-permute-start.7 = (f32[12,1152]{1,0:T(8,128)S(1)}, f32[12,1152]{1,0:T(8,128)S(1)}, u32[]{:S(2)}, u32[]{:S(2)}) collective-permute-start(f32[12,1152]{1,0:T(8,128)S(1)} %slice.63), channel_id=1, source_target_pairs={{0,1},{1,0},{2,3},{3,2},{4,5},{5,4},{6,7},{7,6},{8,9},{9,8},{10,11... | collective-permute-start | bytes 165896 | tf_op jit(solution)/shard_map/pair_return/ppermute | solution.py:64

commit v8 on v7

--- a/solution.py
+++ b/solution.py
@@ -209,6 +209,7 @@
 
     with jax.named_scope("tile_sum"):
         crossed = swap_cores(away).astype(jnp.float32)
+        home = lax.optimization_barrier(home)
         imgs, none = home + crossed, jnp.zeros_like(home)
         first = jnp.where(holds_images, jnp.where(stands_first, imgs, none), crossed)
         second = jnp.where(holds_images, jnp.where(stands_first, none, imgs), home)

time: 134 us -> 133 us (level)
  transfers between devices with their start and end apart: 9 -> 9, of which waited for: 9 -> 9; matrix products, arithmetic and copies ran while one was open for 0% -> 1% of each run, Pallas kernels for 0% -> 0%
where the time goes in v8:
time: 133 us
  starting transfers between devices  60.1 us (45%)
  waiting for transfers between devices  44.2 us (33%)
  blocking collectives  18.3 us (14%)
  other arithmetic  3.42 us (3%)
  Pallas kernels  2.44 us (2%)
  between operations  2.1 us (2%)
  matrix products  2.07 us (2%)
    ppermute x4, starting transfers between devices, swap_cores(): return lax.ppermute(value, BOTH, [(d, d ^ 1) for d in range(n)])  29.6 us
    ppermute x4, waiting for transfers between devices, permute(): return lax.ppermute(value, BOTH, pairs)  25.6 us
    ppermute x4, starting transfers between devices, permute(): return lax.ppermute(value, BOTH, pairs)  25 us
    all_to_all x1, blocking collectives, around(): lax.all_to_all(value, BOTH, 0, 0, axis_index_groups=EIGHTS, tiled=True)  18.3 us
    all_to_all x1, waiting for transfers between devices, around(): lax.all_to_all(value, BOTH, 0, 0, axis_index_groups=EIGHTS, tiled=True)  14.7 us
    all_to_all x1, starting transfers between devices, around(): lax.all_to_all(value, BOTH, 0, 0, axis_index_groups=EIGHTS, tiled=True)  5.46 us
    ppermute x4, waiting for transfers between devices, swap_cores(): return lax.ppermute(value, BOTH, [(d, d ^ 1) for d in range(n)])  3.92 us
  transfers between devices with their start and end apart: 9, of which 9 were waited for; matrix products, arithmetic and copies ran while one was open for 1% of the time, Pallas kernels for 0%

profile of v8, /device:TPU:1, one launch (start us, length us, event | category | flops | bytes accessed | tf_op | source)
XLA Modules:
  0.0 132.7 jit_solution(8140698349303272292)
XLA Ops:
  0.6 1.0 pack_rows.1
  1.7 16.1 %collective-permute-start = (bf16[12,1280]{1,0:T(8,128)(2,1)S(1)}, bf16[12,1280]{1,0:T(8,128)(2,1)S(1)}, u32[]{:S(2)}, u32[]{:S(2)}) collective-permute-start(bf16[12,1280]{1,0:T(8,128)(2,1)S(1)} %get-tuple-element.8), channel_id=1, source_target_pairs={{0,1},{1,0},{2,3},{3,2},{4,5},{5,4},{6,7},{7,6},{8,9},{9,8},{10,11... | collective-permute-start | bytes 92168 | tf_op jit(solution)/shard_map/pair_swap/ppermute | solution.py:64
  17.7 0.8 collective-permute-done
  18.6 10.1 %collective-permute-start.1 = (bf16[24,1280]{1,0:T(8,128)(2,1)S(1)}, bf16[24,1280]{1,0:T(8,128)(2,1)S(1)}, u32[]{:S(2)}, u32[]{:S(2)}) collective-permute-start(bf16[24,1280]{1,0:T(8,128)(2,1)S(1)} %pad_maximum_fusion.3), channel_id=1, source_target_pairs={{0,512},{1,545},{2,514},{3,547},{4,516},{5,549},{6,518},{7,551},{8... | collective-permute-start | bytes 184328 | tf_op jit(solution)/shard_map/gather_z_far/ppermute | solution.py:27
  28.7 3.6 %collective-permute-done.1 = bf16[24,1280]{1,0:T(8,128)(2,1)S(1)} collective-permute-done((bf16[24,1280]{1,0:T(8,128)(2,1)S(1)}, bf16[24,1280]{1,0:T(8,128)(2,1)S(1)}, u32[]{:S(2)}, u32[]{:S(2)}) %collective-permute-start.1) | collective-permute-done | bytes 61472 | tf_op jit(solution)/shard_map/gather_z_far/ppermute | solution.py:27
  32.3 2.5 %collective-permute-start.2 = (bf16[48,1280]{1,0:T(8,128)(2,1)S(1)}, bf16[48,1280]{1,0:T(8,128)(2,1)S(1)}, u32[]{:S(2)}, u32[]{:S(2)}) collective-permute-start(bf16[48,1280]{1,0:T(8,128)(2,1)S(1)} %pad_maximum_fusion.2), channel_id=1, source_target_pairs={{0,128},{1,257},{2,130},{3,259},{4,132},{5,261},{6,134},{7,263},{8... | collective-permute-start | bytes 368648 | tf_op jit(solution)/shard_map/gather_z_mid/ppermute | solution.py:27
  34.8 9.8 %collective-permute-done.2 = bf16[48,1280]{1,0:T(8,128)(2,1)S(1)} collective-permute-done((bf16[48,1280]{1,0:T(8,128)(2,1)S(1)}, bf16[48,1280]{1,0:T(8,128)(2,1)S(1)}, u32[]{:S(2)}, u32[]{:S(2)}) %collective-permute-start.2) | collective-permute-done | bytes 122912 | tf_op jit(solution)/shard_map/gather_z_mid/ppermute | solution.py:27
  44.6 1.4 %eight_copies.1 = bf16[768,1280]{1,0:T(8,128)(2,1)} custom-call(bf16[96,1280]{1,0:T(8,128)(2,1)S(1)} %pad_maximum_fusion.1.block), custom_call_target="tpu_custom_call" | custom-call | tf_op jit(solution)/shard_map/gather_ring/eight_copies/pallas_call | solution.py:111
  46.0 5.5 %all-to-all-start = ((bf16[8,96,1280]{2,1,0:T(8,128)(2,1)}), bf16[8,96,1280]{2,1,0:T(8,128)(2,1)S(1)}, u32[]{:S(2)}, u32[]{:S(2)}) async-start(bf16[8,96,1280]{2,1,0:T(8,128)(2,1)} %bitcast.1), calls=%async_computation | async-start | bytes 3932160 | tf_op jit(solution)/shard_map/gather_ring/all_to_all | solution.py:59
  51.5 14.7 %all-to-all-done = bf16[8,96,1280]{2,1,0:T(8,128)(2,1)S(1)} async-done(((bf16[8,96,1280]{2,1,0:T(8,128)(2,1)}), bf16[8,96,1280]{2,1,0:T(8,128)(2,1)S(1)}, u32[]{:S(2)}, u32[]{:S(2)}) %all-to-all-start) | async-done | bytes 1966112 | tf_op jit(solution)/shard_map/gather_ring/all_to_all | solution.py:59
  66.1 1.1 broadcast_select_fusion.1
  67.2 6.6 %collective-permute-start.3 = (bf16[384,1280]{1,0:T(8,128)(2,1)}, bf16[384,1280]{1,0:T(8,128)(2,1)S(1)}, u32[]{:S(2)}, u32[]{:S(2)}) collective-permute-start(bf16[384,1280]{1,0:T(8,128)(2,1)} %bitcast.2), channel_id=1, source_target_pairs={{0,1},{1,0},{2,3},{3,2},{4,5},{5,4},{6,7},{7,6},{8,9},{9,8},{10,11... | collective-permute-start | bytes 2949128 | tf_op jit(solution)/shard_map/tile_swap/ppermute | solution.py:64
  75.2 1.1 collective-permute-done.3
  76.5 0.8 fusion.8
  77.9 2.3 %collective-permute-start.4 = (bf16[384,1152]{1,0:T(8,128)(2,1)S(1)}, bf16[384,1152]{1,0:T(8,128)(2,1)S(1)}, u32[]{:S(2)}, u32[]{:S(2)}) collective-permute-start(bf16[384,1152]{1,0:T(8,128)(2,1)S(1)} %convolution_convert_fusion), channel_id=1, source_target_pairs={{0,1},{1,0},{2,3},{3,2},{4,5},{5,4},{6,7},{7,6},{8,9},{9,8},{10,11... | collective-permute-start | bytes 2654216 | tf_op jit(solution)/shard_map/tile_sum/ppermute | solution.py:64
  80.2 0.7 fusion.11
  80.9 1.4 %collective-permute-done.4 = bf16[384,1152]{1,0:T(8,128)(2,1)S(1)} collective-permute-done((bf16[384,1152]{1,0:T(8,128)(2,1)S(1)}, bf16[384,1152]{1,0:T(8,128)(2,1)S(1)}, u32[]{:S(2)}, u32[]{:S(2)}) %collective-permute-start.4) | collective-permute-done | bytes 884768 | tf_op jit(solution)/shard_map/tile_sum/ppermute | solution.py:64
  82.8 18.3 %all_to_all.18 = bf16[8,96,1152]{2,1,0:T(8,128)(2,1)S(1)} all-to-all(bf16[8,96,1152]{2,1,0:T(8,128)(2,1)S(1)} %bitcast.7), channel_id=1, replica_groups={{0,8,16,24,992,1000,1008,1016},{1,3,5,7,65,67,69,71},{2,10,18,26,994,10..., dimensions={0} | all-to-all | bytes 3538944 | tf_op jit(solution)/shard_map/ring_sum/all_to_all | solution.py:59
  101.3 1.9 %collective-permute-start.5 = (bf16[48,1152]{1,0:T(8,128)(2,1)S(1)}, bf16[48,1152]{1,0:T(8,128)(2,1)S(1)}, u32[]{:S(2)}, u32[]{:S(2)}) collective-permute-start(bf16[48,1152]{1,0:T(8,128)(2,1)S(1)} %slice.92), channel_id=1, source_target_pairs={{0,128},{1,257},{2,130},{3,259},{4,132},{5,261},{6,134},{7,263},{8... | collective-permute-start | bytes 331784 | tf_op jit(solution)/shard_map/z_mid_sum/ppermute | solution.py:27
  103.3 8.7 %collective-permute-done.5 = bf16[48,1152]{1,0:T(8,128)(2,1)S(1)} collective-permute-done((bf16[48,1152]{1,0:T(8,128)(2,1)S(1)}, bf16[48,1152]{1,0:T(8,128)(2,1)S(1)}, u32[]{:S(2)}, u32[]{:S(2)}) %collective-permute-start.5) | collective-permute-done | bytes 110624 | tf_op jit(solution)/shard_map/z_mid_sum/ppermute | solution.py:27
  112.0 10.6 %collective-permute-start.6 = (bf16[24,1152]{1,0:T(8,128)(2,1)S(1)}, bf16[24,1152]{1,0:T(8,128)(2,1)S(1)}, u32[]{:S(2)}, u32[]{:S(2)}) collective-permute-start(bf16[24,1152]{1,0:T(8,128)(2,1)S(1)} %slice.93), channel_id=1, source_target_pairs={{0,512},{1,545},{2,514},{3,547},{4,516},{5,549},{6,518},{7,551},{8... | collective-permute-start | bytes 165896 | tf_op jit(solution)/shard_map/z_far_sum/ppermute | solution.py:27
  122.6 3.6 %collective-permute-done.6 = bf16[24,1152]{1,0:T(8,128)(2,1)S(1)} collective-permute-done((bf16[24,1152]{1,0:T(8,128)(2,1)S(1)}, bf16[24,1152]{1,0:T(8,128)(2,1)S(1)}, u32[]{:S(2)}, u32[]{:S(2)}) %collective-permute-start.6) | collective-permute-done | bytes 55328 | tf_op jit(solution)/shard_map/z_far_sum/ppermute | solution.py:27
  126.2 4.6 %collective-permute-start.7 = (f32[12,1152]{1,0:T(8,128)S(1)}, f32[12,1152]{1,0:T(8,128)S(1)}, u32[]{:S(2)}, u32[]{:S(2)}) collective-permute-start(f32[12,1152]{1,0:T(8,128)S(1)} %slice.63), channel_id=1, source_target_pairs={{0,1},{1,0},{2,3},{3,2},{4,5},{5,4},{6,7},{7,6},{8,9},{9,8},{10,11... | collective-permute-start | bytes 165896 | tf_op jit(solution)/shard_map/pair_return/ppermute | solution.py:64
  131.9 0.8 subtract_multiply_fusion
  (24 shorter events, 2.9 us)
Async XLA Ops:
  1.7 16.9 %collective-permute-start = (bf16[12,1280]{1,0:T(8,128)(2,1)S(1)}, bf16[12,1280]{1,0:T(8,128)(2,1)S(1)}, u32[]{:S(2)}, u32[]{:S(2)}) collective-permute-start(bf16[12,1280]{1,0:T(8,128)(2,1)S(1)} %get-tuple-element.8), channel_id=1, source_target_pairs={{0,1},{1,0},{2,3},{3,2},{4,5},{5,4},{6,7},{7,6},{8,9},{9,8},{10,11... | collective-permute-start | bytes 92168 | tf_op jit(solution)/shard_map/pair_swap/ppermute | solution.py:64
  18.6 13.7 %collective-permute-start.1 = (bf16[24,1280]{1,0:T(8,128)(2,1)S(1)}, bf16[24,1280]{1,0:T(8,128)(2,1)S(1)}, u32[]{:S(2)}, u32[]{:S(2)}) collective-permute-start(bf16[24,1280]{1,0:T(8,128)(2,1)S(1)} %pad_maximum_fusion.3), channel_id=1, source_target_pairs={{0,512},{1,545},{2,514},{3,547},{4,516},{5,549},{6,518},{7,551},{8... | collective-permute-start | bytes 184328 | tf_op jit(solution)/shard_map/gather_z_far/ppermute | solution.py:27
  32.3 12.3 %collective-permute-start.2 = (bf16[48,1280]{1,0:T(8,128)(2,1)S(1)}, bf16[48,1280]{1,0:T(8,128)(2,1)S(1)}, u32[]{:S(2)}, u32[]{:S(2)}) collective-permute-start(bf16[48,1280]{1,0:T(8,128)(2,1)S(1)} %pad_maximum_fusion.2), channel_id=1, source_target_pairs={{0,128},{1,257},{2,130},{3,259},{4,132},{5,261},{6,134},{7,263},{8... | collective-permute-start | bytes 368648 | tf_op jit(solution)/shard_map/gather_z_mid/ppermute | solution.py:27
  46.0 20.1 %all-to-all-start = ((bf16[8,96,1280]{2,1,0:T(8,128)(2,1)}), bf16[8,96,1280]{2,1,0:T(8,128)(2,1)S(1)}, u32[]{:S(2)}, u32[]{:S(2)}) async-start(bf16[8,96,1280]{2,1,0:T(8,128)(2,1)} %bitcast.1), calls=%async_computation | async-start | bytes 3932160 | tf_op jit(solution)/shard_map/gather_ring/all_to_all | solution.py:59
  67.2 9.0 %collective-permute-start.3 = (bf16[384,1280]{1,0:T(8,128)(2,1)}, bf16[384,1280]{1,0:T(8,128)(2,1)S(1)}, u32[]{:S(2)}, u32[]{:S(2)}) collective-permute-start(bf16[384,1280]{1,0:T(8,128)(2,1)} %bitcast.2), channel_id=1, source_target_pairs={{0,1},{1,0},{2,3},{3,2},{4,5},{5,4},{6,7},{7,6},{8,9},{9,8},{10,11... | collective-permute-start | bytes 2949128 | tf_op jit(solution)/shard_map/tile_swap/ppermute | solution.py:64
  77.9 4.3 %collective-permute-start.4 = (bf16[384,1152]{1,0:T(8,128)(2,1)S(1)}, bf16[384,1152]{1,0:T(8,128)(2,1)S(1)}, u32[]{:S(2)}, u32[]{:S(2)}) collective-permute-start(bf16[384,1152]{1,0:T(8,128)(2,1)S(1)} %convolution_convert_fusion), channel_id=1, source_target_pairs={{0,1},{1,0},{2,3},{3,2},{4,5},{5,4},{6,7},{7,6},{8,9},{9,8},{10,11... | collective-permute-start | bytes 2654216 | tf_op jit(solution)/shard_map/tile_sum/ppermute | solution.py:64
  101.1 30.7 %copy-start = (bf16[12,1152]{1,0:T(8,128)(2,1)S(1)}, bf16[12,1152]{1,0:T(8,128)(2,1)}, u32[]{:S(2)}) copy-start(bf16[12,1152]{1,0:T(8,128)(2,1)} %sentence_in.1) | copy-start | bytes 82948
  101.1 30.7 %copy-start.1 = (bf16[12,1152]{1,0:T(8,128)(2,1)S(1)}, bf16[12,1152]{1,0:T(8,128)(2,1)}, u32[]{:S(2)}) copy-start(bf16[12,1152]{1,0:T(8,128)(2,1)} %photo_in.1) | copy-start | bytes 82948
  101.3 10.7 %collective-permute-start.5 = (bf16[48,1152]{1,0:T(8,128)(2,1)S(1)}, bf16[48,1152]{1,0:T(8,128)(2,1)S(1)}, u32[]{:S(2)}, u32[]{:S(2)}) collective-permute-start(bf16[48,1152]{1,0:T(8,128)(2,1)S(1)} %slice.92), channel_id=1, source_target_pairs={{0,128},{1,257},{2,130},{3,259},{4,132},{5,261},{6,134},{7,263},{8... | collective-permute-start | bytes 331784 | tf_op jit(solution)/shard_map/z_mid_sum/ppermute | solution.py:27
  112.0 14.1 %collective-permute-start.6 = (bf16[24,1152]{1,0:T(8,128)(2,1)S(1)}, bf16[24,1152]{1,0:T(8,128)(2,1)S(1)}, u32[]{:S(2)}, u32[]{:S(2)}) collective-permute-start(bf16[24,1152]{1,0:T(8,128)(2,1)S(1)} %slice.93), channel_id=1, source_target_pairs={{0,512},{1,545},{2,514},{3,547},{4,516},{5,549},{6,518},{7,551},{8... | collective-permute-start | bytes 165896 | tf_op jit(solution)/shard_map/z_far_sum/ppermute | solution.py:27
  126.2 5.5 %collective-permute-start.7 = (f32[12,1152]{1,0:T(8,128)S(1)}, f32[12,1152]{1,0:T(8,128)S(1)}, u32[]{:S(2)}, u32[]{:S(2)}) collective-permute-start(f32[12,1152]{1,0:T(8,128)S(1)} %slice.63), channel_id=1, source_target_pairs={{0,1},{1,0},{2,3},{3,2},{4,5},{5,4},{6,7},{7,6},{8,9},{9,8},{10,11... | collective-permute-start | bytes 165896 | tf_op jit(solution)/shard_map/pair_return/ppermute | solution.py:64
